TPU v7x, 256 devices: a whole 4x4x8 slice. The times are simulated.
256 devices in a mesh: row: 16 (over y, z_hi, core), col: 16 (over x, z_lo).
Axes of the slice: x: 4, y: 4, z: 8 (z_hi: 2, z_lo: 4; z = z_hi * 4 + z_lo), core: 2. Of those that a mesh axis runs over, the one named last changes fastest.
Arguments:
- pair: bfloat16 [1024, 1024, 128], P('row', 'col'), may hold values from -6 to 6
- norm_gain: float32 [128], replicated, may hold values from 0.1 to 1.9
- norm_shift: float32 [128], replicated, may hold values from -3 to 3
- w_query: bfloat16 [128, 128], replicated, may hold values from -1 to 1
- w_key: bfloat16 [128, 128], replicated, may hold values from -0.5 to 0.5
- w_value: bfloat16 [128, 128], replicated, may hold values from -0.5 to 0.5
- w_gate: bfloat16 [128, 128], replicated, may hold values from -0.5 to 0.5
- gate_shift: float32 [128], replicated, may hold values from -1 to 1
- w_bias: float32 [128, 4], replicated, may hold values from -30 to 30
- w_out: bfloat16 [128, 128], replicated, may hold values from -1 to 1
- out_shift: float32 [128], replicated, may hold values from -3 to 3
Outputs:
- update: bfloat16 [1024, 1024, 128], P('row', 'col')
All inputs are finite; a program needn't handle non-finite values.
Results may differ from a plain program's by a relative error of at most 0.0015.
The roundings to bfloat16 on the way count: a program that leaves them out, or rounds other values in their place, can miss the bound.
Values may be sent and summed in bfloat16 or wider, within the bound.
No kernel may reach another device: no remote copies, remote signals or barrier semaphores. Data moves between devices by JAX's collectives and lax.ppermute only.
A program may use at most 128 MiB of HBM per device.

v0:
```python
import functools
import math

import jax
import jax.numpy as jnp
from jax import lax
from jax.experimental import pallas as pl
from jax.experimental.pallas import tpu as pltpu
from jax.sharding import Mesh
from jax.sharding import PartitionSpec as P

F32 = jnp.float32
BF = jnp.bfloat16
CHUNKS = 2
TOGETHER = 2
DEPTH = 32


def dot(a, b):
    return jnp.dot(a, b, preferred_element_type=F32)


def dot_t(a, b):
    return lax.dot_general(a, b, (((1,), (1,)), ((), ())), preferred_element_type=F32)


def fold(function, so_far, value):
    return value if so_far is None else function(so_far, value)


def attend_kernel(
    at,
    x0,
    x1,
    x2,
    x3,
    b00,
    b01,
    b10,
    b11,
    b20,
    b21,
    b30,
    b31,
    w_key,
    w_value_t,
    w_query_t,
    w_gate_t,
    gate_shift,
    w_out,
    out_shift,
    out,
    key_ref,
    value_ref,
    score_ref,
    attended_ref,
):
    rows = (x0, x1, x2, x3)
    bias = ((b00, b01), (b10, b11), (b20, b21), (b30, b31))
    y, zl, core = at[0], at[2], at[3]
    slot = [lax.rem(zl + 4 - part, 4) for part in range(4)]
    heads = [lax.rem(y + 4 - step, 4) for step in range(4)]
    halves = [pl.multiple_of(lax.rem(core + half, 2) * 32, 32) for half in range(2)]
    kept = [{} for _ in range(TOGETHER)]

    def project_query(r):
        tokens = jnp.concatenate([x0[slot[part], r] for part in range(4)], axis=0)
        query = (dot_t(w_query_t[...], tokens) * (1.0 / math.sqrt(DEPTH))).astype(BF)
        gate = jax.nn.sigmoid(dot_t(w_gate_t[...], tokens) + gate_shift[...])
        of_head = lax.broadcasted_iota(jnp.int32, query.shape, 0) // DEPTH
        zero = jnp.zeros_like(query)
        return [jnp.where(of_head == head, query, zero) for head in heads], gate

    def project(r):
        tokens = jnp.concatenate(
            [
                rows[t][s, r, pl.ds(halves[half], 32), :]
                for half in range(2)
                for s in range(4)
                for t in range(4)
            ],
            axis=0,
        )
        key_ref[r] = dot(tokens, w_key[...]).astype(BF)
        value_ref[r] = dot_t(w_value_t[...], tokens).astype(BF)
        kept[r]["query"], kept[r]["gate"] = project_query(r)

    def score(r, a, c, query):
        half, s = divmod(c, 4)
        z_of = [zh * 4 + lax.rem(zl + 4 - s, 4) for zh in range(2)]
        added = jnp.concatenate([bias[a][half][z] for z in z_of], axis=1)
        return dot(key_ref[r, c * 128 : (c + 1) * 128, :], query[a]) + added

    def raise_plain(r, a):
        total = None
        for c in range(8):
            raised = jnp.exp(score(r, a, c, kept[r]["query"]))
            score_ref[r, a, c] = raised
            total = fold(jnp.add, total, jnp.sum(raised.reshape(16, 8, 256), axis=0))
        return jnp.sum(total, axis=0, keepdims=True)

    def raise_shifted(r, a, query):
        largest = None
        for c in range(8):
            scores = score(r, a, c, query)
            score_ref[r, a, c] = scores
            largest = fold(
                jnp.maximum, largest, jnp.max(scores.reshape(16, 8, 256), axis=0)
            )
        largest = jnp.max(largest, axis=0, keepdims=True)
        total = None
        for c in range(8):
            raised = jnp.exp(score_ref[r, a, c] - largest)
            score_ref[r, a, c] = raised
            total = fold(jnp.add, total, jnp.sum(raised.reshape(16, 8, 256), axis=0))
        return jnp.sum(total, axis=0, keepdims=True)

    def weigh(r, a, total):
        scale = 1.0 / total
        weights = jnp.concatenate(
            [(score_ref[r, a, c] * scale).astype(BF) for c in range(8)], axis=0
        )
        own = pl.ds(pl.multiple_of(heads[a] * DEPTH, DEPTH), DEPTH)
        attended_ref[r, own, :] = dot(value_ref[r, own, :], weights)

    def finish(r, gate):
        gated = (gate * attended_ref[r]).astype(BF)
        update = lax.dot_general(
            gated, w_out[...], (((0,), (0,)), ((), ())), preferred_element_type=F32
        )
        update = (update + out_shift[...]).astype(BF)
        for part in range(4):
            out[slot[part], r] = update[part * 64 : (part + 1) * 64]

    for r in range(TOGETHER):
        project(r)
    totals = {}
    for r in range(TOGETHER):
        for a in range(4):
            totals[r, a] = raise_plain(r, a)
    for r in range(TOGETHER):
        for a in range(4):
            weigh(r, a, totals[r, a])
    for r in range(TOGETHER):
        finish(r, kept[r]["gate"])

    safe = None
    for total in totals.values():
        inside = jnp.logical_and(total > 2.0**-60, total < 2.0**120)
        safe = fold(jnp.minimum, safe, jnp.where(inside, 1.0, 0.0))

    @pl.when(jnp.min(safe) < 0.5)
    def _():
        for r in range(TOGETHER):
            query, gate = project_query(r)
            for a in range(4):
                weigh(r, a, raise_shifted(r, a, query))
            finish(r, gate)


def attend(at, rows, first, biases, *weights):
    count = 16 // CHUNKS
    whole = lambda a: pl.BlockSpec(a.shape, lambda i, at: (0,) * a.ndim)
    block = (4, TOGETHER, 64, 128)
    specs = [
        pl.BlockSpec(block, lambda i, at, start=start // TOGETHER: (0, i + start, 0, 0))
        for start in first
    ]
    biases = [b for pair in biases for b in pair]
    return pl.pallas_call(
        attend_kernel,
        out_shape=jax.ShapeDtypeStruct((4, count, 64, 128), BF),
        grid_spec=pltpu.PrefetchScalarGridSpec(
            num_scalar_prefetch=1,
            grid=(count // TOGETHER,),
            in_specs=specs
            + [whole(a) for a in biases]
            + [whole(a) for a in weights],
            out_specs=pl.BlockSpec(block, lambda i, at: (0, i, 0, 0)),
            scratch_shapes=[
                pltpu.VMEM((TOGETHER, 1024, 128), BF),
                pltpu.VMEM((TOGETHER, 128, 1024), BF),
                pltpu.VMEM((TOGETHER, 4, 8, 128, 256), F32),
                pltpu.VMEM((TOGETHER, 128, 256), F32),
            ],
        ),
        compiler_params=pltpu.CompilerParams(
            vmem_limit_bytes=48 << 20, dimension_semantics=("arbitrary",)
        ),
        cost_estimate=pl.CostEstimate(
            flops=count * 300_000_000,
            bytes_accessed=count << 20,
            transcendentals=count << 20,
        ),
        name="attention",
    )(at, *rows, *biases, *weights)


def normalize(values, gain, shift):
    values = values.astype(F32)
    mean = jnp.mean(values, axis=-1, keepdims=True)
    centred = values - mean
    spread = jnp.mean(centred * centred, axis=-1, keepdims=True)
    return (centred * lax.rsqrt(spread + 1e-05) * gain + shift).astype(BF)


def assemble_kernel(at, *refs):
    *blocks, out = refs
    count = blocks[0].shape[0]
    for i, block in enumerate(blocks):
        chunk, step = divmod(i, 4)
        start = lax.rem(at[2] + step, 4) * 16 + chunk * count
        out[pl.ds(start, count)] = block[...]


def assemble(at, blocks):
    return pl.pallas_call(
        assemble_kernel,
        out_shape=jax.ShapeDtypeStruct((64, 64, 128), BF),
        in_specs=[pl.BlockSpec(memory_space=pltpu.SMEM)]
        + [pl.BlockSpec(memory_space=pltpu.VMEM)] * len(blocks),
        out_specs=pl.BlockSpec(memory_space=pltpu.VMEM),
        name="assemble_update",
    )(at, *blocks)


def tie_kernel(array, *rest):
    pass


def after(array, *earlier):
    return pl.pallas_call(
        tie_kernel,
        out_shape=jax.ShapeDtypeStruct(array.shape, array.dtype),
        in_specs=[pl.BlockSpec(memory_space=pl.ANY)] * (1 + len(earlier)),
        out_specs=pl.BlockSpec(memory_space=pl.ANY),
        input_output_aliases={0: 0},
        name="tie",
    )(array, *earlier)


AXES = ("y", "zh", "core", "x", "zl")


def move(array, to):
    pairs = []
    for source in range(256):
        row, col = divmod(source, 16)
        y, zh, core = row // 4, row // 2 % 2, row % 2
        x, zl = divmod(col, 4)
        y, z, core, x = to(y, zh * 4 + zl, core, x)
        y, z, x = y % 4, z % 8, x % 4
        target = ((y * 2 + z // 4) * 2 + core) * 16 + x * 4 + z % 4
        pairs.append((source, target))
    return lax.ppermute(array, AXES, pairs)


def swap_cores(array):
    return move(array, lambda y, z, core, x: (y, z, 1 - core, x))


def turn(z, step):
    return z // 4 * 4 + (z + step) % 4


def on_device(
    pair,
    norm_gain,
    norm_shift,
    w_query,
    w_key,
    w_value,
    w_gate,
    gate_shift,
    w_bias,
    w_out,
    out_shift,
):
    y, core, x, zl = (lax.axis_index(name) for name in ("y", "core", "x", "zl"))
    place = jnp.stack([y, x, zl, core]).astype(jnp.int32)
    normed = normalize(pair, norm_gain, norm_shift)
    count = 16 // CHUNKS

    with jax.named_scope("rows"):
        pieces = []
        for step in range(4):
            part = lax.dynamic_slice_in_dim(normed, (zl + step) % 4 * 16, 16, 0)
            if step:
                part = move(part, lambda y, z, core, x: (y, turn(z, step), core, x))
            pieces.append(part)
        here = jnp.stack(pieces)
        left = move(here, lambda y, z, core, x: (y, z, core, x + 1))
        right = move(here, lambda y, z, core, x: (y, z, core, x - 1))
        across = (
            move(left[:, :count], lambda y, z, core, x: (y, z, core, x + 1)),
            move(right[:, count:], lambda y, z, core, x: (y, z, core, x - 1)),
        )
    with jax.named_scope("bias"):
        tile = jnp.einsum(
            "jkc,ch->hkj", normed.astype(F32), w_bias, precision=lax.Precision.HIGHEST
        )
        kept = lax.dynamic_slice_in_dim(tile, core * 32, 32, 1)
        sent = lax.dynamic_slice_in_dim(tile, (1 - core) * 32, 32, 1)
        got = swap_cores(sent)
        tile = jnp.where(
            core == 0, jnp.concatenate([kept, got], 2), jnp.concatenate([got, kept], 2)
        )
        rounds = []
        for step in range(4):
            part = lax.dynamic_index_in_dim(tile, (x + step) % 4, 0, keepdims=False)
            rounds.append(move(part, lambda y, z, core, x: (x + step, z, core, y)))
        rounds = jnp.stack(rounds + rounds[:3])
        block = lax.dynamic_slice_in_dim(rounds, (y - x) % 4, 4, 0).reshape(128, 128)
        block = after(block, here)
        along_z = lax.all_to_all(
            jnp.broadcast_to(block[None], (8, 128, 128)),
            ("zh", "zl"),
            split_axis=0,
            concat_axis=0,
            tiled=True,
        )
    with jax.named_scope("bias"):
        along_z = after(along_z, left, right)
        biases = []
        for step in range(4):
            moved = along_z
            if step:
                moved = move(along_z, lambda y, z, core, x: (y + step, z, core, x))
            biases.append((moved, swap_cores(moved)))
    blocks = []
    for chunk in range(CHUNKS):
        with jax.named_scope("attention"):
            part = attend(
                place,
                (here, left, across[chunk], right),
                (chunk * count, chunk * count, 0, chunk * count),
                biases,
                w_key,
                w_value.T,
                w_query.T,
                w_gate.T,
                gate_shift[:, None],
                w_out,
                out_shift[None],
            )
            place = after(place, part)
        with jax.named_scope("update"):
            for step in range(4):
                back = part[step]
                if step:
                    back = move(back, lambda y, z, core, x: (y, turn(z, -step), core, x))
                blocks.append(back)
    return assemble(place, blocks)


def solution(mesh):
    parts = Mesh(mesh.devices.reshape(4, 2, 2, 4, 4), AXES)
    tiles = P(("y", "zh", "core"), ("x", "zl"), None)
    return jax.shard_map(
        on_device,
        mesh=parts,
        in_specs=(tiles,) + (P(),) * 10,
        out_specs=tiles,
        check_vma=False,
    )
```

profile of v0, /device:TPU:1, one launch (start us, length us, event | category | flops | bytes accessed | tf_op | source)
XLA Modules:
  0.0 194.4 jit_solution(6802725817075922843)
XLA Ops:
  0.0 1.9 convert_reduce_fusion
  2.0 1.3 fusion.2
  3.3 1.3 fusion.5
  4.6 2.5 %fusion.6 = f32[64,64,4]{1,2,0:T(4,128)S(1)} fusion(bf16[64,64,128]{2,1,0:T(8,128)(2,1)S(1)} %fusion.5, f32[128,4]{0,1:T(4,128)S(1)} %copy-done), kind=kOutput, calls=%fused_computation.38 | convolution fusion | flops 25165824 | bytes 1116160 | tf_op jit(solution)/shard_map/bias/jkc,ch->hkj/dot_general | solution.py:299
  7.1 0.2 dynamic-slice_bitcast_fusion.2
  7.4 3.3 %collective-permute-start.6 = (f32[4,32,64]{1,0,2:T(4,128)S(1)}, f32[4,32,64]{1,0,2:T(4,128)S(1)}, u32[]{:S(2)}, u32[]{:S(2)}) collective-permute-start(f32[4,32,64]{1,0,2:T(4,128)S(1)} %get-tuple-element.18), channel_id=1, source_target_pairs={{0,16},{1,17},{2,18},{3,19},{4,20},{5,21},{6,22},{7,23},{8,24},{9,... | collective-permute-start | bytes 98312 | tf_op jit(solution)/shard_map/bias/ppermute | solution.py:255
  10.8 0.9 collective-permute-done.6
  11.9 0.7 collective-permute-start.7
  12.7 2.7 %collective-permute-start.2 = (bf16[16,64,128]{2,1,0:T(8,128)(2,1)S(1)}, bf16[16,64,128]{2,1,0:T(8,128)(2,1)S(1)}, u32[]{:S(2)}, u32[]{:S(2)}) collective-permute-start(bf16[16,64,128]{2,1,0:T(8,128)(2,1)S(1)} %get-tuple-element.6), channel_id=1, source_target_pairs={{0,3},{1,0},{2,1},{3,2},{4,7},{5,4},{6,5},{7,6},{8,11},{9,8},{10,9... | collective-permute-start | bytes 786440 | tf_op jit(solution)/shard_map/rows/ppermute | solution.py:255
  15.4 0.4 collective-permute-start
  15.7 6.1 %collective-permute-start.10 = (f32[32,128]{1,0:T(8,128)S(1)}, f32[32,128]{1,0:T(8,128)S(1)}, u32[]{:S(2)}, u32[]{:S(2)}) collective-permute-start(f32[32,128]{1,0:T(8,128)S(1)} %get-tuple-element.19), channel_id=1, source_target_pairs={{0,192},{1,193},{2,194},{3,195},{4,0},{5,1},{6,2},{7,3},{8,64},{9,... | collective-permute-start | bytes 49160 | tf_op jit(solution)/shard_map/bias/ppermute | solution.py:255
  21.9 1.9 collective-permute-start.8
  23.8 2.5 %collective-permute-done.8 = f32[32,128]{1,0:T(8,128)S(1)} collective-permute-done((f32[32,128]{1,0:T(8,128)S(1)}, f32[32,128]{1,0:T(8,128)S(1)}, u32[]{:S(2)}, u32[]{:S(2)}) %collective-permute-start.8) | collective-permute-done | bytes 16416 | tf_op jit(solution)/shard_map/bias/ppermute | solution.py:255
  26.2 3.2 %collective-permute-start.9 = (f32[32,128]{1,0:T(8,128)S(1)}, f32[32,128]{1,0:T(8,128)S(1)}, u32[]{:S(2)}, u32[]{:S(2)}) collective-permute-start(f32[32,128]{1,0:T(8,128)S(1)} %get-tuple-element.20), channel_id=1, source_target_pairs={{0,128},{1,129},{2,130},{3,131},{4,192},{5,193},{6,194},{7,195},{8... | collective-permute-start | bytes 49160 | tf_op jit(solution)/shard_map/bias/ppermute | solution.py:255
  29.5 1.0 collective-permute-done.9
  30.5 6.6 %collective-permute-done.1 = bf16[16,64,128]{2,1,0:T(8,128)(2,1)S(1)} collective-permute-done((bf16[16,64,128]{2,1,0:T(8,128)(2,1)S(1)}, bf16[16,64,128]{2,1,0:T(8,128)(2,1)S(1)}, u32[]{:S(2)}, u32[]{:S(2)}) %collective-permute-start.1) | collective-permute-done | bytes 262176 | tf_op jit(solution)/shard_map/rows/ppermute | solution.py:255
  37.1 0.1 pad_maximum_fusion.rest_0_.x0
  37.3 6.1 %collective-permute-start.5 = (bf16[4,16,64,128]{3,2,1,0:T(8,128)(2,1)S(1)}, bf16[4,16,64,128]{3,2,1,0:T(8,128)(2,1)S(1)}, u32[]{:S(2)}, u32[]{:S(2)}) collective-permute-start(bf16[4,16,64,128]{3,2,1,0:T(8,128)(2,1)S(1)} %pad_maximum_fusion.rest_0_.x0), channel_id=1, source_target_pairs={{0,12},{1,13},{2,14},{3,15},{4,0},{5,1},{6,2},{7,3},{8,4},{9,5},{1... | collective-permute-start | bytes 3145736 | tf_op jit(solution)/shard_map/rows/ppermute | solution.py:255
  43.4 0.6 constant_dynamic-slice_fusion
  44.0 0.9 broadcast_in_dim.6
  44.9 23.0 %all_to_all.5.array = f32[8,128,128]{2,1,0:T(8,128)} all-to-all(f32[8,128,128]{2,1,0:T(8,128)S(1)} %broadcast_in_dim.6), channel_id=1, replica_groups=mesh['y'=4,'zh'=2,'core'=2,'x'=4,'zl'=4] {'zh','zl'}, dimensions={0} | all-to-all | bytes 1048576 | tf_op jit(solution)/shard_map/bias/all_to_all | solution.py:315
  68.0 1.0 copy-done.13
  69.0 1.0 copy-done.14
  70.0 1.4 collective-permute-start.16
  71.4 2.0 %collective-permute-start.14 = (f32[8,128,128]{2,1,0:T(8,128)}, f32[8,128,128]{2,1,0:T(8,128)S(1)}, u32[]{:S(2)}, u32[]{:S(2)}) collective-permute-start(f32[8,128,128]{2,1,0:T(8,128)} %tie.5.b00), channel_id=1, source_target_pairs={{0,128},{1,129},{2,130},{3,131},{4,132},{5,133},{6,134},{7,135},{8... | collective-permute-start | bytes 1572872 | tf_op jit(solution)/shard_map/bias/ppermute | solution.py:255
  73.4 1.9 slice.40
  75.3 4.0 %collective-permute-start.11 = (f32[8,128,128]{2,1,0:T(8,128)S(1)}, f32[8,128,128]{2,1,0:T(8,128)S(1)}, u32[]{:S(2)}, u32[]{:S(2)}) collective-permute-start(f32[8,128,128]{2,1,0:T(8,128)S(1)} %copy-done.3), channel_id=1, source_target_pairs={{0,16},{1,17},{2,18},{3,19},{4,20},{5,21},{6,22},{7,23},{8,24},{9,... | collective-permute-start | bytes 1572872 | tf_op jit(solution)/shard_map/bias/ppermute | solution.py:255
  79.2 1.6 collective-permute-done.16.b30
  80.9 7.3 %collective-permute-start.17 = (f32[8,128,128]{2,1,0:T(8,128)S(1)}, f32[8,128,128]{2,1,0:T(8,128)S(1)}, u32[]{:S(2)}, u32[]{:S(2)}) collective-permute-start(f32[8,128,128]{2,1,0:T(8,128)S(1)} %collective-permute-done.16.b30), channel_id=1, source_target_pairs={{0,16},{1,17},{2,18},{3,19},{4,20},{5,21},{6,22},{7,23},{8,24},{9,... | collective-permute-start | bytes 1572872 | tf_op jit(solution)/shard_map/bias/ppermute | solution.py:255
  88.1 3.2 %collective-permute-start.15 = (f32[8,128,128]{2,1,0:T(8,128)S(1)}, f32[8,128,128]{2,1,0:T(8,128)}, u32[]{:S(2)}, u32[]{:S(2)}) collective-permute-start(f32[8,128,128]{2,1,0:T(8,128)S(1)} %collective-permute-done.14.b20), channel_id=1, source_target_pairs={{0,16},{1,17},{2,18},{3,19},{4,20},{5,21},{6,22},{7,23},{8,24},{9,... | collective-permute-start | bytes 1572872 | tf_op jit(solution)/shard_map/bias/ppermute | solution.py:255
  91.3 6.9 %collective-permute-done.12.b10 = f32[8,128,128]{2,1,0:T(8,128)S(1)} collective-permute-done((f32[8,128,128]{2,1,0:T(8,128)}, f32[8,128,128]{2,1,0:T(8,128)S(1)}, u32[]{:S(2)}, u32[]{:S(2)}) %collective-permute-start.12) | collective-permute-done | bytes 524320 | tf_op jit(solution)/shard_map/bias/ppermute | solution.py:255
  98.2 0.5 collective-permute-start.13
  99.2 1.9 slice.41
  101.1 1.3 collective-permute-start.18
  102.6 35.2 %attention.2.rest_0_ = bf16[4,8,64,128]{3,2,1,0:T(8,128)(2,1)S(1)} custom-call(s32[4]{0:T(128)S(1)} %pad_add_fusion.at.array, bf16[4,16,64,128]{3,2,1,0:T(8,128)(2,1)} %copy-done.12, bf16[4,16,64,128]{3,2,1,0:T(8,128)(2,1)} %copy-done.14, bf16[4,8,64,128]{3,2,1,0:T(8,128)(2,1)} %collective-permute-done.4.x2, bf16[4,16,64,128]{3,2,1,0:T(8,128)(2,1)} %copy-done.13, ...), custom_call_target="tpu_custom_call" | custom-call | flops 2400000000 | bytes 8388608 | tf_op jit(solution)/shard_map/attention/attention/pallas_call | solution.py:170
  137.9 0.8 copy-done.2
  138.7 1.9 slice_bitcast_fusion.4
  140.7 1.6 collective-permute-start.20
  142.3 1.6 collective-permute-start.19
  143.8 35.2 %attention.3.rest_0_ = bf16[4,8,64,128]{3,2,1,0:T(8,128)(2,1)S(1)} custom-call(s32[4]{0:T(128)S(1)} %copy-done.5, bf16[4,16,64,128]{3,2,1,0:T(8,128)(2,1)} %copy-done.12, bf16[4,16,64,128]{3,2,1,0:T(8,128)(2,1)} %copy-done.14, bf16[4,8,64,128]{3,2,1,0:T(8,128)(2,1)} %collective-permute-done.18.x2, bf16[4,16,64,128]{3,2,1,0:T(8,128)(2,1)} %copy-done.13, ...), custom_call_target="tpu_custom_call" | custom-call | flops 2400000000 | bytes 8388608 | tf_op jit(solution)/shard_map/attention/attention/pallas_call | solution.py:170
  179.0 0.8 slice_bitcast_fusion
  179.8 0.3 collective-permute-start.24
  180.1 1.2 collective-permute-start.23
  181.3 2.4 %collective-permute-start.22 = (bf16[8,64,128]{2,1,0:T(8,128)(2,1)S(1)}, bf16[8,64,128]{2,1,0:T(8,128)(2,1)S(1)}, u32[]{:S(2)}, u32[]{:S(2)}) collective-permute-start(bf16[8,64,128]{2,1,0:T(8,128)(2,1)S(1)} %get-tuple-element.11), channel_id=1, source_target_pairs={{0,3},{1,0},{2,1},{3,2},{4,7},{5,4},{6,5},{7,6},{8,11},{9,8},{10,9... | collective-permute-start | bytes 393224 | tf_op jit(solution)/shard_map/update/ppermute | solution.py:255
  183.7 2.0 %collective-permute-done.24.refs_7_ = bf16[8,64,128]{2,1,0:T(8,128)(2,1)S(1)} collective-permute-done((bf16[8,64,128]{2,1,0:T(8,128)(2,1)S(1)}, bf16[8,64,128]{2,1,0:T(8,128)(2,1)S(1)}, u32[]{:S(2)}, u32[]{:S(2)}) %collective-permute-start.24) | collective-permute-done | bytes 131104 | tf_op jit(solution)/shard_map/update/ppermute | solution.py:255
  185.7 5.7 %collective-permute-done.23.refs_6_ = bf16[8,64,128]{2,1,0:T(8,128)(2,1)S(1)} collective-permute-done((bf16[8,64,128]{2,1,0:T(8,128)(2,1)S(1)}, bf16[8,64,128]{2,1,0:T(8,128)(2,1)S(1)}, u32[]{:S(2)}, u32[]{:S(2)}) %collective-permute-start.23) | collective-permute-done | bytes 131104 | tf_op jit(solution)/shard_map/update/ppermute | solution.py:255
  191.4 0.6 copy-done.17
  192.1 2.3 %assemble_update.1 = bf16[64,64,128]{2,1,0:T(8,128)(2,1)} custom-call(s32[4]{0:T(128)} %tie.7.at, bf16[8,64,128]{2,1,0:T(8,128)(2,1)} %get-tuple-element.16.refs_0_, bf16[8,64,128]{2,1,0:T(8,128)(2,1)} %collective-permute-done.19.refs_1_, bf16[8,64,128]{2,1,0:T(8,128)(2,1)} %collective-permute-done.20.refs_2_, bf16[8,64,128]{2,1,0:T(8,128)(2,1)} %copy-done.15, ...), custom_call_target="tpu_custom_call" | custom-call | tf_op jit(solution)/shard_map/assemble_update/pallas_call | solution.py:217
  (91 shorter events, 1.3 us)
Async XLA Ops:
  0.0 4.6 %copy-start = (f32[128,4]{0,1:T(4,128)S(1)}, f32[128,4]{0,1:T(4,128)}, u32[]{:S(2)}) copy-start(f32[128,4]{0,1:T(4,128)} %param.19) | copy-start | bytes 6148
  0.0 2.0 %copy-start.11 = (bf16[64,64,128]{2,1,0:T(8,128)(2,1)S(1)}, bf16[64,64,128]{2,1,0:T(8,128)(2,1)}, u32[]{:S(2)}) copy-start(bf16[64,64,128]{2,1,0:T(8,128)(2,1)} %param.11) | copy-start | bytes 3145732
  0.0 3.3 %copy-start.23 = (f32[128]{0:T(128)S(1)}, f32[128]{0:T(128)}, u32[]{:S(2)}) copy-start(f32[128]{0:T(128)} %param.13) | copy-start | bytes 1540
  0.0 3.3 %copy-start.24 = (f32[128]{0:T(128)S(1)}, f32[128]{0:T(128)}, u32[]{:S(2)}) copy-start(f32[128]{0:T(128)} %param.12) | copy-start | bytes 1540
  7.4 4.3 %collective-permute-start.6 = (f32[4,32,64]{1,0,2:T(4,128)S(1)}, f32[4,32,64]{1,0,2:T(4,128)S(1)}, u32[]{:S(2)}, u32[]{:S(2)}) collective-permute-start(f32[4,32,64]{1,0,2:T(4,128)S(1)} %get-tuple-element.18), channel_id=1, source_target_pairs={{0,16},{1,17},{2,18},{3,19},{4,20},{5,21},{6,22},{7,23},{8,24},{9,... | collective-permute-start | bytes 98312 | tf_op jit(solution)/shard_map/bias/ppermute | solution.py:255
  11.9 10.0 %collective-permute-start.7 = (f32[32,128]{1,0:T(8,128)S(1)}, f32[32,128]{1,0:T(8,128)S(1)}, u32[]{:S(2)}, u32[]{:S(2)}) collective-permute-start(f32[32,128]{1,0:T(8,128)S(1)} %get-tuple-element.22), channel_id=1, source_target_pairs={{0,0},{1,1},{2,2},{3,3},{4,64},{5,65},{6,66},{7,67},{8,128},{9,129... | collective-permute-start | bytes 49160 | tf_op jit(solution)/shard_map/bias/ppermute | solution.py:255
  12.7 17.9 %collective-permute-start.2 = (bf16[16,64,128]{2,1,0:T(8,128)(2,1)S(1)}, bf16[16,64,128]{2,1,0:T(8,128)(2,1)S(1)}, u32[]{:S(2)}, u32[]{:S(2)}) collective-permute-start(bf16[16,64,128]{2,1,0:T(8,128)(2,1)S(1)} %get-tuple-element.6), channel_id=1, source_target_pairs={{0,3},{1,0},{2,1},{3,2},{4,7},{5,4},{6,5},{7,6},{8,11},{9,8},{10,9... | collective-permute-start | bytes 786440 | tf_op jit(solution)/shard_map/rows/ppermute | solution.py:255
  15.4 21.8 %collective-permute-start.1 = (bf16[16,64,128]{2,1,0:T(8,128)(2,1)S(1)}, bf16[16,64,128]{2,1,0:T(8,128)(2,1)S(1)}, u32[]{:S(2)}, u32[]{:S(2)}) collective-permute-start(bf16[16,64,128]{2,1,0:T(8,128)(2,1)S(1)} %get-tuple-element.7), channel_id=1, source_target_pairs={{0,2},{1,3},{2,0},{3,1},{4,6},{5,7},{6,4},{7,5},{8,10},{9,11},{10,... | collective-permute-start | bytes 786440 | tf_op jit(solution)/shard_map/rows/ppermute | solution.py:255
  15.4 21.8 %collective-permute-start = (bf16[16,64,128]{2,1,0:T(8,128)(2,1)S(1)}, bf16[16,64,128]{2,1,0:T(8,128)(2,1)S(1)}, u32[]{:S(2)}, u32[]{:S(2)}) collective-permute-start(bf16[16,64,128]{2,1,0:T(8,128)(2,1)S(1)} %get-tuple-element.8), channel_id=1, source_target_pairs={{0,1},{1,2},{2,3},{3,0},{4,5},{5,6},{6,7},{7,4},{8,9},{9,10},{10,1... | collective-permute-start | bytes 786440 | tf_op jit(solution)/shard_map/rows/ppermute | solution.py:255
  15.7 14.7 %collective-permute-start.10 = (f32[32,128]{1,0:T(8,128)S(1)}, f32[32,128]{1,0:T(8,128)S(1)}, u32[]{:S(2)}, u32[]{:S(2)}) collective-permute-start(f32[32,128]{1,0:T(8,128)S(1)} %get-tuple-element.19), channel_id=1, source_target_pairs={{0,192},{1,193},{2,194},{3,195},{4,0},{5,1},{6,2},{7,3},{8,64},{9,... | collective-permute-start | bytes 49160 | tf_op jit(solution)/shard_map/bias/ppermute | solution.py:255
  21.9 4.4 %collective-permute-start.8 = (f32[32,128]{1,0:T(8,128)S(1)}, f32[32,128]{1,0:T(8,128)S(1)}, u32[]{:S(2)}, u32[]{:S(2)}) collective-permute-start(f32[32,128]{1,0:T(8,128)S(1)} %get-tuple-element.21), channel_id=1, source_target_pairs={{0,64},{1,65},{2,66},{3,67},{4,128},{5,129},{6,130},{7,131},{8,192... | collective-permute-start | bytes 49160 | tf_op jit(solution)/shard_map/bias/ppermute | solution.py:255
  26.2 4.2 %collective-permute-start.9 = (f32[32,128]{1,0:T(8,128)S(1)}, f32[32,128]{1,0:T(8,128)S(1)}, u32[]{:S(2)}, u32[]{:S(2)}) collective-permute-start(f32[32,128]{1,0:T(8,128)S(1)} %get-tuple-element.20), channel_id=1, source_target_pairs={{0,128},{1,129},{2,130},{3,131},{4,192},{5,193},{6,194},{7,195},{8... | collective-permute-start | bytes 49160 | tf_op jit(solution)/shard_map/bias/ppermute | solution.py:255
  37.3 6.8 %copy-start.12 = (bf16[4,16,64,128]{3,2,1,0:T(8,128)(2,1)}, bf16[4,16,64,128]{3,2,1,0:T(8,128)(2,1)S(1)}, u32[]{:S(2)}) copy-start(bf16[4,16,64,128]{3,2,1,0:T(8,128)(2,1)S(1)} %pad_maximum_fusion.rest_0_.x0) | copy-start | bytes 3145732
  37.3 30.7 %collective-permute-start.5 = (bf16[4,16,64,128]{3,2,1,0:T(8,128)(2,1)S(1)}, bf16[4,16,64,128]{3,2,1,0:T(8,128)(2,1)S(1)}, u32[]{:S(2)}, u32[]{:S(2)}) collective-permute-start(bf16[4,16,64,128]{3,2,1,0:T(8,128)(2,1)S(1)} %pad_maximum_fusion.rest_0_.x0), channel_id=1, source_target_pairs={{0,12},{1,13},{2,14},{3,15},{4,0},{5,1},{6,2},{7,3},{8,4},{9,5},{1... | collective-permute-start | bytes 3145736 | tf_op jit(solution)/shard_map/rows/ppermute | solution.py:255
  43.4 24.6 %collective-permute-start.3 = (bf16[4,16,64,128]{3,2,1,0:T(8,128)(2,1)S(1)}, bf16[4,16,64,128]{3,2,1,0:T(8,128)(2,1)S(1)}, u32[]{:S(2)}, u32[]{:S(2)}) collective-permute-start(bf16[4,16,64,128]{3,2,1,0:T(8,128)(2,1)S(1)} %pad_maximum_fusion.rest_0_.x0), channel_id=1, source_target_pairs={{0,4},{1,5},{2,6},{3,7},{4,8},{5,9},{6,10},{7,11},{8,12},{9,13},{1... | collective-permute-start | bytes 3145736 | tf_op jit(solution)/shard_map/rows/ppermute | solution.py:255
  68.0 1.0 copy-start.13
  69.0 1.0 copy-start.14
  70.0 5.3 %copy-start.3 = (f32[8,128,128]{2,1,0:T(8,128)S(1)}, f32[8,128,128]{2,1,0:T(8,128)}, u32[]{:S(2)}) copy-start(f32[8,128,128]{2,1,0:T(8,128)} %tie.5.b00) | copy-start | bytes 1572868
  70.0 28.7 %copy-start.19 = (bf16[128,128]{1,0:T(8,128)(2,1)S(1)}, bf16[128,128]{1,0:T(8,128)(2,1)}, u32[]{:S(2)}) copy-start(bf16[128,128]{1,0:T(8,128)(2,1)} %param.14) | copy-start | bytes 98308
  70.0 28.9 %copy-start.20 = (bf16[128,128]{1,0:T(8,128)(2,1)S(1)}, bf16[128,128]{1,0:T(8,128)(2,1)}, u32[]{:S(2)}) copy-start(bf16[128,128]{1,0:T(8,128)(2,1)} %param.16) | copy-start | bytes 98308
  70.0 29.0 %copy-start.21 = (bf16[128,128]{1,0:T(8,128)(2,1)S(1)}, bf16[128,128]{1,0:T(8,128)(2,1)}, u32[]{:S(2)}) copy-start(bf16[128,128]{1,0:T(8,128)(2,1)} %param.17) | copy-start | bytes 98308
  70.0 29.1 %copy-start.22 = (f32[128]{0:T(128)S(1)}, f32[128]{0:T(128)}, u32[]{:S(2)}) copy-start(f32[128]{0:T(128)} %param.18) | copy-start | bytes 1540
  70.0 32.6 %copy-start.8 = (bf16[128,128]{1,0:T(8,128)(2,1)S(1)}, bf16[128,128]{1,0:T(8,128)(2,1)}, u32[]{:S(2)}) copy-start(bf16[128,128]{1,0:T(8,128)(2,1)} %w_key.3) | copy-start | bytes 98308
  70.0 32.6 %copy-start.9 = (bf16[128,128]{1,0:T(8,128)(2,1)S(1)}, bf16[128,128]{1,0:T(8,128)(2,1)}, u32[]{:S(2)}) copy-start(bf16[128,128]{1,0:T(8,128)(2,1)} %w_out.3) | copy-start | bytes 98308
  70.0 32.6 %copy-start.10 = (f32[128]{0:T(128)S(1)}, f32[128]{0:T(128)}, u32[]{:S(2)}) copy-start(f32[128]{0:T(128)} %param.21) | copy-start | bytes 1540
  70.0 10.8 %collective-permute-start.16 = (f32[8,128,128]{2,1,0:T(8,128)}, f32[8,128,128]{2,1,0:T(8,128)S(1)}, u32[]{:S(2)}, u32[]{:S(2)}) collective-permute-start(f32[8,128,128]{2,1,0:T(8,128)} %tie.5.b00), channel_id=1, source_target_pairs={{0,192},{1,193},{2,194},{3,195},{4,196},{5,197},{6,198},{7,199},{8... | collective-permute-start | bytes 1572872 | tf_op jit(solution)/shard_map/bias/ppermute | solution.py:255
  71.4 16.7 %collective-permute-start.14 = (f32[8,128,128]{2,1,0:T(8,128)}, f32[8,128,128]{2,1,0:T(8,128)S(1)}, u32[]{:S(2)}, u32[]{:S(2)}) collective-permute-start(f32[8,128,128]{2,1,0:T(8,128)} %tie.5.b00), channel_id=1, source_target_pairs={{0,128},{1,129},{2,130},{3,131},{4,132},{5,133},{6,134},{7,135},{8... | collective-permute-start | bytes 1572872 | tf_op jit(solution)/shard_map/bias/ppermute | solution.py:255
  73.4 24.8 %collective-permute-start.12 = (f32[8,128,128]{2,1,0:T(8,128)}, f32[8,128,128]{2,1,0:T(8,128)S(1)}, u32[]{:S(2)}, u32[]{:S(2)}) collective-permute-start(f32[8,128,128]{2,1,0:T(8,128)} %tie.5.b00), channel_id=1, source_target_pairs={{0,64},{1,65},{2,66},{3,67},{4,68},{5,69},{6,70},{7,71},{8,72},{9,... | collective-permute-start | bytes 1572872 | tf_op jit(solution)/shard_map/bias/ppermute | solution.py:255
  75.3 25.8 %collective-permute-start.4 = (bf16[4,8,64,128]{3,2,1,0:T(8,128)(2,1)}, bf16[4,8,64,128]{3,2,1,0:T(8,128)(2,1)}, u32[]{:S(2)}, u32[]{:S(2)}) collective-permute-start(bf16[4,8,64,128]{3,2,1,0:T(8,128)(2,1)} %slice.40), channel_id=1, source_target_pairs={{0,4},{1,5},{2,6},{3,7},{4,8},{5,9},{6,10},{7,11},{8,12},{9,13},{1... | collective-permute-start | bytes 1572872 | tf_op jit(solution)/shard_map/rows/ppermute | solution.py:255
  75.3 27.2 %collective-permute-start.11 = (f32[8,128,128]{2,1,0:T(8,128)S(1)}, f32[8,128,128]{2,1,0:T(8,128)S(1)}, u32[]{:S(2)}, u32[]{:S(2)}) collective-permute-start(f32[8,128,128]{2,1,0:T(8,128)S(1)} %copy-done.3), channel_id=1, source_target_pairs={{0,16},{1,17},{2,18},{3,19},{4,20},{5,21},{6,22},{7,23},{8,24},{9,... | collective-permute-start | bytes 1572872 | tf_op jit(solution)/shard_map/bias/ppermute | solution.py:255
  80.9 21.7 %collective-permute-start.17 = (f32[8,128,128]{2,1,0:T(8,128)S(1)}, f32[8,128,128]{2,1,0:T(8,128)S(1)}, u32[]{:S(2)}, u32[]{:S(2)}) collective-permute-start(f32[8,128,128]{2,1,0:T(8,128)S(1)} %collective-permute-done.16.b30), channel_id=1, source_target_pairs={{0,16},{1,17},{2,18},{3,19},{4,20},{5,21},{6,22},{7,23},{8,24},{9,... | collective-permute-start | bytes 1572872 | tf_op jit(solution)/shard_map/bias/ppermute | solution.py:255
  88.1 14.4 %collective-permute-start.15 = (f32[8,128,128]{2,1,0:T(8,128)S(1)}, f32[8,128,128]{2,1,0:T(8,128)}, u32[]{:S(2)}, u32[]{:S(2)}) collective-permute-start(f32[8,128,128]{2,1,0:T(8,128)S(1)} %collective-permute-done.14.b20), channel_id=1, source_target_pairs={{0,16},{1,17},{2,18},{3,19},{4,20},{5,21},{6,22},{7,23},{8,24},{9,... | collective-permute-start | bytes 1572872 | tf_op jit(solution)/shard_map/bias/ppermute | solution.py:255
  98.2 4.3 %collective-permute-start.13 = (f32[8,128,128]{2,1,0:T(8,128)S(1)}, f32[8,128,128]{2,1,0:T(8,128)}, u32[]{:S(2)}, u32[]{:S(2)}) collective-permute-start(f32[8,128,128]{2,1,0:T(8,128)S(1)} %collective-permute-done.12.b10), channel_id=1, source_target_pairs={{0,16},{1,17},{2,18},{3,19},{4,20},{5,21},{6,22},{7,23},{8,24},{9,... | collective-permute-start | bytes 1572872 | tf_op jit(solution)/shard_map/bias/ppermute | solution.py:255
  101.1 42.8 %collective-permute-start.18 = (bf16[4,8,64,128]{3,2,1,0:T(8,128)(2,1)}, bf16[4,8,64,128]{3,2,1,0:T(8,128)(2,1)}, u32[]{:S(2)}, u32[]{:S(2)}) collective-permute-start(bf16[4,8,64,128]{3,2,1,0:T(8,128)(2,1)} %slice.41), channel_id=1, source_target_pairs={{0,12},{1,13},{2,14},{3,15},{4,0},{5,1},{6,2},{7,3},{8,4},{9,5},{1... | collective-permute-start | bytes 1572872 | tf_op jit(solution)/shard_map/rows/ppermute | solution.py:255
  102.5 35.3 %copy-start.4 = (s32[4]{0:T(128)}, s32[4]{0:T(128)S(1)}, u32[]{:S(2)}) copy-start(s32[4]{0:T(128)S(1)} %pad_add_fusion.at.array) | copy-start | bytes 52
  102.5 35.3 %copy-start.6 = (f32[8,128,128]{2,1,0:T(8,128)}, f32[8,128,128]{2,1,0:T(8,128)S(1)}, u32[]{:S(2)}) copy-start(f32[8,128,128]{2,1,0:T(8,128)S(1)} %collective-permute-done.17.b31) | copy-start | bytes 1572868
  137.8 0.8 copy-start.2
  138.7 5.2 %copy-start.5 = (s32[4]{0:T(128)S(1)}, s32[4]{0:T(128)}, u32[]{:S(2)}) copy-start(s32[4]{0:T(128)} %tie.6.at.array) | copy-start | bytes 52
  138.7 5.2 %copy-start.7 = (f32[8,128,128]{2,1,0:T(8,128)S(1)}, f32[8,128,128]{2,1,0:T(8,128)}, u32[]{:S(2)}) copy-start(f32[8,128,128]{2,1,0:T(8,128)} %copy-done.6) | copy-start | bytes 1572868
  140.6 40.8 %collective-permute-start.21 = (bf16[8,64,128]{2,1,0:T(8,128)(2,1)S(1)}, bf16[8,64,128]{2,1,0:T(8,128)(2,1)S(1)}, u32[]{:S(2)}, u32[]{:S(2)}) collective-permute-start(bf16[8,64,128]{2,1,0:T(8,128)(2,1)S(1)} %get-tuple-element.13), channel_id=1, source_target_pairs={{0,1},{1,2},{2,3},{3,0},{4,5},{5,6},{6,7},{7,4},{8,9},{9,10},{10,1... | collective-permute-start | bytes 393224 | tf_op jit(solution)/shard_map/update/ppermute | solution.py:255
  140.7 43.0 %collective-permute-start.20 = (bf16[8,64,128]{2,1,0:T(8,128)(2,1)}, bf16[8,64,128]{2,1,0:T(8,128)(2,1)}, u32[]{:S(2)}, u32[]{:S(2)}) collective-permute-start(bf16[8,64,128]{2,1,0:T(8,128)(2,1)} %get-tuple-element.14), channel_id=1, source_target_pairs={{0,2},{1,3},{2,0},{3,1},{4,6},{5,7},{6,4},{7,5},{8,10},{9,11},{10,... | collective-permute-start | bytes 393224 | tf_op jit(solution)/shard_map/update/ppermute | solution.py:255
  142.3 41.5 %collective-permute-start.19 = (bf16[8,64,128]{2,1,0:T(8,128)(2,1)}, bf16[8,64,128]{2,1,0:T(8,128)(2,1)}, u32[]{:S(2)}, u32[]{:S(2)}) collective-permute-start(bf16[8,64,128]{2,1,0:T(8,128)(2,1)} %get-tuple-element.15), channel_id=1, source_target_pairs={{0,3},{1,0},{2,1},{3,2},{4,7},{5,4},{6,5},{7,6},{8,11},{9,8},{10,9... | collective-permute-start | bytes 393224 | tf_op jit(solution)/shard_map/update/ppermute | solution.py:255
  179.0 4.7 %copy-start.1 = (bf16[4,8,64,128]{3,2,1,0:T(8,128)(2,1)}, bf16[4,8,64,128]{3,2,1,0:T(8,128)(2,1)S(1)}, u32[]{:S(2)}) copy-start(bf16[4,8,64,128]{3,2,1,0:T(8,128)(2,1)S(1)} %attention.3.rest_0_) | copy-start | bytes 1572868
  179.8 5.8 %collective-permute-start.24 = (bf16[8,64,128]{2,1,0:T(8,128)(2,1)S(1)}, bf16[8,64,128]{2,1,0:T(8,128)(2,1)S(1)}, u32[]{:S(2)}, u32[]{:S(2)}) collective-permute-start(bf16[8,64,128]{2,1,0:T(8,128)(2,1)S(1)} %get-tuple-element.9), channel_id=1, source_target_pairs={{0,1},{1,2},{2,3},{3,0},{4,5},{5,6},{6,7},{7,4},{8,9},{9,10},{10,1... | collective-permute-start | bytes 393224 | tf_op jit(solution)/shard_map/update/ppermute | solution.py:255
  180.1 11.2 %collective-permute-start.23 = (bf16[8,64,128]{2,1,0:T(8,128)(2,1)S(1)}, bf16[8,64,128]{2,1,0:T(8,128)(2,1)S(1)}, u32[]{:S(2)}, u32[]{:S(2)}) collective-permute-start(bf16[8,64,128]{2,1,0:T(8,128)(2,1)S(1)} %get-tuple-element.10), channel_id=1, source_target_pairs={{0,2},{1,3},{2,0},{3,1},{4,6},{5,7},{6,4},{7,5},{8,10},{9,11},{10,... | collective-permute-start | bytes 393224 | tf_op jit(solution)/shard_map/update/ppermute | solution.py:255
  181.3 10.0 %copy-start.15 = (bf16[8,64,128]{2,1,0:T(8,128)(2,1)}, bf16[8,64,128]{2,1,0:T(8,128)(2,1)S(1)}, u32[]{:S(2)}) copy-start(bf16[8,64,128]{2,1,0:T(8,128)(2,1)S(1)} %collective-permute-done.21.refs_3_) | copy-start | bytes 393220
  181.3 10.0 %collective-permute-start.22 = (bf16[8,64,128]{2,1,0:T(8,128)(2,1)S(1)}, bf16[8,64,128]{2,1,0:T(8,128)(2,1)S(1)}, u32[]{:S(2)}, u32[]{:S(2)}) collective-permute-start(bf16[8,64,128]{2,1,0:T(8,128)(2,1)S(1)} %get-tuple-element.11), channel_id=1, source_target_pairs={{0,3},{1,0},{2,1},{3,2},{4,7},{5,4},{6,5},{7,6},{8,11},{9,8},{10,9... | collective-permute-start | bytes 393224 | tf_op jit(solution)/shard_map/update/ppermute | solution.py:255
  185.7 5.7 %copy-start.16 = (bf16[8,64,128]{2,1,0:T(8,128)(2,1)}, bf16[8,64,128]{2,1,0:T(8,128)(2,1)S(1)}, u32[]{:S(2)}) copy-start(bf16[8,64,128]{2,1,0:T(8,128)(2,1)S(1)} %collective-permute-done.24.refs_7_) | copy-start | bytes 393220
  (2 other events, 1.4 us)
where the time goes:
time: 196 us; the launch traced here: 194 us
  Pallas kernels  72.8 us (37%)
  starting transfers between devices  51.2 us (26%)
  waiting for transfers between devices  27.2 us (14%)
  blocking collectives  23 us (12%)
  local copies, waits for them, and re-layouts  12.5 us (6%)
  other arithmetic  4.85 us (2%)
  matrix products  2.53 us (1%)
    pallas_call x2, Pallas kernels, attend(): pl.pallas_call(attend_kernel, out_shape=jax.ShapeDtypeStruct((4, count, 6...  70.4 us
    ppermute x25, starting transfers between devices, move(): return lax.ppermute(array, AXES, pairs)  51.2 us
    ppermute x25, waiting for transfers between devices, move(): return lax.ppermute(array, AXES, pairs)  27.2 us
    all_to_all x1, blocking collectives, on_device(): lax.all_to_all(jnp.broadcast_to(block[None], (8, 128, 128)), ('zh', 'zl')...  23 us
    unnamed x59, local copies, waits for them, and re-layouts  3.95 us
  transfers between devices with their start and end apart: 25, of which 8 were waited for; matrix products, arithmetic and copies ran while one was open for 4% of the time, Pallas kernels for 36%

commit v1 on v0

--- a/solution.py
+++ b/solution.py
@@ -49,11 +49,15 @@
     gate_shift,
     w_out,
     out_shift,
-    out,
+    out0,
+    out1,
+    out2,
+    out3,
     key_ref,
     value_ref,
     score_ref,
     attended_ref,
+    update_ref,
 ):
     rows = (x0, x1, x2, x3)
     bias = ((b00, b01), (b10, b11), (b20, b21), (b30, b31))
@@ -64,7 +68,7 @@
     kept = [{} for _ in range(TOGETHER)]
 
     def project_query(r):
-        tokens = jnp.concatenate([x0[slot[part], r] for part in range(4)], axis=0)
+        tokens = jnp.concatenate([x0[r, slot[part]] for part in range(4)], axis=0)
         query = (dot_t(w_query_t[...], tokens) * (1.0 / math.sqrt(DEPTH))).astype(BF)
         gate = jax.nn.sigmoid(dot_t(w_gate_t[...], tokens) + gate_shift[...])
         of_head = lax.broadcasted_iota(jnp.int32, query.shape, 0) // DEPTH
@@ -74,7 +78,7 @@
     def project(r):
         tokens = jnp.concatenate(
             [
-                rows[t][s, r, pl.ds(halves[half], 32), :]
+                rows[t][r, s, pl.ds(halves[half], 32), :]
                 for half in range(2)
                 for s in range(4)
                 for t in range(4)
@@ -128,9 +132,10 @@
         update = lax.dot_general(
             gated, w_out[...], (((0,), (0,)), ((), ())), preferred_element_type=F32
         )
-        update = (update + out_shift[...]).astype(BF)
-        for part in range(4):
-            out[slot[part], r] = update[part * 64 : (part + 1) * 64]
+        update_ref[r] = (update + out_shift[...]).astype(BF)
+        for s, out in enumerate((out0, out1, out2, out3)):
+            start = pl.multiple_of(slot[s] * 64, 64)
+            out[r] = update_ref[r, pl.ds(start, 64), :]
 
     for r in range(TOGETHER):
         project(r)
@@ -161,27 +166,28 @@
 def attend(at, rows, first, biases, *weights):
     count = 16 // CHUNKS
     whole = lambda a: pl.BlockSpec(a.shape, lambda i, at: (0,) * a.ndim)
-    block = (4, TOGETHER, 64, 128)
+    block = (TOGETHER, 4, 64, 128)
     specs = [
-        pl.BlockSpec(block, lambda i, at, start=start // TOGETHER: (0, i + start, 0, 0))
+        pl.BlockSpec(block, lambda i, at, start=start // TOGETHER: (i + start, 0, 0, 0))
         for start in first
     ]
     biases = [b for pair in biases for b in pair]
     return pl.pallas_call(
         attend_kernel,
-        out_shape=jax.ShapeDtypeStruct((4, count, 64, 128), BF),
+        out_shape=[jax.ShapeDtypeStruct((count, 64, 128), BF)] * 4,
         grid_spec=pltpu.PrefetchScalarGridSpec(
             num_scalar_prefetch=1,
             grid=(count // TOGETHER,),
             in_specs=specs
             + [whole(a) for a in biases]
             + [whole(a) for a in weights],
-            out_specs=pl.BlockSpec(block, lambda i, at: (0, i, 0, 0)),
+            out_specs=[pl.BlockSpec((TOGETHER, 64, 128), lambda i, at: (i, 0, 0))] * 4,
             scratch_shapes=[
                 pltpu.VMEM((TOGETHER, 1024, 128), BF),
                 pltpu.VMEM((TOGETHER, 128, 1024), BF),
                 pltpu.VMEM((TOGETHER, 4, 8, 128, 256), F32),
                 pltpu.VMEM((TOGETHER, 128, 256), F32),
+                pltpu.VMEM((TOGETHER, 256, 128), BF),
             ],
         ),
         compiler_params=pltpu.CompilerParams(
@@ -196,21 +202,47 @@
     )(at, *rows, *biases, *weights)
 
 
-def normalize(values, gain, shift):
-    values = values.astype(F32)
-    mean = jnp.mean(values, axis=-1, keepdims=True)
-    centred = values - mean
-    spread = jnp.mean(centred * centred, axis=-1, keepdims=True)
-    return (centred * lax.rsqrt(spread + 1e-05) * gain + shift).astype(BF)
+def normalize_kernel(at, pair, gain, shift, normed, cut0, cut1, cut2, cut3):
+    for step, cut in enumerate((cut0, cut1, cut2, cut3)):
+        start = lax.rem(at[2] + step, 4) * 16
+        for i in range(0, 16, 4):
+            values = pair[pl.ds(start + i, 4)].astype(F32)
+            mean = jnp.mean(values, axis=-1, keepdims=True)
+            centred = values - mean
+            spread = jnp.mean(centred * centred, axis=-1, keepdims=True)
+            scaled = centred * lax.rsqrt(spread + 1e-05) * gain[...] + shift[...]
+            scaled = scaled.astype(BF)
+            normed[pl.ds(start + i, 4)] = scaled
+            cut[i : i + 4] = scaled
+
+
+def normalize(at, pair, gain, shift):
+    vmem = pl.BlockSpec(memory_space=pltpu.VMEM)
+    cut = jax.ShapeDtypeStruct((16, 64, 128), BF)
+    normed, *cuts = pl.pallas_call(
+        normalize_kernel,
+        out_shape=[jax.ShapeDtypeStruct(pair.shape, BF)] + [cut] * 4,
+        in_specs=[pl.BlockSpec(memory_space=pltpu.SMEM), vmem, vmem, vmem],
+        out_specs=[vmem] * 5,
+        name="normalize",
+    )(at, pair, gain[None, None], shift[None, None])
+    return normed, cuts
 
 
 def assemble_kernel(at, *refs):
-    *blocks, out = refs
+    *blocks, out, done = refs
     count = blocks[0].shape[0]
+    copies = []
     for i, block in enumerate(blocks):
         chunk, step = divmod(i, 4)
         start = lax.rem(at[2] + step, 4) * 16 + chunk * count
-        out[pl.ds(start, count)] = block[...]
+        copies.append(
+            pltpu.make_async_copy(block, out.at[pl.ds(start, count)], done.at[i])
+        )
+    for copy in copies:
+        copy.start()
+    for copy in copies:
+        copy.wait()
 
 
 def assemble(at, blocks):
@@ -218,8 +250,9 @@
         assemble_kernel,
         out_shape=jax.ShapeDtypeStruct((64, 64, 128), BF),
         in_specs=[pl.BlockSpec(memory_space=pltpu.SMEM)]
-        + [pl.BlockSpec(memory_space=pltpu.VMEM)] * len(blocks),
-        out_specs=pl.BlockSpec(memory_space=pltpu.VMEM),
+        + [pl.BlockSpec(memory_space=pl.ANY)] * len(blocks),
+        out_specs=pl.BlockSpec(memory_space=pl.ANY),
+        scratch_shapes=[pltpu.SemaphoreType.DMA((len(blocks),))],
         name="assemble_update",
     )(at, *blocks)
 
@@ -278,22 +311,22 @@
 ):
     y, core, x, zl = (lax.axis_index(name) for name in ("y", "core", "x", "zl"))
     place = jnp.stack([y, x, zl, core]).astype(jnp.int32)
-    normed = normalize(pair, norm_gain, norm_shift)
+    normed, cuts = normalize(place, pair, norm_gain, norm_shift)
     count = 16 // CHUNKS
 
     with jax.named_scope("rows"):
         pieces = []
         for step in range(4):
-            part = lax.dynamic_slice_in_dim(normed, (zl + step) % 4 * 16, 16, 0)
+            part = cuts[step]
             if step:
                 part = move(part, lambda y, z, core, x: (y, turn(z, step), core, x))
             pieces.append(part)
-        here = jnp.stack(pieces)
+        here = jnp.stack(pieces, axis=1)
         left = move(here, lambda y, z, core, x: (y, z, core, x + 1))
         right = move(here, lambda y, z, core, x: (y, z, core, x - 1))
         across = (
-            move(left[:, :count], lambda y, z, core, x: (y, z, core, x + 1)),
-            move(right[:, count:], lambda y, z, core, x: (y, z, core, x - 1)),
+            move(left[:count], lambda y, z, core, x: (y, z, core, x + 1)),
+            move(right[count:], lambda y, z, core, x: (y, z, core, x - 1)),
         )
     with jax.named_scope("bias"):
         tile = jnp.einsum(
@@ -311,7 +344,7 @@
             rounds.append(move(part, lambda y, z, core, x: (x + step, z, core, y)))
         rounds = jnp.stack(rounds + rounds[:3])
         block = lax.dynamic_slice_in_dim(rounds, (y - x) % 4, 4, 0).reshape(128, 128)
-        block = after(block, here)
+        block = after(block, *[piece[0] for piece in pieces[1:]])
         along_z = lax.all_to_all(
             jnp.broadcast_to(block[None], (8, 128, 128)),
             ("zh", "zl"),
@@ -320,7 +353,7 @@
             tiled=True,
         )
     with jax.named_scope("bias"):
-        along_z = after(along_z, left, right)
+        along_z = after(along_z, left[0, 0], right[0, 0])
         biases = []
         for step in range(4):
             moved = along_z
@@ -328,6 +361,7 @@
                 moved = move(along_z, lambda y, z, core, x: (y + step, z, core, x))
             biases.append((moved, swap_cores(moved)))
     blocks = []
+    start = place
     for chunk in range(CHUNKS):
         with jax.named_scope("attention"):
             part = attend(
@@ -343,14 +377,14 @@
                 w_out,
                 out_shift[None],
             )
-            place = after(place, part)
+            place = after(place, part[0][0])
         with jax.named_scope("update"):
             for step in range(4):
                 back = part[step]
                 if step:
                     back = move(back, lambda y, z, core, x: (y, turn(z, -step), core, x))
                 blocks.append(back)
-    return assemble(place, blocks)
+    return assemble(start, blocks)
 
 
 def solution(mesh):

time: 196 us -> 244 us (1.24)
  Pallas kernels: 72.8 us -> 108 us
  waiting for transfers between devices: 27.2 us -> 54 us
  blocking collectives: 23 us -> 0 us
  local copies, waits for them, and re-layouts: 12.5 us -> 20.4 us
  starting transfers between devices: 51.2 us -> 56.1 us
  other arithmetic: 4.85 us -> 0.82 us
    pallas_call x1, Pallas kernels: 2.33 us -> 33.6 us  [assemble(): pl.pallas_call(assemble_kernel, out_shape=jax.ShapeDtypeStruct((64, 64, 1...]
    all_to_all x1 -> x0, blocking collectives: 23 us -> none  [on_device(): lax.all_to_all(jnp.broadcast_to(block[None], (8, 128, 128)), ('zh', 'zl')...]
    ppermute x25, waiting for transfers between devices: 27.2 us -> 48.4 us  [move(): return lax.ppermute(array, AXES, pairs)]
    all_to_all x0 -> x1, starting transfers between devices: none -> 11.5 us  [on_device(): lax.all_to_all(jnp.broadcast_to(block[None], (8, 128, 128)), ('zh', 'zl')...]
    ppermute x25, starting transfers between devices: 51.2 us -> 44.6 us  [move(): return lax.ppermute(array, AXES, pairs)]
    unnamed x59 -> x78, local copies, waits for them, and re-layouts: 3.95 us -> 10.2 us
    all_to_all x0 -> x1, waiting for transfers between devices: none -> 5.56 us  [on_device(): lax.all_to_all(jnp.broadcast_to(block[None], (8, 128, 128)), ('zh', 'zl')...]
    pallas_call x2 -> x3, Pallas kernels: 70.4 us -> 74.6 us  [the longest x2 70.4 us: attend(): pl.pallas_call(attend_kernel, out_shape=[jax.ShapeDtypeStruct((count, 64,...]
  transfers between devices with their start and end apart: 25 -> 26, of which waited for: 8 -> 13; matrix products, arithmetic and copies ran while one was open for 4% -> 4% of each run, Pallas kernels for 36% -> 14%
where the time goes in v1:
time: 244 us
  Pallas kernels  108 us (44%)
  starting transfers between devices  56.1 us (23%)
  waiting for transfers between devices  54 us (22%)
  local copies, waits for them, and re-layouts  20.4 us (8%)
  matrix products  3.73 us (2%)
    pallas_call x2, Pallas kernels, attend(): pl.pallas_call(attend_kernel, out_shape=[jax.ShapeDtypeStruct((count, 64,...  70.4 us
    ppermute x25, waiting for transfers between devices, move(): return lax.ppermute(array, AXES, pairs)  48.4 us
    ppermute x25, starting transfers between devices, move(): return lax.ppermute(array, AXES, pairs)  44.6 us
    pallas_call x1, Pallas kernels, assemble(): pl.pallas_call(assemble_kernel, out_shape=jax.ShapeDtypeStruct((64, 64, 1...  33.6 us
    all_to_all x1, starting transfers between devices, on_device(): lax.all_to_all(jnp.broadcast_to(block[None], (8, 128, 128)), ('zh', 'zl')...  11.5 us
    unnamed x78, local copies, waits for them, and re-layouts  10.2 us
    all_to_all x1, waiting for transfers between devices, on_device(): lax.all_to_all(jnp.broadcast_to(block[None], (8, 128, 128)), ('zh', 'zl')...  5.56 us
  transfers between devices with their start and end apart: 26, of which 13 were waited for; matrix products, arithmetic and copies ran while one was open for 4% of the time, Pallas kernels for 14%

profile of v1, /device:TPU:1, one launch (start us, length us, event | category | flops | bytes accessed | tf_op | source)
XLA Modules:
  0.0 243.6 jit_solution(4677655524369267380)
XLA Ops:
  0.6 4.1 %normalize.1 = (bf16[64,64,128]{2,1,0:T(8,128)(2,1)}, bf16[16,64,128]{2,1,0:T(8,128)(2,1)}, bf16[16,64,128]{2,1,0:T(8,128)(2,1)}, bf16[16,64,128]{2,1,0:T(8,128)(2,1)}, bf16[16,64,128]{2,1,0:T(8,128)(2,1)}) custom-call(s32[4]{0:T(128)} %pad_add_fusion.at, bf16[64,64,128]{2,1,0:T(8,128)(2,1)} %pair.1, f32[1,1,128]{2,1,0:T(1,128)} %bitcast.68, ...), custom_call_target="tpu_custom_call" | custom-call | tf_op jit(solution)/shard_map/normalize/pallas_call | solution.py:222
  4.7 3.7 %fusion = f32[64,64,4]{1,2,0:T(4,128)S(1)} fusion(bf16[64,64,128]{2,1,0:T(8,128)(2,1)} %get-tuple-element.22, f32[128,4]{0,1:T(4,128)S(1)} %copy-done), kind=kOutput, calls=%fused_computation.21 | convolution fusion | flops 25165824 | bytes 1116160 | tf_op jit(solution)/shard_map/bias/jkc,ch->hkj/dot_general | solution.py:332
  8.7 3.3 %collective-permute-start.6 = (f32[4,32,64]{1,0,2:T(4,128)S(1)}, f32[4,32,64]{1,0,2:T(4,128)S(1)}, u32[]{:S(2)}, u32[]{:S(2)}) collective-permute-start(f32[4,32,64]{1,0,2:T(4,128)S(1)} %get-tuple-element.32), channel_id=1, source_target_pairs={{0,16},{1,17},{2,18},{3,19},{4,20},{5,21},{6,22},{7,23},{8,24},{9,... | collective-permute-start | bytes 98312 | tf_op jit(solution)/shard_map/bias/ppermute | solution.py:288
  12.1 0.9 collective-permute-done.6
  13.2 0.8 collective-permute-start.7
  14.2 2.9 %collective-permute-start.1 = (bf16[16,64,128]{2,1,0:T(8,128)(2,1)S(1)}, bf16[16,64,128]{2,1,0:T(8,128)(2,1)S(1)}, u32[]{:S(2)}, u32[]{:S(2)}) collective-permute-start(bf16[16,64,128]{2,1,0:T(8,128)(2,1)S(1)} %copy-done.32), channel_id=1, source_target_pairs={{0,2},{1,3},{2,0},{3,1},{4,6},{5,7},{6,4},{7,5},{8,10},{9,11},{10,... | collective-permute-start | bytes 786440 | tf_op jit(solution)/shard_map/rows/ppermute | solution.py:288
  17.0 0.7 collective-permute-start.2
  17.8 6.1 %collective-permute-start.10 = (f32[32,128]{1,0:T(8,128)S(1)}, f32[32,128]{1,0:T(8,128)S(1)}, u32[]{:S(2)}, u32[]{:S(2)}) collective-permute-start(f32[32,128]{1,0:T(8,128)S(1)} %get-tuple-element.33), channel_id=1, source_target_pairs={{0,192},{1,193},{2,194},{3,195},{4,0},{5,1},{6,2},{7,3},{8,64},{9,... | collective-permute-start | bytes 49160 | tf_op jit(solution)/shard_map/bias/ppermute | solution.py:288
  23.9 1.9 collective-permute-start.8
  25.8 2.4 collective-permute-done.8
  28.1 3.3 %collective-permute-start.9 = (f32[32,128]{1,0:T(8,128)S(1)}, f32[32,128]{1,0:T(8,128)S(1)}, u32[]{:S(2)}, u32[]{:S(2)}) collective-permute-start(f32[32,128]{1,0:T(8,128)S(1)} %get-tuple-element.34), channel_id=1, source_target_pairs={{0,128},{1,129},{2,130},{3,131},{4,192},{5,193},{6,194},{7,195},{8... | collective-permute-start | bytes 49160 | tf_op jit(solution)/shard_map/bias/ppermute | solution.py:288
  31.5 0.9 collective-permute-done.9
  33.0 1.7 collective-permute-done.1
  34.9 6.5 %collective-permute-start.5 = (bf16[16,4,64,128]{3,2,1,0:T(8,128)(2,1)S(1)}, bf16[16,4,64,128]{3,2,1,0:T(8,128)(2,1)S(1)}, u32[]{:S(2)}, u32[]{:S(2)}) collective-permute-start(bf16[16,4,64,128]{3,2,1,0:T(8,128)(2,1)S(1)} %pad_maximum_fusion.x0), channel_id=1, source_target_pairs={{0,12},{1,13},{2,14},{3,15},{4,0},{5,1},{6,2},{7,3},{8,4},{9,5},{1... | collective-permute-start | bytes 3145736 | tf_op jit(solution)/shard_map/rows/ppermute | solution.py:288
  43.2 1.7 broadcast_in_dim.22
  44.9 11.5 %all-to-all-start = ((f32[8,128,128]{2,1,0:T(8,128)}), f32[8,128,128]{2,1,0:T(8,128)S(1)}, u32[]{:S(2)}, u32[]{:S(2)}) async-start(f32[8,128,128]{2,1,0:T(8,128)} %broadcast_in_dim.22), calls=%async_computation | async-start | bytes 1048576 | tf_op jit(solution)/shard_map/bias/all_to_all | solution.py:348
  56.3 7.0 %collective-permute-done.5.x3 = bf16[16,4,64,128]{3,2,1,0:T(8,128)(2,1)S(1)} collective-permute-done((bf16[16,4,64,128]{3,2,1,0:T(8,128)(2,1)S(1)}, bf16[16,4,64,128]{3,2,1,0:T(8,128)(2,1)S(1)}, u32[]{:S(2)}, u32[]{:S(2)}) %collective-permute-start.5) | collective-permute-done | bytes 1048608 | tf_op jit(solution)/shard_map/rows/ppermute | solution.py:288
  63.9 2.6 %collective-permute-done.3.x1 = bf16[16,4,64,128]{3,2,1,0:T(8,128)(2,1)} collective-permute-done((bf16[16,4,64,128]{3,2,1,0:T(8,128)(2,1)S(1)}, bf16[16,4,64,128]{3,2,1,0:T(8,128)(2,1)}, u32[]{:S(2)}, u32[]{:S(2)}) %collective-permute-start.3) | collective-permute-done | bytes 1048608 | tf_op jit(solution)/shard_map/rows/ppermute | solution.py:288
  66.5 1.3 slice_bitcast_fusion.1.rest_0_
  67.8 5.6 %all-to-all-done.array = f32[8,128,128]{2,1,0:T(8,128)S(1)} async-done(((f32[8,128,128]{2,1,0:T(8,128)}), f32[8,128,128]{2,1,0:T(8,128)S(1)}, u32[]{:S(2)}, u32[]{:S(2)}) %all-to-all-start) | async-done | bytes 524320 | tf_op jit(solution)/shard_map/bias/all_to_all | solution.py:348
  73.4 0.8 copy-done.1
  74.2 1.2 collective-permute-start.16
  75.4 2.1 collective-permute-start.14
  77.5 1.1 slice.32
  78.9 2.4 collective-permute-start.11
  81.3 5.4 %collective-permute-done.16.b30 = f32[8,128,128]{2,1,0:T(8,128)S(1)} collective-permute-done((f32[8,128,128]{2,1,0:T(8,128)}, f32[8,128,128]{2,1,0:T(8,128)S(1)}, u32[]{:S(2)}, u32[]{:S(2)}) %collective-permute-start.16) | collective-permute-done | bytes 524320 | tf_op jit(solution)/shard_map/bias/ppermute | solution.py:288
  86.7 4.0 %collective-permute-start.17 = (f32[8,128,128]{2,1,0:T(8,128)S(1)}, f32[8,128,128]{2,1,0:T(8,128)S(1)}, u32[]{:S(2)}, u32[]{:S(2)}) collective-permute-start(f32[8,128,128]{2,1,0:T(8,128)S(1)} %collective-permute-done.16.b30), channel_id=1, source_target_pairs={{0,16},{1,17},{2,18},{3,19},{4,20},{5,21},{6,22},{7,23},{8,24},{9,... | collective-permute-start | bytes 1572872 | tf_op jit(solution)/shard_map/bias/ppermute | solution.py:288
  90.7 3.2 %collective-permute-start.15 = (f32[8,128,128]{2,1,0:T(8,128)S(1)}, f32[8,128,128]{2,1,0:T(8,128)}, u32[]{:S(2)}, u32[]{:S(2)}) collective-permute-start(f32[8,128,128]{2,1,0:T(8,128)S(1)} %collective-permute-done.14.b20), channel_id=1, source_target_pairs={{0,16},{1,17},{2,18},{3,19},{4,20},{5,21},{6,22},{7,23},{8,24},{9,... | collective-permute-start | bytes 1572872 | tf_op jit(solution)/shard_map/bias/ppermute | solution.py:288
  93.9 8.3 %collective-permute-done.12.b10 = f32[8,128,128]{2,1,0:T(8,128)S(1)} collective-permute-done((f32[8,128,128]{2,1,0:T(8,128)}, f32[8,128,128]{2,1,0:T(8,128)S(1)}, u32[]{:S(2)}, u32[]{:S(2)}) %collective-permute-start.12) | collective-permute-done | bytes 524320 | tf_op jit(solution)/shard_map/bias/ppermute | solution.py:288
  102.7 1.9 slice.38
  104.6 0.8 copy-done.7
  105.4 1.3 collective-permute-start.21
  107.4 0.6 copy-done.28
  108.2 0.6 copy-done.29
  108.9 0.7 copy-done.30
  110.4 1.0 copy-done.8
  111.5 35.1 %attention.2 = (bf16[8,64,128]{2,1,0:T(8,128)(2,1)S(1)}, bf16[8,64,128]{2,1,0:T(8,128)(2,1)S(1)}, bf16[8,64,128]{2,1,0:T(8,128)(2,1)S(1)}, bf16[8,64,128]{2,1,0:T(8,128)(2,1)S(1)}) custom-call(s32[4]{0:T(128)S(1)} %copy-done.5, bf16[16,4,64,128]{3,2,1,0:T(8,128)(2,1)} %copy-done.18, bf16[16,4,64,128]{3,2,1,0:T(8,128)(2,1)} %collective-permute-done.3.x1, ...), custom_call_target="tpu_custom_call" | custom-call | flops 2400000000 | bytes 8388608 | tf_op jit(solution)/shard_map/attention/attention/pallas_call | solution.py:175
  146.5 0.6 copy-done.9
  147.2 0.7 copy-done.11
  147.9 0.7 copy-done.13
  149.2 0.7 copy-done.6
  149.8 35.4 %attention.3 = (bf16[8,64,128]{2,1,0:T(8,128)(2,1)S(1)}, bf16[8,64,128]{2,1,0:T(8,128)(2,1)S(1)}, bf16[8,64,128]{2,1,0:T(8,128)(2,1)S(1)}, bf16[8,64,128]{2,1,0:T(8,128)(2,1)S(1)}) custom-call(s32[4]{0:T(128)S(1)} %copy-done.6, bf16[16,4,64,128]{3,2,1,0:T(8,128)(2,1)} %copy-done.18, bf16[16,4,64,128]{3,2,1,0:T(8,128)(2,1)} %collective-permute-done.3.x1, ...), custom_call_target="tpu_custom_call" | custom-call | flops 2400000000 | bytes 8388608 | tf_op jit(solution)/shard_map/attention/attention/pallas_call | solution.py:175
  186.1 1.2 collective-permute-start.24
  187.3 2.1 collective-permute-start.18
  189.8 1.5 collective-permute-done.22.refs_5_
  191.3 6.7 %collective-permute-done.23.refs_6_ = bf16[8,64,128]{2,1,0:T(8,128)(2,1)S(1)} collective-permute-done((bf16[8,64,128]{2,1,0:T(8,128)(2,1)S(1)}, bf16[8,64,128]{2,1,0:T(8,128)(2,1)S(1)}, u32[]{:S(2)}, u32[]{:S(2)}) %collective-permute-start.23) | collective-permute-done | bytes 131104 | tf_op jit(solution)/shard_map/update/ppermute | solution.py:288
  198.6 10.6 %collective-permute-done.19.refs_2_ = bf16[8,64,128]{2,1,0:T(8,128)(2,1)S(1)} collective-permute-done((bf16[8,64,128]{2,1,0:T(8,128)(2,1)S(1)}, bf16[8,64,128]{2,1,0:T(8,128)(2,1)S(1)}, u32[]{:S(2)}, u32[]{:S(2)}) %collective-permute-start.19) | collective-permute-done | bytes 131104 | tf_op jit(solution)/shard_map/update/ppermute | solution.py:288
  209.9 33.6 %assemble_update.1 = bf16[64,64,128]{2,1,0:T(8,128)(2,1)} custom-call(s32[4]{0:T(128)} %pad_add_fusion.at, bf16[8,64,128]{2,1,0:T(8,128)(2,1)} %copy-done.3, bf16[8,64,128]{2,1,0:T(8,128)(2,1)} %copy-done.24, bf16[8,64,128]{2,1,0:T(8,128)(2,1)} %copy-done.25, bf16[8,64,128]{2,1,0:T(8,128)(2,1)} %copy-done.26, bf16[8,64,128]{2,1,0:T(8,128)(2,1)} %copy-done.4, ...), custom_call_target="tpu_custom_call" | custom-call | tf_op jit(solution)/shard_map/assemble_update/pallas_call | solution.py:249
  (109 shorter events, 10.2 us)
Async XLA Ops:
  0.0 4.7 %copy-start = (f32[128,4]{0,1:T(4,128)S(1)}, f32[128,4]{0,1:T(4,128)}, u32[]{:S(2)}) copy-start(f32[128,4]{0,1:T(4,128)} %param.19) | copy-start | bytes 6148
  8.7 4.3 %collective-permute-start.6 = (f32[4,32,64]{1,0,2:T(4,128)S(1)}, f32[4,32,64]{1,0,2:T(4,128)S(1)}, u32[]{:S(2)}, u32[]{:S(2)}) collective-permute-start(f32[4,32,64]{1,0,2:T(4,128)S(1)} %get-tuple-element.32), channel_id=1, source_target_pairs={{0,16},{1,17},{2,18},{3,19},{4,20},{5,21},{6,22},{7,23},{8,24},{9,... | collective-permute-start | bytes 98312 | tf_op jit(solution)/shard_map/bias/ppermute | solution.py:288
  12.0 2.0 copy-start.33
  12.1 2.0 copy-start.32
  12.1 4.9 %copy-start.31 = (bf16[16,64,128]{2,1,0:T(8,128)(2,1)S(1)}, bf16[16,64,128]{2,1,0:T(8,128)(2,1)}, u32[]{:S(2)}) copy-start(bf16[16,64,128]{2,1,0:T(8,128)(2,1)} %get-tuple-element.21) | copy-start | bytes 786436
  13.2 21.5 %copy-start.20 = (bf16[16,64,128]{2,1,0:T(8,128)(2,1)S(1)}, bf16[16,64,128]{2,1,0:T(8,128)(2,1)}, u32[]{:S(2)}) copy-start(bf16[16,64,128]{2,1,0:T(8,128)(2,1)} %get-tuple-element.18) | copy-start | bytes 786436
  13.2 10.6 %collective-permute-start.7 = (f32[32,128]{1,0:T(8,128)S(1)}, f32[32,128]{1,0:T(8,128)S(1)}, u32[]{:S(2)}, u32[]{:S(2)}) collective-permute-start(f32[32,128]{1,0:T(8,128)S(1)} %get-tuple-element.36), channel_id=1, source_target_pairs={{0,0},{1,1},{2,2},{3,3},{4,64},{5,65},{6,66},{7,67},{8,128},{9,129... | collective-permute-start | bytes 49160 | tf_op jit(solution)/shard_map/bias/ppermute | solution.py:288
  14.1 19.0 %collective-permute-start = (bf16[16,64,128]{2,1,0:T(8,128)(2,1)S(1)}, bf16[16,64,128]{2,1,0:T(8,128)(2,1)S(1)}, u32[]{:S(2)}, u32[]{:S(2)}) collective-permute-start(bf16[16,64,128]{2,1,0:T(8,128)(2,1)S(1)} %copy-done.33), channel_id=1, source_target_pairs={{0,1},{1,2},{2,3},{3,0},{4,5},{5,6},{6,7},{7,4},{8,9},{9,10},{10,1... | collective-permute-start | bytes 786440 | tf_op jit(solution)/shard_map/rows/ppermute | solution.py:288
  14.2 20.6 %collective-permute-start.1 = (bf16[16,64,128]{2,1,0:T(8,128)(2,1)S(1)}, bf16[16,64,128]{2,1,0:T(8,128)(2,1)S(1)}, u32[]{:S(2)}, u32[]{:S(2)}) collective-permute-start(bf16[16,64,128]{2,1,0:T(8,128)(2,1)S(1)} %copy-done.32), channel_id=1, source_target_pairs={{0,2},{1,3},{2,0},{3,1},{4,6},{5,7},{6,4},{7,5},{8,10},{9,11},{10,... | collective-permute-start | bytes 786440 | tf_op jit(solution)/shard_map/rows/ppermute | solution.py:288
  17.0 17.7 %collective-permute-start.2 = (bf16[16,64,128]{2,1,0:T(8,128)(2,1)S(1)}, bf16[16,64,128]{2,1,0:T(8,128)(2,1)S(1)}, u32[]{:S(2)}, u32[]{:S(2)}) collective-permute-start(bf16[16,64,128]{2,1,0:T(8,128)(2,1)S(1)} %copy-done.31), channel_id=1, source_target_pairs={{0,3},{1,0},{2,1},{3,2},{4,7},{5,4},{6,5},{7,6},{8,11},{9,8},{10,9... | collective-permute-start | bytes 786440 | tf_op jit(solution)/shard_map/rows/ppermute | solution.py:288
  17.8 14.6 %collective-permute-start.10 = (f32[32,128]{1,0:T(8,128)S(1)}, f32[32,128]{1,0:T(8,128)S(1)}, u32[]{:S(2)}, u32[]{:S(2)}) collective-permute-start(f32[32,128]{1,0:T(8,128)S(1)} %get-tuple-element.33), channel_id=1, source_target_pairs={{0,192},{1,193},{2,194},{3,195},{4,0},{5,1},{6,2},{7,3},{8,64},{9,... | collective-permute-start | bytes 49160 | tf_op jit(solution)/shard_map/bias/ppermute | solution.py:288
  23.9 4.2 %collective-permute-start.8 = (f32[32,128]{1,0:T(8,128)S(1)}, f32[32,128]{1,0:T(8,128)S(1)}, u32[]{:S(2)}, u32[]{:S(2)}) collective-permute-start(f32[32,128]{1,0:T(8,128)S(1)} %get-tuple-element.35), channel_id=1, source_target_pairs={{0,64},{1,65},{2,66},{3,67},{4,128},{5,129},{6,130},{7,131},{8,192... | collective-permute-start | bytes 49160 | tf_op jit(solution)/shard_map/bias/ppermute | solution.py:288
  28.1 4.2 %collective-permute-start.9 = (f32[32,128]{1,0:T(8,128)S(1)}, f32[32,128]{1,0:T(8,128)S(1)}, u32[]{:S(2)}, u32[]{:S(2)}) collective-permute-start(f32[32,128]{1,0:T(8,128)S(1)} %get-tuple-element.34), channel_id=1, source_target_pairs={{0,128},{1,129},{2,130},{3,131},{4,192},{5,193},{6,194},{7,195},{8... | collective-permute-start | bytes 49160 | tf_op jit(solution)/shard_map/bias/ppermute | solution.py:288
  34.9 38.5 %copy-start.18 = (bf16[16,4,64,128]{3,2,1,0:T(8,128)(2,1)}, bf16[16,4,64,128]{3,2,1,0:T(8,128)(2,1)S(1)}, u32[]{:S(2)}) copy-start(bf16[16,4,64,128]{3,2,1,0:T(8,128)(2,1)S(1)} %pad_maximum_fusion.x0) | copy-start | bytes 3145732
  34.9 28.4 %collective-permute-start.5 = (bf16[16,4,64,128]{3,2,1,0:T(8,128)(2,1)S(1)}, bf16[16,4,64,128]{3,2,1,0:T(8,128)(2,1)S(1)}, u32[]{:S(2)}, u32[]{:S(2)}) collective-permute-start(bf16[16,4,64,128]{3,2,1,0:T(8,128)(2,1)S(1)} %pad_maximum_fusion.x0), channel_id=1, source_target_pairs={{0,12},{1,13},{2,14},{3,15},{4,0},{5,1},{6,2},{7,3},{8,4},{9,5},{1... | collective-permute-start | bytes 3145736 | tf_op jit(solution)/shard_map/rows/ppermute | solution.py:288
  41.4 25.1 %collective-permute-start.3 = (bf16[16,4,64,128]{3,2,1,0:T(8,128)(2,1)S(1)}, bf16[16,4,64,128]{3,2,1,0:T(8,128)(2,1)}, u32[]{:S(2)}, u32[]{:S(2)}) collective-permute-start(bf16[16,4,64,128]{3,2,1,0:T(8,128)(2,1)S(1)} %pad_maximum_fusion.x0), channel_id=1, source_target_pairs={{0,4},{1,5},{2,6},{3,7},{4,8},{5,9},{6,10},{7,11},{8,12},{9,13},{1... | collective-permute-start | bytes 3145736 | tf_op jit(solution)/shard_map/rows/ppermute | solution.py:288
  44.9 28.6 %all-to-all-start = ((f32[8,128,128]{2,1,0:T(8,128)}), f32[8,128,128]{2,1,0:T(8,128)S(1)}, u32[]{:S(2)}, u32[]{:S(2)}) async-start(f32[8,128,128]{2,1,0:T(8,128)} %broadcast_in_dim.22), calls=%async_computation | async-start | bytes 1048576 | tf_op jit(solution)/shard_map/bias/all_to_all | solution.py:348
  63.3 12.1 %copy-start.19 = (bf16[16,4,64,128]{3,2,1,0:T(8,128)(2,1)}, bf16[16,4,64,128]{3,2,1,0:T(8,128)(2,1)S(1)}, u32[]{:S(2)}) copy-start(bf16[16,4,64,128]{3,2,1,0:T(8,128)(2,1)S(1)} %collective-permute-done.5.x3) | copy-start | bytes 3145732
  73.4 0.8 copy-start.1
  74.2 4.7 %copy-start.2 = (f32[8,128,128]{2,1,0:T(8,128)S(1)}, f32[8,128,128]{2,1,0:T(8,128)}, u32[]{:S(2)}) copy-start(f32[8,128,128]{2,1,0:T(8,128)} %tie.4.b00) | copy-start | bytes 1572868
  74.2 12.5 %collective-permute-start.16 = (f32[8,128,128]{2,1,0:T(8,128)}, f32[8,128,128]{2,1,0:T(8,128)S(1)}, u32[]{:S(2)}, u32[]{:S(2)}) collective-permute-start(f32[8,128,128]{2,1,0:T(8,128)} %tie.4.b00), channel_id=1, source_target_pairs={{0,192},{1,193},{2,194},{3,195},{4,196},{5,197},{6,198},{7,199},{8... | collective-permute-start | bytes 1572872 | tf_op jit(solution)/shard_map/bias/ppermute | solution.py:288
  75.4 15.3 %collective-permute-start.14 = (f32[8,128,128]{2,1,0:T(8,128)}, f32[8,128,128]{2,1,0:T(8,128)S(1)}, u32[]{:S(2)}, u32[]{:S(2)}) collective-permute-start(f32[8,128,128]{2,1,0:T(8,128)} %tie.4.b00), channel_id=1, source_target_pairs={{0,128},{1,129},{2,130},{3,131},{4,132},{5,133},{6,134},{7,135},{8... | collective-permute-start | bytes 1572872 | tf_op jit(solution)/shard_map/bias/ppermute | solution.py:288
  77.5 24.7 %collective-permute-start.12 = (f32[8,128,128]{2,1,0:T(8,128)}, f32[8,128,128]{2,1,0:T(8,128)S(1)}, u32[]{:S(2)}, u32[]{:S(2)}) collective-permute-start(f32[8,128,128]{2,1,0:T(8,128)} %tie.4.b00), channel_id=1, source_target_pairs={{0,64},{1,65},{2,66},{3,67},{4,68},{5,69},{6,70},{7,71},{8,72},{9,... | collective-permute-start | bytes 1572872 | tf_op jit(solution)/shard_map/bias/ppermute | solution.py:288
  78.6 28.1 %copy-start.5 = (s32[4]{0:T(128)S(1)}, s32[4]{0:T(128)}, u32[]{:S(2)}) copy-start(s32[4]{0:T(128)} %pad_add_fusion.at) | copy-start | bytes 52
  78.6 28.7 %copy-start.27 = (bf16[128,128]{1,0:T(8,128)(2,1)S(1)}, bf16[128,128]{1,0:T(8,128)(2,1)}, u32[]{:S(2)}) copy-start(bf16[128,128]{1,0:T(8,128)(2,1)} %param.14) | copy-start | bytes 98308
  78.6 26.0 %collective-permute-start.4 = (bf16[8,4,64,128]{3,2,1,0:T(8,128)(2,1)S(1)}, bf16[8,4,64,128]{3,2,1,0:T(8,128)(2,1)S(1)}, u32[]{:S(2)}, u32[]{:S(2)}) collective-permute-start(bf16[8,4,64,128]{3,2,1,0:T(8,128)(2,1)S(1)} %slice.32), channel_id=1, source_target_pairs={{0,4},{1,5},{2,6},{3,7},{4,8},{5,9},{6,10},{7,11},{8,12},{9,13},{1... | collective-permute-start | bytes 1572872 | tf_op jit(solution)/shard_map/rows/ppermute | solution.py:288
  78.9 30.8 %collective-permute-start.11 = (f32[8,128,128]{2,1,0:T(8,128)S(1)}, f32[8,128,128]{2,1,0:T(8,128)S(1)}, u32[]{:S(2)}, u32[]{:S(2)}) collective-permute-start(f32[8,128,128]{2,1,0:T(8,128)S(1)} %copy-done.2), channel_id=1, source_target_pairs={{0,16},{1,17},{2,18},{3,19},{4,20},{5,21},{6,22},{7,23},{8,24},{9,... | collective-permute-start | bytes 1572872 | tf_op jit(solution)/shard_map/bias/ppermute | solution.py:288
  86.7 23.0 %collective-permute-start.17 = (f32[8,128,128]{2,1,0:T(8,128)S(1)}, f32[8,128,128]{2,1,0:T(8,128)S(1)}, u32[]{:S(2)}, u32[]{:S(2)}) collective-permute-start(f32[8,128,128]{2,1,0:T(8,128)S(1)} %collective-permute-done.16.b30), channel_id=1, source_target_pairs={{0,16},{1,17},{2,18},{3,19},{4,20},{5,21},{6,22},{7,23},{8,24},{9,... | collective-permute-start | bytes 1572872 | tf_op jit(solution)/shard_map/bias/ppermute | solution.py:288
  90.7 19.0 %collective-permute-start.15 = (f32[8,128,128]{2,1,0:T(8,128)S(1)}, f32[8,128,128]{2,1,0:T(8,128)}, u32[]{:S(2)}, u32[]{:S(2)}) collective-permute-start(f32[8,128,128]{2,1,0:T(8,128)S(1)} %collective-permute-done.14.b20), channel_id=1, source_target_pairs={{0,16},{1,17},{2,18},{3,19},{4,20},{5,21},{6,22},{7,23},{8,24},{9,... | collective-permute-start | bytes 1572872 | tf_op jit(solution)/shard_map/bias/ppermute | solution.py:288
  102.2 7.5 %collective-permute-start.13 = (f32[8,128,128]{2,1,0:T(8,128)S(1)}, f32[8,128,128]{2,1,0:T(8,128)}, u32[]{:S(2)}, u32[]{:S(2)}) collective-permute-start(f32[8,128,128]{2,1,0:T(8,128)S(1)} %collective-permute-done.12.b10), channel_id=1, source_target_pairs={{0,16},{1,17},{2,18},{3,19},{4,20},{5,21},{6,22},{7,23},{8,24},{9,... | collective-permute-start | bytes 1572872 | tf_op jit(solution)/shard_map/bias/ppermute | solution.py:288
  104.6 0.8 copy-start.7
  105.4 43.8 %collective-permute-start.21 = (bf16[8,4,64,128]{3,2,1,0:T(8,128)(2,1)}, bf16[8,4,64,128]{3,2,1,0:T(8,128)(2,1)}, u32[]{:S(2)}, u32[]{:S(2)}) collective-permute-start(bf16[8,4,64,128]{3,2,1,0:T(8,128)(2,1)} %slice.38), channel_id=1, source_target_pairs={{0,12},{1,13},{2,14},{3,15},{4,0},{5,1},{6,2},{7,3},{8,4},{9,5},{1... | collective-permute-start | bytes 1572872 | tf_op jit(solution)/shard_map/rows/ppermute | solution.py:288
  109.6 0.8 copy-start.16
  110.4 1.0 copy-start.8
  148.5 36.7 %copy-start.3 = (bf16[8,64,128]{2,1,0:T(8,128)(2,1)}, bf16[8,64,128]{2,1,0:T(8,128)(2,1)S(1)}, u32[]{:S(2)}) copy-start(bf16[8,64,128]{2,1,0:T(8,128)(2,1)S(1)} %get-tuple-element.23.refs_0_) | copy-start | bytes 393220
  149.8 37.5 %copy-start.14 = (bf16[8,64,128]{2,1,0:T(8,128)(2,1)S(1)}, bf16[8,64,128]{2,1,0:T(8,128)(2,1)}, u32[]{:S(2)}) copy-start(bf16[8,64,128]{2,1,0:T(8,128)(2,1)} %copy-done.13) | copy-start | bytes 393220
  149.8 39.6 %copy-start.12 = (bf16[8,64,128]{2,1,0:T(8,128)(2,1)S(1)}, bf16[8,64,128]{2,1,0:T(8,128)(2,1)}, u32[]{:S(2)}) copy-start(bf16[8,64,128]{2,1,0:T(8,128)(2,1)} %copy-done.11) | copy-start | bytes 393220
  149.8 41.4 %copy-start.10 = (bf16[8,64,128]{2,1,0:T(8,128)(2,1)S(1)}, bf16[8,64,128]{2,1,0:T(8,128)(2,1)}, u32[]{:S(2)}) copy-start(bf16[8,64,128]{2,1,0:T(8,128)(2,1)} %copy-done.9) | copy-start | bytes 393220
  185.9 5.4 %collective-permute-start.22 = (bf16[8,64,128]{2,1,0:T(8,128)(2,1)S(1)}, bf16[8,64,128]{2,1,0:T(8,128)(2,1)S(1)}, u32[]{:S(2)}, u32[]{:S(2)}) collective-permute-start(bf16[8,64,128]{2,1,0:T(8,128)(2,1)S(1)} %get-tuple-element.28), channel_id=1, source_target_pairs={{0,3},{1,0},{2,1},{3,2},{4,7},{5,4},{6,5},{7,6},{8,11},{9,8},{10,9... | collective-permute-start | bytes 393224 | tf_op jit(solution)/shard_map/update/ppermute | solution.py:288
  185.9 12.1 %collective-permute-start.23 = (bf16[8,64,128]{2,1,0:T(8,128)(2,1)S(1)}, bf16[8,64,128]{2,1,0:T(8,128)(2,1)S(1)}, u32[]{:S(2)}, u32[]{:S(2)}) collective-permute-start(bf16[8,64,128]{2,1,0:T(8,128)(2,1)S(1)} %get-tuple-element.29), channel_id=1, source_target_pairs={{0,2},{1,3},{2,0},{3,1},{4,6},{5,7},{6,4},{7,5},{8,10},{9,11},{10,... | collective-permute-start | bytes 393224 | tf_op jit(solution)/shard_map/update/ppermute | solution.py:288
  186.1 11.8 %collective-permute-start.24 = (bf16[8,64,128]{2,1,0:T(8,128)(2,1)S(1)}, bf16[8,64,128]{2,1,0:T(8,128)(2,1)S(1)}, u32[]{:S(2)}, u32[]{:S(2)}) collective-permute-start(bf16[8,64,128]{2,1,0:T(8,128)(2,1)S(1)} %get-tuple-element.30), channel_id=1, source_target_pairs={{0,1},{1,2},{2,3},{3,0},{4,5},{5,6},{6,7},{7,4},{8,9},{9,10},{10,1... | collective-permute-start | bytes 393224 | tf_op jit(solution)/shard_map/update/ppermute | solution.py:288
  187.3 11.3 %collective-permute-start.18 = (bf16[8,64,128]{2,1,0:T(8,128)(2,1)S(1)}, bf16[8,64,128]{2,1,0:T(8,128)(2,1)S(1)}, u32[]{:S(2)}, u32[]{:S(2)}) collective-permute-start(bf16[8,64,128]{2,1,0:T(8,128)(2,1)S(1)} %copy-done.14), channel_id=1, source_target_pairs={{0,3},{1,0},{2,1},{3,2},{4,7},{5,4},{6,5},{7,6},{8,11},{9,8},{10,9... | collective-permute-start | bytes 393224 | tf_op jit(solution)/shard_map/update/ppermute | solution.py:288
  189.4 19.8 %collective-permute-start.19 = (bf16[8,64,128]{2,1,0:T(8,128)(2,1)S(1)}, bf16[8,64,128]{2,1,0:T(8,128)(2,1)S(1)}, u32[]{:S(2)}, u32[]{:S(2)}) collective-permute-start(bf16[8,64,128]{2,1,0:T(8,128)(2,1)S(1)} %copy-done.12), channel_id=1, source_target_pairs={{0,2},{1,3},{2,0},{3,1},{4,6},{5,7},{6,4},{7,5},{8,10},{9,11},{10,... | collective-permute-start | bytes 393224 | tf_op jit(solution)/shard_map/update/ppermute | solution.py:288
  191.3 17.9 %copy-start.21 = (bf16[8,64,128]{2,1,0:T(8,128)(2,1)}, bf16[8,64,128]{2,1,0:T(8,128)(2,1)S(1)}, u32[]{:S(2)}) copy-start(bf16[8,64,128]{2,1,0:T(8,128)(2,1)S(1)} %collective-permute-done.22.refs_5_) | copy-start | bytes 393220
  191.3 17.9 %collective-permute-start.20 = (bf16[8,64,128]{2,1,0:T(8,128)(2,1)S(1)}, bf16[8,64,128]{2,1,0:T(8,128)(2,1)S(1)}, u32[]{:S(2)}, u32[]{:S(2)}) collective-permute-start(bf16[8,64,128]{2,1,0:T(8,128)(2,1)S(1)} %copy-done.10), channel_id=1, source_target_pairs={{0,1},{1,2},{2,3},{3,0},{4,5},{5,6},{6,7},{7,4},{8,9},{9,10},{10,1... | collective-permute-start | bytes 393224 | tf_op jit(solution)/shard_map/update/ppermute | solution.py:288
  197.9 11.3 %copy-start.22 = (bf16[8,64,128]{2,1,0:T(8,128)(2,1)}, bf16[8,64,128]{2,1,0:T(8,128)(2,1)S(1)}, u32[]{:S(2)}) copy-start(bf16[8,64,128]{2,1,0:T(8,128)(2,1)S(1)} %collective-permute-done.23.refs_6_) | copy-start | bytes 393220
  197.9 11.3 %copy-start.23 = (bf16[8,64,128]{2,1,0:T(8,128)(2,1)}, bf16[8,64,128]{2,1,0:T(8,128)(2,1)S(1)}, u32[]{:S(2)}) copy-start(bf16[8,64,128]{2,1,0:T(8,128)(2,1)S(1)} %collective-permute-done.24.refs_7_) | copy-start | bytes 393220
  198.6 10.6 %copy-start.24 = (bf16[8,64,128]{2,1,0:T(8,128)(2,1)}, bf16[8,64,128]{2,1,0:T(8,128)(2,1)S(1)}, u32[]{:S(2)}) copy-start(bf16[8,64,128]{2,1,0:T(8,128)(2,1)S(1)} %collective-permute-done.18.refs_1_) | copy-start | bytes 393220
  (12 other events, 8.2 us)

commit v2 on v0

--- a/solution.py
+++ b/solution.py
@@ -162,10 +162,8 @@
     count = 16 // CHUNKS
     whole = lambda a: pl.BlockSpec(a.shape, lambda i, at: (0,) * a.ndim)
     block = (4, TOGETHER, 64, 128)
-    specs = [
-        pl.BlockSpec(block, lambda i, at, start=start // TOGETHER: (0, i + start, 0, 0))
-        for start in first
-    ]
+    start = first // TOGETHER
+    specs = [pl.BlockSpec(block, lambda i, at: (0, i + start, 0, 0))] * 4
     biases = [b for pair in biases for b in pair]
     return pl.pallas_call(
         attend_kernel,
@@ -291,10 +289,7 @@
         here = jnp.stack(pieces)
         left = move(here, lambda y, z, core, x: (y, z, core, x + 1))
         right = move(here, lambda y, z, core, x: (y, z, core, x - 1))
-        across = (
-            move(left[:, :count], lambda y, z, core, x: (y, z, core, x + 1)),
-            move(right[:, count:], lambda y, z, core, x: (y, z, core, x - 1)),
-        )
+        across = move(here, lambda y, z, core, x: (y, z, core, x + 2))
     with jax.named_scope("bias"):
         tile = jnp.einsum(
             "jkc,ch->hkj", normed.astype(F32), w_bias, precision=lax.Precision.HIGHEST
@@ -332,8 +327,8 @@
         with jax.named_scope("attention"):
             part = attend(
                 place,
-                (here, left, across[chunk], right),
-                (chunk * count, chunk * count, 0, chunk * count),
+                (here, left, across, right),
+                chunk * count,
                 biases,
                 w_key,
                 w_value.T,

time: 196 us -> 198 us (1.010)
    slice x2 -> x0, local copies, waits for them, and re-layouts: 3.75 us -> none  [the longest x1 1.88 us: on_device(): left[:, :count]]
    unnamed x59 -> x63, local copies, waits for them, and re-layouts: 3.95 us -> 5.77 us
    ppermute x25 -> x24, waiting for transfers between devices: 27.2 us -> 28.8 us  [move(): return lax.ppermute(array, AXES, pairs)]
    ppermute x25 -> x24, starting transfers between devices: 51.2 us -> 52.5 us  [move(): return lax.ppermute(array, AXES, pairs)]
  transfers between devices with their start and end apart: 25 -> 24, of which waited for: 8 -> 9; matrix products, arithmetic and copies ran while one was open for 4% -> 2% of each run, Pallas kernels for 36% -> 18%
where the time goes in v2:
time: 198 us; the launch traced here: 196 us
  Pallas kernels  72.4 us (37%)
  starting transfers between devices  52.5 us (27%)
  waiting for transfers between devices  28.8 us (15%)
  blocking collectives  23 us (12%)
  local copies, waits for them, and re-layouts  10.6 us (5%)
  other arithmetic  5.82 us (3%)
  matrix products  2.53 us (1%)
    pallas_call x2, Pallas kernels, attend(): pl.pallas_call(attend_kernel, out_shape=jax.ShapeDtypeStruct((4, count, 6...  70.1 us
    ppermute x24, starting transfers between devices, move(): return lax.ppermute(array, AXES, pairs)  52.5 us
    ppermute x24, waiting for transfers between devices, move(): return lax.ppermute(array, AXES, pairs)  28.8 us
    all_to_all x1, blocking collectives, on_device(): lax.all_to_all(jnp.broadcast_to(block[None], (8, 128, 128)), ('zh', 'zl')...  23 us
    unnamed x63, local copies, waits for them, and re-layouts  5.77 us
  transfers between devices with their start and end apart: 24, of which 9 were waited for; matrix products, arithmetic and copies ran while one was open for 2% of the time, Pallas kernels for 18%

profile of v2, /device:TPU:1, one launch (start us, length us, event | category | flops | bytes accessed | tf_op | source)
XLA Modules:
  0.0 196.2 jit_solution(9716149220550186780)
XLA Ops:
  0.0 1.9 convert_reduce_fusion
  2.0 1.3 fusion.2
  3.3 1.3 fusion.5
  4.6 2.5 %fusion.6 = f32[64,64,4]{1,2,0:T(4,128)S(1)} fusion(bf16[64,64,128]{2,1,0:T(8,128)(2,1)S(1)} %fusion.5, f32[128,4]{0,1:T(4,128)S(1)} %copy-done), kind=kOutput, calls=%fused_computation.38 | convolution fusion | flops 25165824 | bytes 1116160 | tf_op jit(solution)/shard_map/bias/jkc,ch->hkj/dot_general | solution.py:294
  7.4 3.3 %collective-permute-start.6 = (f32[4,32,64]{1,0,2:T(4,128)S(1)}, f32[4,32,64]{1,0,2:T(4,128)S(1)}, u32[]{:S(2)}, u32[]{:S(2)}) collective-permute-start(f32[4,32,64]{1,0,2:T(4,128)S(1)} %get-tuple-element.18), channel_id=1, source_target_pairs={{0,16},{1,17},{2,18},{3,19},{4,20},{5,21},{6,22},{7,23},{8,24},{9,... | collective-permute-start | bytes 98312 | tf_op jit(solution)/shard_map/bias/ppermute | solution.py:253
  10.8 0.9 collective-permute-done.6
  11.9 0.7 collective-permute-start.7
  12.7 2.7 %collective-permute-start.2 = (bf16[16,64,128]{2,1,0:T(8,128)(2,1)S(1)}, bf16[16,64,128]{2,1,0:T(8,128)(2,1)S(1)}, u32[]{:S(2)}, u32[]{:S(2)}) collective-permute-start(bf16[16,64,128]{2,1,0:T(8,128)(2,1)S(1)} %get-tuple-element.6), channel_id=1, source_target_pairs={{0,3},{1,0},{2,1},{3,2},{4,7},{5,4},{6,5},{7,6},{8,11},{9,8},{10,9... | collective-permute-start | bytes 786440 | tf_op jit(solution)/shard_map/rows/ppermute | solution.py:253
  15.4 0.4 collective-permute-start
  15.7 6.1 %collective-permute-start.10 = (f32[32,128]{1,0:T(8,128)S(1)}, f32[32,128]{1,0:T(8,128)S(1)}, u32[]{:S(2)}, u32[]{:S(2)}) collective-permute-start(f32[32,128]{1,0:T(8,128)S(1)} %get-tuple-element.19), channel_id=1, source_target_pairs={{0,192},{1,193},{2,194},{3,195},{4,0},{5,1},{6,2},{7,3},{8,64},{9,... | collective-permute-start | bytes 49160 | tf_op jit(solution)/shard_map/bias/ppermute | solution.py:253
  21.9 1.9 collective-permute-start.8
  23.8 2.5 %collective-permute-done.8 = f32[32,128]{1,0:T(8,128)S(1)} collective-permute-done((f32[32,128]{1,0:T(8,128)S(1)}, f32[32,128]{1,0:T(8,128)S(1)}, u32[]{:S(2)}, u32[]{:S(2)}) %collective-permute-start.8) | collective-permute-done | bytes 16416 | tf_op jit(solution)/shard_map/bias/ppermute | solution.py:253
  26.2 3.2 %collective-permute-start.9 = (f32[32,128]{1,0:T(8,128)S(1)}, f32[32,128]{1,0:T(8,128)S(1)}, u32[]{:S(2)}, u32[]{:S(2)}) collective-permute-start(f32[32,128]{1,0:T(8,128)S(1)} %get-tuple-element.20), channel_id=1, source_target_pairs={{0,128},{1,129},{2,130},{3,131},{4,192},{5,193},{6,194},{7,195},{8... | collective-permute-start | bytes 49160 | tf_op jit(solution)/shard_map/bias/ppermute | solution.py:253
  29.5 1.0 collective-permute-done.9
  30.5 6.6 %collective-permute-done.1 = bf16[16,64,128]{2,1,0:T(8,128)(2,1)S(1)} collective-permute-done((bf16[16,64,128]{2,1,0:T(8,128)(2,1)S(1)}, bf16[16,64,128]{2,1,0:T(8,128)(2,1)S(1)}, u32[]{:S(2)}, u32[]{:S(2)}) %collective-permute-start.1) | collective-permute-done | bytes 262176 | tf_op jit(solution)/shard_map/rows/ppermute | solution.py:253
  37.1 1.1 pad_maximum_fusion.rest_0_.x0
  38.2 6.1 %collective-permute-start.5 = (bf16[4,16,64,128]{3,2,1,0:T(8,128)(2,1)}, bf16[4,16,64,128]{3,2,1,0:T(8,128)(2,1)S(1)}, u32[]{:S(2)}, u32[]{:S(2)}) collective-permute-start(bf16[4,16,64,128]{3,2,1,0:T(8,128)(2,1)} %pad_maximum_fusion.rest_0_.x0), channel_id=1, source_target_pairs={{0,12},{1,13},{2,14},{3,15},{4,0},{5,1},{6,2},{7,3},{8,4},{9,5},{1... | collective-permute-start | bytes 3145736 | tf_op jit(solution)/shard_map/rows/ppermute | solution.py:253
  44.3 0.6 constant_dynamic-slice_fusion
  44.9 0.9 broadcast_in_dim.6
  45.8 23.0 %all_to_all.5.array = f32[8,128,128]{2,1,0:T(8,128)} all-to-all(f32[8,128,128]{2,1,0:T(8,128)S(1)} %broadcast_in_dim.6), channel_id=1, replica_groups=mesh['y'=4,'zh'=2,'core'=2,'x'=4,'zl'=4] {'zh','zl'}, dimensions={0} | all-to-all | bytes 1048576 | tf_op jit(solution)/shard_map/bias/all_to_all | solution.py:310
  68.9 1.0 copy-done.15
  69.9 1.0 copy-done.16
  70.9 1.1 collective-permute-start.16
  72.0 1.9 collective-permute-start.4
  73.9 1.5 collective-permute-start.14
  75.4 3.8 %collective-permute-start.11 = (f32[8,128,128]{2,1,0:T(8,128)}, f32[8,128,128]{2,1,0:T(8,128)S(1)}, u32[]{:S(2)}, u32[]{:S(2)}) collective-permute-start(f32[8,128,128]{2,1,0:T(8,128)} %tie.5.b00), channel_id=1, source_target_pairs={{0,16},{1,17},{2,18},{3,19},{4,20},{5,21},{6,22},{7,23},{8,24},{9,... | collective-permute-start | bytes 1572872 | tf_op jit(solution)/shard_map/bias/ppermute | solution.py:253
  79.2 2.6 %collective-permute-done.16.b30 = f32[8,128,128]{2,1,0:T(8,128)S(1)} collective-permute-done((f32[8,128,128]{2,1,0:T(8,128)}, f32[8,128,128]{2,1,0:T(8,128)S(1)}, u32[]{:S(2)}, u32[]{:S(2)}) %collective-permute-start.16) | collective-permute-done | bytes 524320 | tf_op jit(solution)/shard_map/bias/ppermute | solution.py:253
  81.8 7.2 %collective-permute-start.17 = (f32[8,128,128]{2,1,0:T(8,128)S(1)}, f32[8,128,128]{2,1,0:T(8,128)S(1)}, u32[]{:S(2)}, u32[]{:S(2)}) collective-permute-start(f32[8,128,128]{2,1,0:T(8,128)S(1)} %collective-permute-done.16.b30), channel_id=1, source_target_pairs={{0,16},{1,17},{2,18},{3,19},{4,20},{5,21},{6,22},{7,23},{8,24},{9,... | collective-permute-start | bytes 1572872 | tf_op jit(solution)/shard_map/bias/ppermute | solution.py:253
  88.9 5.2 %collective-permute-start.15 = (f32[8,128,128]{2,1,0:T(8,128)S(1)}, f32[8,128,128]{2,1,0:T(8,128)S(1)}, u32[]{:S(2)}, u32[]{:S(2)}) collective-permute-start(f32[8,128,128]{2,1,0:T(8,128)S(1)} %collective-permute-done.14.b20), channel_id=1, source_target_pairs={{0,16},{1,17},{2,18},{3,19},{4,20},{5,21},{6,22},{7,23},{8,24},{9,... | collective-permute-start | bytes 1572872 | tf_op jit(solution)/shard_map/bias/ppermute | solution.py:253
  94.1 6.6 %collective-permute-done.12.b10 = f32[8,128,128]{2,1,0:T(8,128)S(1)} collective-permute-done((f32[8,128,128]{2,1,0:T(8,128)}, f32[8,128,128]{2,1,0:T(8,128)S(1)}, u32[]{:S(2)}, u32[]{:S(2)}) %collective-permute-start.12) | collective-permute-done | bytes 524320 | tf_op jit(solution)/shard_map/bias/ppermute | solution.py:253
  100.7 0.5 collective-permute-start.13
  101.8 1.0 collective-permute-done.13.b11
  102.9 1.0 copy-done.3
  103.9 35.1 %attention.2.rest_0_ = bf16[4,8,64,128]{3,2,1,0:T(8,128)(2,1)S(1)} custom-call(s32[4]{0:T(128)S(1)} %pad_add_fusion.at.array, bf16[4,16,64,128]{3,2,1,0:T(8,128)(2,1)} %pad_maximum_fusion.rest_0_.x0, bf16[4,16,64,128]{3,2,1,0:T(8,128)(2,1)} %copy-done.16, bf16[4,16,64,128]{3,2,1,0:T(8,128)(2,1)} %collective-permute-done.4.x2, ...), custom_call_target="tpu_custom_call" | custom-call | flops 2400000000 | bytes 8388608 | tf_op jit(solution)/shard_map/attention/attention/pallas_call | solution.py:168
  139.0 0.8 copy-done.2
  139.8 0.8 copy-done.9
  140.7 2.0 %slice_bitcast_fusion.4 = (bf16[8,64,128]{2,1,0:T(8,128)(2,1)S(1)}, bf16[8,64,128]{2,1,0:T(8,128)(2,1)}, bf16[8,64,128]{2,1,0:T(8,128)(2,1)}, bf16[8,64,128]{2,1,0:T(8,128)(2,1)}) fusion(bf16[4,8,64,128]{3,2,1,0:T(8,128)(2,1)} %copy-done.2), kind=kLoop, calls=%fused_computation.14 | loop fusion | bytes 1048576 | tf_op jit(solution)/shard_map/update/squeeze | solution.py:344
  142.9 1.1 collective-permute-start.19
  144.0 1.9 collective-permute-start.18
  145.9 35.0 %attention.3.rest_0_ = bf16[4,8,64,128]{3,2,1,0:T(8,128)(2,1)S(1)} custom-call(s32[4]{0:T(128)S(1)} %copy-done.6, bf16[4,16,64,128]{3,2,1,0:T(8,128)(2,1)} %pad_maximum_fusion.rest_0_.x0, bf16[4,16,64,128]{3,2,1,0:T(8,128)(2,1)} %copy-done.16, bf16[4,16,64,128]{3,2,1,0:T(8,128)(2,1)} %collective-permute-done.4.x2, bf16[4,16,64,128]{3,2,1,0:T(8,128)(2,1)} %copy-done.15, ...), custom_call_target="tpu_custom_call" | custom-call | flops 2400000000 | bytes 8388608 | tf_op jit(solution)/shard_map/attention/attention/pallas_call | solution.py:168
  181.0 0.8 slice_bitcast_fusion
  181.8 0.3 collective-permute-start.23
  182.1 1.2 collective-permute-start.22
  183.2 2.4 %collective-permute-start.21 = (bf16[8,64,128]{2,1,0:T(8,128)(2,1)S(1)}, bf16[8,64,128]{2,1,0:T(8,128)(2,1)S(1)}, u32[]{:S(2)}, u32[]{:S(2)}) collective-permute-start(bf16[8,64,128]{2,1,0:T(8,128)(2,1)S(1)} %get-tuple-element.11), channel_id=1, source_target_pairs={{0,3},{1,0},{2,1},{3,2},{4,7},{5,4},{6,5},{7,6},{8,11},{9,8},{10,9... | collective-permute-start | bytes 393224 | tf_op jit(solution)/shard_map/update/ppermute | solution.py:253
  185.6 2.0 %collective-permute-done.23.refs_7_ = bf16[8,64,128]{2,1,0:T(8,128)(2,1)S(1)} collective-permute-done((bf16[8,64,128]{2,1,0:T(8,128)(2,1)S(1)}, bf16[8,64,128]{2,1,0:T(8,128)(2,1)S(1)}, u32[]{:S(2)}, u32[]{:S(2)}) %collective-permute-start.23) | collective-permute-done | bytes 131104 | tf_op jit(solution)/shard_map/update/ppermute | solution.py:253
  187.6 5.6 %collective-permute-done.22.refs_6_ = bf16[8,64,128]{2,1,0:T(8,128)(2,1)S(1)} collective-permute-done((bf16[8,64,128]{2,1,0:T(8,128)(2,1)S(1)}, bf16[8,64,128]{2,1,0:T(8,128)(2,1)S(1)}, u32[]{:S(2)}, u32[]{:S(2)}) %collective-permute-start.22) | collective-permute-done | bytes 131104 | tf_op jit(solution)/shard_map/update/ppermute | solution.py:253
  193.2 0.6 copy-done.19
  193.9 2.3 %assemble_update.1 = bf16[64,64,128]{2,1,0:T(8,128)(2,1)} custom-call(s32[4]{0:T(128)} %tie.7.at, bf16[8,64,128]{2,1,0:T(8,128)(2,1)} %get-tuple-element.16.refs_0_, bf16[8,64,128]{2,1,0:T(8,128)(2,1)} %collective-permute-done.18.refs_1_, bf16[8,64,128]{2,1,0:T(8,128)(2,1)} %collective-permute-done.19.refs_2_, bf16[8,64,128]{2,1,0:T(8,128)(2,1)} %copy-done.17, ...), custom_call_target="tpu_custom_call" | custom-call | tf_op jit(solution)/shard_map/assemble_update/pallas_call | solution.py:215
  (91 shorter events, 1.6 us)
Async XLA Ops:
  0.0 4.6 %copy-start = (f32[128,4]{0,1:T(4,128)S(1)}, f32[128,4]{0,1:T(4,128)}, u32[]{:S(2)}) copy-start(f32[128,4]{0,1:T(4,128)} %param.19) | copy-start | bytes 6148
  0.0 2.0 copy-start.14
  0.0 3.3 %copy-start.25 = (f32[128]{0:T(128)S(1)}, f32[128]{0:T(128)}, u32[]{:S(2)}) copy-start(f32[128]{0:T(128)} %param.13) | copy-start | bytes 1540
  0.0 3.3 %copy-start.26 = (f32[128]{0:T(128)S(1)}, f32[128]{0:T(128)}, u32[]{:S(2)}) copy-start(f32[128]{0:T(128)} %param.12) | copy-start | bytes 1540
  7.4 4.3 %collective-permute-start.6 = (f32[4,32,64]{1,0,2:T(4,128)S(1)}, f32[4,32,64]{1,0,2:T(4,128)S(1)}, u32[]{:S(2)}, u32[]{:S(2)}) collective-permute-start(f32[4,32,64]{1,0,2:T(4,128)S(1)} %get-tuple-element.18), channel_id=1, source_target_pairs={{0,16},{1,17},{2,18},{3,19},{4,20},{5,21},{6,22},{7,23},{8,24},{9,... | collective-permute-start | bytes 98312 | tf_op jit(solution)/shard_map/bias/ppermute | solution.py:253
  11.9 10.0 %collective-permute-start.7 = (f32[32,128]{1,0:T(8,128)S(1)}, f32[32,128]{1,0:T(8,128)S(1)}, u32[]{:S(2)}, u32[]{:S(2)}) collective-permute-start(f32[32,128]{1,0:T(8,128)S(1)} %get-tuple-element.22), channel_id=1, source_target_pairs={{0,0},{1,1},{2,2},{3,3},{4,64},{5,65},{6,66},{7,67},{8,128},{9,129... | collective-permute-start | bytes 49160 | tf_op jit(solution)/shard_map/bias/ppermute | solution.py:253
  12.7 17.9 %collective-permute-start.2 = (bf16[16,64,128]{2,1,0:T(8,128)(2,1)S(1)}, bf16[16,64,128]{2,1,0:T(8,128)(2,1)S(1)}, u32[]{:S(2)}, u32[]{:S(2)}) collective-permute-start(bf16[16,64,128]{2,1,0:T(8,128)(2,1)S(1)} %get-tuple-element.6), channel_id=1, source_target_pairs={{0,3},{1,0},{2,1},{3,2},{4,7},{5,4},{6,5},{7,6},{8,11},{9,8},{10,9... | collective-permute-start | bytes 786440 | tf_op jit(solution)/shard_map/rows/ppermute | solution.py:253
  15.4 21.8 %collective-permute-start.1 = (bf16[16,64,128]{2,1,0:T(8,128)(2,1)S(1)}, bf16[16,64,128]{2,1,0:T(8,128)(2,1)S(1)}, u32[]{:S(2)}, u32[]{:S(2)}) collective-permute-start(bf16[16,64,128]{2,1,0:T(8,128)(2,1)S(1)} %get-tuple-element.7), channel_id=1, source_target_pairs={{0,2},{1,3},{2,0},{3,1},{4,6},{5,7},{6,4},{7,5},{8,10},{9,11},{10,... | collective-permute-start | bytes 786440 | tf_op jit(solution)/shard_map/rows/ppermute | solution.py:253
  15.4 21.8 %collective-permute-start = (bf16[16,64,128]{2,1,0:T(8,128)(2,1)S(1)}, bf16[16,64,128]{2,1,0:T(8,128)(2,1)S(1)}, u32[]{:S(2)}, u32[]{:S(2)}) collective-permute-start(bf16[16,64,128]{2,1,0:T(8,128)(2,1)S(1)} %get-tuple-element.8), channel_id=1, source_target_pairs={{0,1},{1,2},{2,3},{3,0},{4,5},{5,6},{6,7},{7,4},{8,9},{9,10},{10,1... | collective-permute-start | bytes 786440 | tf_op jit(solution)/shard_map/rows/ppermute | solution.py:253
  15.7 14.7 %collective-permute-start.10 = (f32[32,128]{1,0:T(8,128)S(1)}, f32[32,128]{1,0:T(8,128)S(1)}, u32[]{:S(2)}, u32[]{:S(2)}) collective-permute-start(f32[32,128]{1,0:T(8,128)S(1)} %get-tuple-element.19), channel_id=1, source_target_pairs={{0,192},{1,193},{2,194},{3,195},{4,0},{5,1},{6,2},{7,3},{8,64},{9,... | collective-permute-start | bytes 49160 | tf_op jit(solution)/shard_map/bias/ppermute | solution.py:253
  21.9 4.4 %collective-permute-start.8 = (f32[32,128]{1,0:T(8,128)S(1)}, f32[32,128]{1,0:T(8,128)S(1)}, u32[]{:S(2)}, u32[]{:S(2)}) collective-permute-start(f32[32,128]{1,0:T(8,128)S(1)} %get-tuple-element.21), channel_id=1, source_target_pairs={{0,64},{1,65},{2,66},{3,67},{4,128},{5,129},{6,130},{7,131},{8,192... | collective-permute-start | bytes 49160 | tf_op jit(solution)/shard_map/bias/ppermute | solution.py:253
  26.2 4.2 %collective-permute-start.9 = (f32[32,128]{1,0:T(8,128)S(1)}, f32[32,128]{1,0:T(8,128)S(1)}, u32[]{:S(2)}, u32[]{:S(2)}) collective-permute-start(f32[32,128]{1,0:T(8,128)S(1)} %get-tuple-element.20), channel_id=1, source_target_pairs={{0,128},{1,129},{2,130},{3,131},{4,192},{5,193},{6,194},{7,195},{8... | collective-permute-start | bytes 49160 | tf_op jit(solution)/shard_map/bias/ppermute | solution.py:253
  38.2 30.7 %collective-permute-start.5 = (bf16[4,16,64,128]{3,2,1,0:T(8,128)(2,1)}, bf16[4,16,64,128]{3,2,1,0:T(8,128)(2,1)S(1)}, u32[]{:S(2)}, u32[]{:S(2)}) collective-permute-start(bf16[4,16,64,128]{3,2,1,0:T(8,128)(2,1)} %pad_maximum_fusion.rest_0_.x0), channel_id=1, source_target_pairs={{0,12},{1,13},{2,14},{3,15},{4,0},{5,1},{6,2},{7,3},{8,4},{9,5},{1... | collective-permute-start | bytes 3145736 | tf_op jit(solution)/shard_map/rows/ppermute | solution.py:253
  44.3 24.6 %collective-permute-start.3 = (bf16[4,16,64,128]{3,2,1,0:T(8,128)(2,1)}, bf16[4,16,64,128]{3,2,1,0:T(8,128)(2,1)S(1)}, u32[]{:S(2)}, u32[]{:S(2)}) collective-permute-start(bf16[4,16,64,128]{3,2,1,0:T(8,128)(2,1)} %pad_maximum_fusion.rest_0_.x0), channel_id=1, source_target_pairs={{0,4},{1,5},{2,6},{3,7},{4,8},{5,9},{6,10},{7,11},{8,12},{9,13},{1... | collective-permute-start | bytes 3145736 | tf_op jit(solution)/shard_map/rows/ppermute | solution.py:253
  68.8 32.4 %copy-start.21 = (bf16[128,128]{1,0:T(8,128)(2,1)S(1)}, bf16[128,128]{1,0:T(8,128)(2,1)}, u32[]{:S(2)}) copy-start(bf16[128,128]{1,0:T(8,128)(2,1)} %param.14) | copy-start | bytes 98308
  68.8 32.5 %copy-start.22 = (bf16[128,128]{1,0:T(8,128)(2,1)S(1)}, bf16[128,128]{1,0:T(8,128)(2,1)}, u32[]{:S(2)}) copy-start(bf16[128,128]{1,0:T(8,128)(2,1)} %param.16) | copy-start | bytes 98308
  68.9 32.6 %copy-start.23 = (bf16[128,128]{1,0:T(8,128)(2,1)S(1)}, bf16[128,128]{1,0:T(8,128)(2,1)}, u32[]{:S(2)}) copy-start(bf16[128,128]{1,0:T(8,128)(2,1)} %param.17) | copy-start | bytes 98308
  68.9 32.7 %copy-start.24 = (f32[128]{0:T(128)S(1)}, f32[128]{0:T(128)}, u32[]{:S(2)}) copy-start(f32[128]{0:T(128)} %param.18) | copy-start | bytes 1540
  68.9 34.0 %copy-start.11 = (bf16[128,128]{1,0:T(8,128)(2,1)S(1)}, bf16[128,128]{1,0:T(8,128)(2,1)}, u32[]{:S(2)}) copy-start(bf16[128,128]{1,0:T(8,128)(2,1)} %w_key.3) | copy-start | bytes 98308
  68.9 34.0 %copy-start.12 = (bf16[128,128]{1,0:T(8,128)(2,1)S(1)}, bf16[128,128]{1,0:T(8,128)(2,1)}, u32[]{:S(2)}) copy-start(bf16[128,128]{1,0:T(8,128)(2,1)} %w_out.3) | copy-start | bytes 98308
  68.9 34.0 %copy-start.13 = (f32[128]{0:T(128)S(1)}, f32[128]{0:T(128)}, u32[]{:S(2)}) copy-start(f32[128]{0:T(128)} %param.21) | copy-start | bytes 1540
  68.9 1.0 copy-start.15
  69.9 1.0 copy-start.16
  70.9 10.9 %collective-permute-start.16 = (f32[8,128,128]{2,1,0:T(8,128)}, f32[8,128,128]{2,1,0:T(8,128)S(1)}, u32[]{:S(2)}, u32[]{:S(2)}) collective-permute-start(f32[8,128,128]{2,1,0:T(8,128)} %tie.5.b00), channel_id=1, source_target_pairs={{0,192},{1,193},{2,194},{3,195},{4,196},{5,197},{6,198},{7,199},{8... | collective-permute-start | bytes 1572872 | tf_op jit(solution)/shard_map/bias/ppermute | solution.py:253
  72.0 29.8 %collective-permute-start.4 = (bf16[4,16,64,128]{3,2,1,0:T(8,128)(2,1)}, bf16[4,16,64,128]{3,2,1,0:T(8,128)(2,1)}, u32[]{:S(2)}, u32[]{:S(2)}) collective-permute-start(bf16[4,16,64,128]{3,2,1,0:T(8,128)(2,1)} %pad_maximum_fusion.rest_0_.x0), channel_id=1, source_target_pairs={{0,8},{1,9},{2,10},{3,11},{4,12},{5,13},{6,14},{7,15},{8,0},{9,1},... | collective-permute-start | bytes 3145736 | tf_op jit(solution)/shard_map/rows/ppermute | solution.py:253
  73.9 15.0 %collective-permute-start.14 = (f32[8,128,128]{2,1,0:T(8,128)}, f32[8,128,128]{2,1,0:T(8,128)S(1)}, u32[]{:S(2)}, u32[]{:S(2)}) collective-permute-start(f32[8,128,128]{2,1,0:T(8,128)} %tie.5.b00), channel_id=1, source_target_pairs={{0,128},{1,129},{2,130},{3,131},{4,132},{5,133},{6,134},{7,135},{8... | collective-permute-start | bytes 1572872 | tf_op jit(solution)/shard_map/bias/ppermute | solution.py:253
  75.4 25.3 %collective-permute-start.12 = (f32[8,128,128]{2,1,0:T(8,128)}, f32[8,128,128]{2,1,0:T(8,128)S(1)}, u32[]{:S(2)}, u32[]{:S(2)}) collective-permute-start(f32[8,128,128]{2,1,0:T(8,128)} %tie.5.b00), channel_id=1, source_target_pairs={{0,64},{1,65},{2,66},{3,67},{4,68},{5,69},{6,70},{7,71},{8,72},{9,... | collective-permute-start | bytes 1572872 | tf_op jit(solution)/shard_map/bias/ppermute | solution.py:253
  75.4 26.4 %collective-permute-start.11 = (f32[8,128,128]{2,1,0:T(8,128)}, f32[8,128,128]{2,1,0:T(8,128)S(1)}, u32[]{:S(2)}, u32[]{:S(2)}) collective-permute-start(f32[8,128,128]{2,1,0:T(8,128)} %tie.5.b00), channel_id=1, source_target_pairs={{0,16},{1,17},{2,18},{3,19},{4,20},{5,21},{6,22},{7,23},{8,24},{9,... | collective-permute-start | bytes 1572872 | tf_op jit(solution)/shard_map/bias/ppermute | solution.py:253
  81.8 20.0 %collective-permute-start.17 = (f32[8,128,128]{2,1,0:T(8,128)S(1)}, f32[8,128,128]{2,1,0:T(8,128)S(1)}, u32[]{:S(2)}, u32[]{:S(2)}) collective-permute-start(f32[8,128,128]{2,1,0:T(8,128)S(1)} %collective-permute-done.16.b30), channel_id=1, source_target_pairs={{0,16},{1,17},{2,18},{3,19},{4,20},{5,21},{6,22},{7,23},{8,24},{9,... | collective-permute-start | bytes 1572872 | tf_op jit(solution)/shard_map/bias/ppermute | solution.py:253
  88.9 12.9 %collective-permute-start.15 = (f32[8,128,128]{2,1,0:T(8,128)S(1)}, f32[8,128,128]{2,1,0:T(8,128)S(1)}, u32[]{:S(2)}, u32[]{:S(2)}) collective-permute-start(f32[8,128,128]{2,1,0:T(8,128)S(1)} %collective-permute-done.14.b20), channel_id=1, source_target_pairs={{0,16},{1,17},{2,18},{3,19},{4,20},{5,21},{6,22},{7,23},{8,24},{9,... | collective-permute-start | bytes 1572872 | tf_op jit(solution)/shard_map/bias/ppermute | solution.py:253
  100.7 2.2 %collective-permute-start.13 = (f32[8,128,128]{2,1,0:T(8,128)S(1)}, f32[8,128,128]{2,1,0:T(8,128)}, u32[]{:S(2)}, u32[]{:S(2)}) collective-permute-start(f32[8,128,128]{2,1,0:T(8,128)S(1)} %collective-permute-done.12.b10), channel_id=1, source_target_pairs={{0,16},{1,17},{2,18},{3,19},{4,20},{5,21},{6,22},{7,23},{8,24},{9,... | collective-permute-start | bytes 1572872 | tf_op jit(solution)/shard_map/bias/ppermute | solution.py:253
  101.8 37.2 %copy-start.5 = (s32[4]{0:T(128)}, s32[4]{0:T(128)S(1)}, u32[]{:S(2)}) copy-start(s32[4]{0:T(128)S(1)} %pad_add_fusion.at.array) | copy-start | bytes 52
  101.8 37.2 %copy-start.7 = (f32[8,128,128]{2,1,0:T(8,128)}, f32[8,128,128]{2,1,0:T(8,128)S(1)}, u32[]{:S(2)}) copy-start(f32[8,128,128]{2,1,0:T(8,128)S(1)} %collective-permute-done.17.b31) | copy-start | bytes 1572868
  102.9 1.0 copy-start.3
  139.0 0.8 copy-start.2
  140.6 5.3 %copy-start.4 = (f32[8,128,128]{2,1,0:T(8,128)S(1)}, f32[8,128,128]{2,1,0:T(8,128)}, u32[]{:S(2)}) copy-start(f32[8,128,128]{2,1,0:T(8,128)} %tie.5.b00) | copy-start | bytes 1572868
  140.6 5.3 %copy-start.6 = (s32[4]{0:T(128)S(1)}, s32[4]{0:T(128)}, u32[]{:S(2)}) copy-start(s32[4]{0:T(128)} %tie.6.at.array) | copy-start | bytes 52
  140.6 5.3 %copy-start.8 = (f32[8,128,128]{2,1,0:T(8,128)S(1)}, f32[8,128,128]{2,1,0:T(8,128)}, u32[]{:S(2)}) copy-start(f32[8,128,128]{2,1,0:T(8,128)} %copy-done.7) | copy-start | bytes 1572868
  140.6 5.3 %copy-start.10 = (f32[8,128,128]{2,1,0:T(8,128)S(1)}, f32[8,128,128]{2,1,0:T(8,128)}, u32[]{:S(2)}) copy-start(f32[8,128,128]{2,1,0:T(8,128)} %copy-done.9) | copy-start | bytes 1572868
  142.6 40.6 %collective-permute-start.20 = (bf16[8,64,128]{2,1,0:T(8,128)(2,1)S(1)}, bf16[8,64,128]{2,1,0:T(8,128)(2,1)S(1)}, u32[]{:S(2)}, u32[]{:S(2)}) collective-permute-start(bf16[8,64,128]{2,1,0:T(8,128)(2,1)S(1)} %get-tuple-element.13), channel_id=1, source_target_pairs={{0,1},{1,2},{2,3},{3,0},{4,5},{5,6},{6,7},{7,4},{8,9},{9,10},{10,1... | collective-permute-start | bytes 393224 | tf_op jit(solution)/shard_map/update/ppermute | solution.py:253
  142.9 42.7 %collective-permute-start.19 = (bf16[8,64,128]{2,1,0:T(8,128)(2,1)}, bf16[8,64,128]{2,1,0:T(8,128)(2,1)}, u32[]{:S(2)}, u32[]{:S(2)}) collective-permute-start(bf16[8,64,128]{2,1,0:T(8,128)(2,1)} %get-tuple-element.14), channel_id=1, source_target_pairs={{0,2},{1,3},{2,0},{3,1},{4,6},{5,7},{6,4},{7,5},{8,10},{9,11},{10,... | collective-permute-start | bytes 393224 | tf_op jit(solution)/shard_map/update/ppermute | solution.py:253
  144.0 41.6 %collective-permute-start.18 = (bf16[8,64,128]{2,1,0:T(8,128)(2,1)}, bf16[8,64,128]{2,1,0:T(8,128)(2,1)}, u32[]{:S(2)}, u32[]{:S(2)}) collective-permute-start(bf16[8,64,128]{2,1,0:T(8,128)(2,1)} %get-tuple-element.15), channel_id=1, source_target_pairs={{0,3},{1,0},{2,1},{3,2},{4,7},{5,4},{6,5},{7,6},{8,11},{9,8},{10,9... | collective-permute-start | bytes 393224 | tf_op jit(solution)/shard_map/update/ppermute | solution.py:253
  181.0 4.6 %copy-start.1 = (bf16[4,8,64,128]{3,2,1,0:T(8,128)(2,1)}, bf16[4,8,64,128]{3,2,1,0:T(8,128)(2,1)S(1)}, u32[]{:S(2)}) copy-start(bf16[4,8,64,128]{3,2,1,0:T(8,128)(2,1)S(1)} %attention.3.rest_0_) | copy-start | bytes 1572868
  181.8 5.8 %collective-permute-start.23 = (bf16[8,64,128]{2,1,0:T(8,128)(2,1)S(1)}, bf16[8,64,128]{2,1,0:T(8,128)(2,1)S(1)}, u32[]{:S(2)}, u32[]{:S(2)}) collective-permute-start(bf16[8,64,128]{2,1,0:T(8,128)(2,1)S(1)} %get-tuple-element.9), channel_id=1, source_target_pairs={{0,1},{1,2},{2,3},{3,0},{4,5},{5,6},{6,7},{7,4},{8,9},{9,10},{10,1... | collective-permute-start | bytes 393224 | tf_op jit(solution)/shard_map/update/ppermute | solution.py:253
  182.1 11.1 %collective-permute-start.22 = (bf16[8,64,128]{2,1,0:T(8,128)(2,1)S(1)}, bf16[8,64,128]{2,1,0:T(8,128)(2,1)S(1)}, u32[]{:S(2)}, u32[]{:S(2)}) collective-permute-start(bf16[8,64,128]{2,1,0:T(8,128)(2,1)S(1)} %get-tuple-element.10), channel_id=1, source_target_pairs={{0,2},{1,3},{2,0},{3,1},{4,6},{5,7},{6,4},{7,5},{8,10},{9,11},{10,... | collective-permute-start | bytes 393224 | tf_op jit(solution)/shard_map/update/ppermute | solution.py:253
  183.2 10.0 %copy-start.17 = (bf16[8,64,128]{2,1,0:T(8,128)(2,1)}, bf16[8,64,128]{2,1,0:T(8,128)(2,1)S(1)}, u32[]{:S(2)}) copy-start(bf16[8,64,128]{2,1,0:T(8,128)(2,1)S(1)} %collective-permute-done.20.refs_3_) | copy-start | bytes 393220
  183.2 9.9 %collective-permute-start.21 = (bf16[8,64,128]{2,1,0:T(8,128)(2,1)S(1)}, bf16[8,64,128]{2,1,0:T(8,128)(2,1)S(1)}, u32[]{:S(2)}, u32[]{:S(2)}) collective-permute-start(bf16[8,64,128]{2,1,0:T(8,128)(2,1)S(1)} %get-tuple-element.11), channel_id=1, source_target_pairs={{0,3},{1,0},{2,1},{3,2},{4,7},{5,4},{6,5},{7,6},{8,11},{9,8},{10,9... | collective-permute-start | bytes 393224 | tf_op jit(solution)/shard_map/update/ppermute | solution.py:253
  187.6 5.6 %copy-start.18 = (bf16[8,64,128]{2,1,0:T(8,128)(2,1)}, bf16[8,64,128]{2,1,0:T(8,128)(2,1)S(1)}, u32[]{:S(2)}) copy-start(bf16[8,64,128]{2,1,0:T(8,128)(2,1)S(1)} %collective-permute-done.23.refs_7_) | copy-start | bytes 393220
  (3 other events, 2.2 us)

commit v3 on v0

--- a/solution.py
+++ b/solution.py
@@ -281,13 +281,37 @@
     normed = normalize(pair, norm_gain, norm_shift)
     count = 16 // CHUNKS
 
-    with jax.named_scope("rows"):
+    with jax.named_scope("bias"):
+        tile = jnp.einsum(
+            "jkc,ch->hkj", normed.astype(F32), w_bias, precision=lax.Precision.HIGHEST
+        )
+        kept = lax.dynamic_slice_in_dim(tile, core * 32, 32, 1)
+        sent = lax.dynamic_slice_in_dim(tile, (1 - core) * 32, 32, 1)
+        got = swap_cores(sent)
+        tile = jnp.where(
+            core == 0, jnp.concatenate([kept, got], 2), jnp.concatenate([got, kept], 2)
+        )
+        rounds = []
+        for step in range(4):
+            part = lax.dynamic_index_in_dim(tile, (x + step) % 4, 0, keepdims=False)
+            rounds.append(move(part, lambda y, z, core, x: (x + step, z, core, y)))
+        rounds = jnp.stack(rounds + rounds[:3])
+        block = lax.dynamic_slice_in_dim(rounds, (y - x) % 4, 4, 0).reshape(128, 128)
+        turned = after(place, block)[2]
         pieces = []
         for step in range(4):
-            part = lax.dynamic_slice_in_dim(normed, (zl + step) % 4 * 16, 16, 0)
+            part = lax.dynamic_slice_in_dim(normed, (turned + step) % 4 * 16, 16, 0)
             if step:
                 part = move(part, lambda y, z, core, x: (y, turn(z, step), core, x))
             pieces.append(part)
+        along_z = lax.all_to_all(
+            jnp.broadcast_to(block[None], (8, 128, 128)),
+            ("zh", "zl"),
+            split_axis=0,
+            concat_axis=0,
+            tiled=True,
+        )
+    with jax.named_scope("rows"):
         here = jnp.stack(pieces)
         left = move(here, lambda y, z, core, x: (y, z, core, x + 1))
         right = move(here, lambda y, z, core, x: (y, z, core, x - 1))
@@ -296,31 +320,7 @@
             move(right[:, count:], lambda y, z, core, x: (y, z, core, x - 1)),
         )
     with jax.named_scope("bias"):
-        tile = jnp.einsum(
-            "jkc,ch->hkj", normed.astype(F32), w_bias, precision=lax.Precision.HIGHEST
-        )
-        kept = lax.dynamic_slice_in_dim(tile, core * 32, 32, 1)
-        sent = lax.dynamic_slice_in_dim(tile, (1 - core) * 32, 32, 1)
-        got = swap_cores(sent)
-        tile = jnp.where(
-            core == 0, jnp.concatenate([kept, got], 2), jnp.concatenate([got, kept], 2)
-        )
-        rounds = []
-        for step in range(4):
-            part = lax.dynamic_index_in_dim(tile, (x + step) % 4, 0, keepdims=False)
-            rounds.append(move(part, lambda y, z, core, x: (x + step, z, core, y)))
-        rounds = jnp.stack(rounds + rounds[:3])
-        block = lax.dynamic_slice_in_dim(rounds, (y - x) % 4, 4, 0).reshape(128, 128)
-        block = after(block, here)
-        along_z = lax.all_to_all(
-            jnp.broadcast_to(block[None], (8, 128, 128)),
-            ("zh", "zl"),
-            split_axis=0,
-            concat_axis=0,
-            tiled=True,
-        )
-    with jax.named_scope("bias"):
-        along_z = after(along_z, left, right)
+        along_z = after(along_z, *pieces[1:])
         biases = []
         for step in range(4):
             moved = along_z

time: 196 us -> 203 us (1.036); the launches traced: 194 us -> 199 us
  blocking collectives: 23 us -> 0 us
  waiting for transfers between devices: 27.2 us -> 38.8 us
  starting transfers between devices: 51.2 us -> 61.6 us
  between operations: 0.41 us -> 4.54 us
    all_to_all x1 -> x0, blocking collectives: 23 us -> none  [on_device(): lax.all_to_all(jnp.broadcast_to(block[None], (8, 128, 128)), ('zh', 'zl')...]
    all_to_all x0 -> x1, waiting for transfers between devices: none -> 12.3 us  [on_device(): lax.all_to_all(jnp.broadcast_to(block[None], (8, 128, 128)), ('zh', 'zl')...]
    all_to_all x0 -> x1, starting transfers between devices: none -> 6.57 us  [on_device(): lax.all_to_all(jnp.broadcast_to(block[None], (8, 128, 128)), ('zh', 'zl')...]
    ppermute x25, starting transfers between devices: 51.2 us -> 55.1 us  [move(): return lax.ppermute(array, AXES, pairs)]
  transfers between devices with their start and end apart: 25 -> 26, of which waited for: 8 -> 8; matrix products, arithmetic and copies ran while one was open for 4% -> 5% of each run, Pallas kernels for 36% -> 35%
where the time goes in v3:
time: 203 us; the launch traced here: 199 us
  Pallas kernels  72.7 us (36%)
  starting transfers between devices  61.6 us (30%)
  waiting for transfers between devices  38.8 us (19%)
  local copies, waits for them, and re-layouts  13 us (6%)
  other arithmetic  5.85 us (3%)
  between operations  4.54 us (2%)
  matrix products  2.53 us (1%)
    pallas_call x2, Pallas kernels, attend(): pl.pallas_call(attend_kernel, out_shape=jax.ShapeDtypeStruct((4, count, 6...  70.3 us
    ppermute x25, starting transfers between devices, move(): return lax.ppermute(array, AXES, pairs)  55.1 us
    ppermute x25, waiting for transfers between devices, move(): return lax.ppermute(array, AXES, pairs)  26.5 us
    all_to_all x1, waiting for transfers between devices, on_device(): lax.all_to_all(jnp.broadcast_to(block[None], (8, 128, 128)), ('zh', 'zl')...  12.3 us
    all_to_all x1, starting transfers between devices, on_device(): lax.all_to_all(jnp.broadcast_to(block[None], (8, 128, 128)), ('zh', 'zl')...  6.57 us
  transfers between devices with their start and end apart: 26, of which 8 were waited for; matrix products, arithmetic and copies ran while one was open for 5% of the time, Pallas kernels for 35%

profile of v3, /device:TPU:1, one launch (start us, length us, event | category | flops | bytes accessed | tf_op | source)
XLA Modules:
  0.0 199.0 jit_solution(4318158479190626991)
XLA Ops:
  0.0 1.9 convert_reduce_fusion
  2.0 1.3 fusion.2
  3.3 1.3 fusion.5
  4.6 2.5 %fusion.6 = f32[64,64,4]{1,2,0:T(4,128)S(1)} fusion(bf16[64,64,128]{2,1,0:T(8,128)(2,1)S(1)} %fusion.5, f32[128,4]{0,1:T(4,128)S(1)} %copy-done), kind=kOutput, calls=%fused_computation.38 | convolution fusion | flops 25165824 | bytes 1116160 | tf_op jit(solution)/shard_map/bias/jkc,ch->hkj/dot_general | solution.py:285
  7.1 0.2 dynamic-slice_bitcast_fusion.2
  7.4 3.3 %collective-permute-start = (f32[4,32,64]{1,0,2:T(4,128)S(1)}, f32[4,32,64]{1,0,2:T(4,128)S(1)}, u32[]{:S(2)}, u32[]{:S(2)}) collective-permute-start(f32[4,32,64]{1,0,2:T(4,128)S(1)} %get-tuple-element.18), channel_id=1, source_target_pairs={{0,16},{1,17},{2,18},{3,19},{4,20},{5,21},{6,22},{7,23},{8,24},{9,... | collective-permute-start | bytes 98312 | tf_op jit(solution)/shard_map/bias/ppermute | solution.py:255
  10.8 0.9 collective-permute-done
  11.9 0.7 collective-permute-start.1
  12.7 0.5 copy.45.array
  13.2 4.4 %collective-permute-start.4 = (f32[32,128]{1,0:T(8,128)S(1)}, f32[32,128]{1,0:T(8,128)S(1)}, u32[]{:S(2)}, u32[]{:S(2)}) collective-permute-start(f32[32,128]{1,0:T(8,128)S(1)} %get-tuple-element.19), channel_id=1, source_target_pairs={{0,192},{1,193},{2,194},{3,195},{4,0},{5,1},{6,2},{7,3},{8,64},{9,... | collective-permute-start | bytes 49160 | tf_op jit(solution)/shard_map/bias/ppermute | solution.py:255
  17.6 2.6 %collective-permute-start.3 = (f32[32,128]{1,0:T(8,128)S(1)}, f32[32,128]{1,0:T(8,128)S(1)}, u32[]{:S(2)}, u32[]{:S(2)}) collective-permute-start(f32[32,128]{1,0:T(8,128)S(1)} %get-tuple-element.20), channel_id=1, source_target_pairs={{0,128},{1,129},{2,130},{3,131},{4,192},{5,193},{6,194},{7,195},{8... | collective-permute-start | bytes 49160 | tf_op jit(solution)/shard_map/bias/ppermute | solution.py:255
  20.2 3.8 %collective-permute-done.2 = f32[32,128]{1,0:T(8,128)S(1)} collective-permute-done((f32[32,128]{1,0:T(8,128)S(1)}, f32[32,128]{1,0:T(8,128)S(1)}, u32[]{:S(2)}, u32[]{:S(2)}) %collective-permute-start.2) | collective-permute-done | bytes 16416 | tf_op jit(solution)/shard_map/bias/ppermute | solution.py:255
  24.0 0.6 constant_dynamic-slice_fusion.3
  24.7 1.2 slice.33
  30.1 4.4 %collective-permute-start.7 = (bf16[16,64,128]{2,1,0:T(8,128)(2,1)S(1)}, bf16[16,64,128]{2,1,0:T(8,128)(2,1)S(1)}, u32[]{:S(2)}, u32[]{:S(2)}) collective-permute-start(bf16[16,64,128]{2,1,0:T(8,128)(2,1)S(1)} %get-tuple-element.6), channel_id=1, source_target_pairs={{0,3},{1,0},{2,1},{3,2},{4,7},{5,4},{6,5},{7,6},{8,11},{9,8},{10,9... | collective-permute-start | bytes 786440 | tf_op jit(solution)/shard_map/bias/ppermute | solution.py:255
  34.6 0.4 collective-permute-start.5
  34.9 0.8 broadcast_in_dim.6
  35.8 6.6 %all-to-all-start = ((f32[8,128,128]{2,1,0:T(8,128)}), f32[8,128,128]{2,1,0:T(8,128)S(1)}, u32[]{:S(2)}, u32[]{:S(2)}) async-start(f32[8,128,128]{2,1,0:T(8,128)} %broadcast_in_dim.6), calls=%async_computation | async-start | bytes 1048576 | tf_op jit(solution)/shard_map/bias/all_to_all | solution.py:307
  42.4 12.0 %collective-permute-done.6.rest_1_ = bf16[16,64,128]{2,1,0:T(8,128)(2,1)S(1)} collective-permute-done((bf16[16,64,128]{2,1,0:T(8,128)(2,1)S(1)}, bf16[16,64,128]{2,1,0:T(8,128)(2,1)S(1)}, u32[]{:S(2)}, u32[]{:S(2)}) %collective-permute-start.6) | collective-permute-done | bytes 262176 | tf_op jit(solution)/shard_map/bias/ppermute | solution.py:255
  54.3 1.1 pad_maximum_fusion.x0
  55.6 2.7 %collective-permute-start.10 = (bf16[4,16,64,128]{3,2,1,0:T(8,128)(2,1)}, bf16[4,16,64,128]{3,2,1,0:T(8,128)(2,1)}, u32[]{:S(2)}, u32[]{:S(2)}) collective-permute-start(bf16[4,16,64,128]{3,2,1,0:T(8,128)(2,1)} %pad_maximum_fusion.x0), channel_id=1, source_target_pairs={{0,12},{1,13},{2,14},{3,15},{4,0},{5,1},{6,2},{7,3},{8,4},{9,5},{1... | collective-permute-start | bytes 3145736 | tf_op jit(solution)/shard_map/rows/ppermute | solution.py:255
  58.2 12.3 %all-to-all-done.array = f32[8,128,128]{2,1,0:T(8,128)S(1)} async-done(((f32[8,128,128]{2,1,0:T(8,128)}), f32[8,128,128]{2,1,0:T(8,128)S(1)}, u32[]{:S(2)}, u32[]{:S(2)}) %all-to-all-start) | async-done | bytes 524320 | tf_op jit(solution)/shard_map/bias/all_to_all | solution.py:307
  70.5 0.8 copy-done.1
  71.4 1.8 collective-permute-start.16
  73.2 0.3 collective-permute-start.14
  73.5 0.4 collective-permute-start.12
  73.9 9.9 %collective-permute-start.11 = (f32[8,128,128]{2,1,0:T(8,128)}, f32[8,128,128]{2,1,0:T(8,128)S(1)}, u32[]{:S(2)}, u32[]{:S(2)}) collective-permute-start(f32[8,128,128]{2,1,0:T(8,128)} %tie.5.b00), channel_id=1, source_target_pairs={{0,16},{1,17},{2,18},{3,19},{4,20},{5,21},{6,22},{7,23},{8,24},{9,... | collective-permute-start | bytes 1572872 | tf_op jit(solution)/shard_map/bias/ppermute | solution.py:255
  83.8 1.9 slice.44
  85.7 11.3 %collective-permute-start.17 = (f32[8,128,128]{2,1,0:T(8,128)S(1)}, f32[8,128,128]{2,1,0:T(8,128)S(1)}, u32[]{:S(2)}, u32[]{:S(2)}) collective-permute-start(f32[8,128,128]{2,1,0:T(8,128)S(1)} %collective-permute-done.16.b30), channel_id=1, source_target_pairs={{0,16},{1,17},{2,18},{3,19},{4,20},{5,21},{6,22},{7,23},{8,24},{9,... | collective-permute-start | bytes 1572872 | tf_op jit(solution)/shard_map/bias/ppermute | solution.py:255
  96.9 3.2 %collective-permute-done.12.b10 = f32[8,128,128]{2,1,0:T(8,128)S(1)} collective-permute-done((f32[8,128,128]{2,1,0:T(8,128)}, f32[8,128,128]{2,1,0:T(8,128)S(1)}, u32[]{:S(2)}, u32[]{:S(2)}) %collective-permute-start.12) | collective-permute-done | bytes 524320 | tf_op jit(solution)/shard_map/bias/ppermute | solution.py:255
  100.1 0.4 collective-permute-start.13
  100.5 1.9 slice.45
  103.1 35.2 %attention.2.rest_0_ = bf16[4,8,64,128]{3,2,1,0:T(8,128)(2,1)S(1)} custom-call(s32[4]{0:T(128)S(1)} %pad_add_fusion.at.array, bf16[4,16,64,128]{3,2,1,0:T(8,128)(2,1)} %pad_maximum_fusion.x0, bf16[4,16,64,128]{3,2,1,0:T(8,128)(2,1)} %collective-permute-done.8.x1, bf16[4,8,64,128]{3,2,1,0:T(8,128)(2,1)} %collective-permute-done.9.x2, ...), custom_call_target="tpu_custom_call" | custom-call | flops 2400000000 | bytes 8388608 | tf_op jit(solution)/shard_map/attention/attention/pallas_call | solution.py:170
  138.3 0.8 copy-done.4
  139.1 1.9 slice_bitcast_fusion.4
  141.0 2.5 %collective-permute-start.21 = (bf16[8,64,128]{2,1,0:T(8,128)(2,1)S(1)}, bf16[8,64,128]{2,1,0:T(8,128)(2,1)S(1)}, u32[]{:S(2)}, u32[]{:S(2)}) collective-permute-start(bf16[8,64,128]{2,1,0:T(8,128)(2,1)S(1)} %get-tuple-element.13), channel_id=1, source_target_pairs={{0,1},{1,2},{2,3},{3,0},{4,5},{5,6},{6,7},{7,4},{8,9},{9,10},{10,1... | collective-permute-start | bytes 393224 | tf_op jit(solution)/shard_map/update/ppermute | solution.py:255
  143.5 4.1 %collective-permute-start.20 = (bf16[8,64,128]{2,1,0:T(8,128)(2,1)}, bf16[8,64,128]{2,1,0:T(8,128)(2,1)}, u32[]{:S(2)}, u32[]{:S(2)}) collective-permute-start(bf16[8,64,128]{2,1,0:T(8,128)(2,1)} %get-tuple-element.14), channel_id=1, source_target_pairs={{0,2},{1,3},{2,0},{3,1},{4,6},{5,7},{6,4},{7,5},{8,10},{9,11},{10,... | collective-permute-start | bytes 393224 | tf_op jit(solution)/shard_map/update/ppermute | solution.py:255
  147.7 2.4 %collective-permute-start.19 = (bf16[8,64,128]{2,1,0:T(8,128)(2,1)}, bf16[8,64,128]{2,1,0:T(8,128)(2,1)}, u32[]{:S(2)}, u32[]{:S(2)}) collective-permute-start(bf16[8,64,128]{2,1,0:T(8,128)(2,1)} %get-tuple-element.15), channel_id=1, source_target_pairs={{0,3},{1,0},{2,1},{3,2},{4,7},{5,4},{6,5},{7,6},{8,11},{9,8},{10,9... | collective-permute-start | bytes 393224 | tf_op jit(solution)/shard_map/update/ppermute | solution.py:255
  150.0 35.2 %attention.3.rest_0_ = bf16[4,8,64,128]{3,2,1,0:T(8,128)(2,1)S(1)} custom-call(s32[4]{0:T(128)S(1)} %copy-done.6, bf16[4,16,64,128]{3,2,1,0:T(8,128)(2,1)} %pad_maximum_fusion.x0, bf16[4,16,64,128]{3,2,1,0:T(8,128)(2,1)} %collective-permute-done.8.x1, bf16[4,8,64,128]{3,2,1,0:T(8,128)(2,1)} %collective-permute-done.18.x2, ...), custom_call_target="tpu_custom_call" | custom-call | flops 2400000000 | bytes 8388608 | tf_op jit(solution)/shard_map/attention/attention/pallas_call | solution.py:170
  185.2 0.8 slice_bitcast_fusion
  186.0 0.3 collective-permute-start.23
  186.3 3.1 %collective-permute-start.22 = (bf16[8,64,128]{2,1,0:T(8,128)(2,1)S(1)}, bf16[8,64,128]{2,1,0:T(8,128)(2,1)S(1)}, u32[]{:S(2)}, u32[]{:S(2)}) collective-permute-start(bf16[8,64,128]{2,1,0:T(8,128)(2,1)S(1)} %get-tuple-element.11), channel_id=1, source_target_pairs={{0,3},{1,0},{2,1},{3,2},{4,7},{5,4},{6,5},{7,6},{8,11},{9,8},{10,9... | collective-permute-start | bytes 393224 | tf_op jit(solution)/shard_map/update/ppermute | solution.py:255
  189.4 2.5 %collective-permute-done.24.refs_7_ = bf16[8,64,128]{2,1,0:T(8,128)(2,1)S(1)} collective-permute-done((bf16[8,64,128]{2,1,0:T(8,128)(2,1)S(1)}, bf16[8,64,128]{2,1,0:T(8,128)(2,1)S(1)}, u32[]{:S(2)}, u32[]{:S(2)}) %collective-permute-start.24) | collective-permute-done | bytes 131104 | tf_op jit(solution)/shard_map/update/ppermute | solution.py:255
  191.8 3.9 %collective-permute-done.23.refs_6_ = bf16[8,64,128]{2,1,0:T(8,128)(2,1)S(1)} collective-permute-done((bf16[8,64,128]{2,1,0:T(8,128)(2,1)S(1)}, bf16[8,64,128]{2,1,0:T(8,128)(2,1)S(1)}, u32[]{:S(2)}, u32[]{:S(2)}) %collective-permute-start.23) | collective-permute-done | bytes 131104 | tf_op jit(solution)/shard_map/update/ppermute | solution.py:255
  195.7 0.3 collective-permute-done.22.refs_5_
  196.0 0.3 copy-done.19
  196.4 0.3 copy-done.20
  196.7 2.3 %assemble_update.1 = bf16[64,64,128]{2,1,0:T(8,128)(2,1)} custom-call(s32[4]{0:T(128)} %tie.7.at, bf16[8,64,128]{2,1,0:T(8,128)(2,1)} %get-tuple-element.16.refs_0_, bf16[8,64,128]{2,1,0:T(8,128)(2,1)} %collective-permute-done.19.refs_1_, bf16[8,64,128]{2,1,0:T(8,128)(2,1)} %collective-permute-done.20.refs_2_, bf16[8,64,128]{2,1,0:T(8,128)(2,1)} %copy-done.17, ...), custom_call_target="tpu_custom_call" | custom-call | tf_op jit(solution)/shard_map/assemble_update/pallas_call | solution.py:217
  (98 shorter events, 1.4 us)
Async XLA Ops:
  0.0 4.6 %copy-start = (f32[128,4]{0,1:T(4,128)S(1)}, f32[128,4]{0,1:T(4,128)}, u32[]{:S(2)}) copy-start(f32[128,4]{0,1:T(4,128)} %param.19) | copy-start | bytes 6148
  0.0 2.0 copy-start.12
  0.0 3.3 %copy-start.25 = (f32[128]{0:T(128)S(1)}, f32[128]{0:T(128)}, u32[]{:S(2)}) copy-start(f32[128]{0:T(128)} %param.13) | copy-start | bytes 1540
  0.0 3.3 %copy-start.26 = (f32[128]{0:T(128)S(1)}, f32[128]{0:T(128)}, u32[]{:S(2)}) copy-start(f32[128]{0:T(128)} %param.12) | copy-start | bytes 1540
  7.4 4.3 %collective-permute-start = (f32[4,32,64]{1,0,2:T(4,128)S(1)}, f32[4,32,64]{1,0,2:T(4,128)S(1)}, u32[]{:S(2)}, u32[]{:S(2)}) collective-permute-start(f32[4,32,64]{1,0,2:T(4,128)S(1)} %get-tuple-element.18), channel_id=1, source_target_pairs={{0,16},{1,17},{2,18},{3,19},{4,20},{5,21},{6,22},{7,23},{8,24},{9,... | collective-permute-start | bytes 98312 | tf_op jit(solution)/shard_map/bias/ppermute | solution.py:255
  11.9 8.3 %collective-permute-start.1 = (f32[32,128]{1,0:T(8,128)S(1)}, f32[32,128]{1,0:T(8,128)S(1)}, u32[]{:S(2)}, u32[]{:S(2)}) collective-permute-start(f32[32,128]{1,0:T(8,128)S(1)} %get-tuple-element.22), channel_id=1, source_target_pairs={{0,0},{1,1},{2,2},{3,3},{4,64},{5,65},{6,66},{7,67},{8,128},{9,129... | collective-permute-start | bytes 49160 | tf_op jit(solution)/shard_map/bias/ppermute | solution.py:255
  12.7 90.4 %copy-start.5 = (s32[4]{0:T(128)}, s32[4]{0:T(128)S(1)}, u32[]{:S(2)}) copy-start(s32[4]{0:T(128)S(1)} %pad_add_fusion.at.array) | copy-start | bytes 52
  13.2 10.8 %collective-permute-start.4 = (f32[32,128]{1,0:T(8,128)S(1)}, f32[32,128]{1,0:T(8,128)S(1)}, u32[]{:S(2)}, u32[]{:S(2)}) collective-permute-start(f32[32,128]{1,0:T(8,128)S(1)} %get-tuple-element.19), channel_id=1, source_target_pairs={{0,192},{1,193},{2,194},{3,195},{4,0},{5,1},{6,2},{7,3},{8,64},{9,... | collective-permute-start | bytes 49160 | tf_op jit(solution)/shard_map/bias/ppermute | solution.py:255
  17.6 6.4 %collective-permute-start.3 = (f32[32,128]{1,0:T(8,128)S(1)}, f32[32,128]{1,0:T(8,128)S(1)}, u32[]{:S(2)}, u32[]{:S(2)}) collective-permute-start(f32[32,128]{1,0:T(8,128)S(1)} %get-tuple-element.20), channel_id=1, source_target_pairs={{0,128},{1,129},{2,130},{3,131},{4,192},{5,193},{6,194},{7,195},{8... | collective-permute-start | bytes 49160 | tf_op jit(solution)/shard_map/bias/ppermute | solution.py:255
  20.2 3.8 %collective-permute-start.2 = (f32[32,128]{1,0:T(8,128)S(1)}, f32[32,128]{1,0:T(8,128)S(1)}, u32[]{:S(2)}, u32[]{:S(2)}) collective-permute-start(f32[32,128]{1,0:T(8,128)S(1)} %get-tuple-element.21), channel_id=1, source_target_pairs={{0,64},{1,65},{2,66},{3,67},{4,128},{5,129},{6,130},{7,131},{8,192... | collective-permute-start | bytes 49160 | tf_op jit(solution)/shard_map/bias/ppermute | solution.py:255
  30.0 4.9 %copy-start.16 = (f32[4,32,128]{2,1,0:T(8,128)S(1)}, f32[4,32,128]{2,1,0:T(8,128)}, u32[]{:S(2)}) copy-start(f32[4,32,128]{2,1,0:T(8,128)} %constant_dynamic-slice_fusion.3) | copy-start | bytes 196612
  30.1 12.2 %collective-permute-start.7 = (bf16[16,64,128]{2,1,0:T(8,128)(2,1)S(1)}, bf16[16,64,128]{2,1,0:T(8,128)(2,1)S(1)}, u32[]{:S(2)}, u32[]{:S(2)}) collective-permute-start(bf16[16,64,128]{2,1,0:T(8,128)(2,1)S(1)} %get-tuple-element.6), channel_id=1, source_target_pairs={{0,3},{1,0},{2,1},{3,2},{4,7},{5,4},{6,5},{7,6},{8,11},{9,8},{10,9... | collective-permute-start | bytes 786440 | tf_op jit(solution)/shard_map/bias/ppermute | solution.py:255
  34.6 19.8 %collective-permute-start.6 = (bf16[16,64,128]{2,1,0:T(8,128)(2,1)S(1)}, bf16[16,64,128]{2,1,0:T(8,128)(2,1)S(1)}, u32[]{:S(2)}, u32[]{:S(2)}) collective-permute-start(bf16[16,64,128]{2,1,0:T(8,128)(2,1)S(1)} %get-tuple-element.7), channel_id=1, source_target_pairs={{0,2},{1,3},{2,0},{3,1},{4,6},{5,7},{6,4},{7,5},{8,10},{9,11},{10,... | collective-permute-start | bytes 786440 | tf_op jit(solution)/shard_map/bias/ppermute | solution.py:255
  34.6 19.8 %collective-permute-start.5 = (bf16[16,64,128]{2,1,0:T(8,128)(2,1)S(1)}, bf16[16,64,128]{2,1,0:T(8,128)(2,1)S(1)}, u32[]{:S(2)}, u32[]{:S(2)}) collective-permute-start(bf16[16,64,128]{2,1,0:T(8,128)(2,1)S(1)} %get-tuple-element.8), channel_id=1, source_target_pairs={{0,1},{1,2},{2,3},{3,0},{4,5},{5,6},{6,7},{7,4},{8,9},{9,10},{10,1... | collective-permute-start | bytes 786440 | tf_op jit(solution)/shard_map/bias/ppermute | solution.py:255
  35.8 34.7 %all-to-all-start = ((f32[8,128,128]{2,1,0:T(8,128)}), f32[8,128,128]{2,1,0:T(8,128)S(1)}, u32[]{:S(2)}, u32[]{:S(2)}) async-start(f32[8,128,128]{2,1,0:T(8,128)} %broadcast_in_dim.6), calls=%async_computation | async-start | bytes 1048576 | tf_op jit(solution)/shard_map/bias/all_to_all | solution.py:307
  42.3 13.1 %copy-start.13 = (bf16[16,64,128]{2,1,0:T(8,128)(2,1)}, bf16[16,64,128]{2,1,0:T(8,128)(2,1)S(1)}, u32[]{:S(2)}) copy-start(bf16[16,64,128]{2,1,0:T(8,128)(2,1)S(1)} %collective-permute-done.7.rest_2_) | copy-start | bytes 786436
  54.3 1.1 copy-start.14
  55.5 18.4 %collective-permute-start.8 = (bf16[4,16,64,128]{3,2,1,0:T(8,128)(2,1)}, bf16[4,16,64,128]{3,2,1,0:T(8,128)(2,1)}, u32[]{:S(2)}, u32[]{:S(2)}) collective-permute-start(bf16[4,16,64,128]{3,2,1,0:T(8,128)(2,1)} %pad_maximum_fusion.x0), channel_id=1, source_target_pairs={{0,4},{1,5},{2,6},{3,7},{4,8},{5,9},{6,10},{7,11},{8,12},{9,13},{1... | collective-permute-start | bytes 3145736 | tf_op jit(solution)/shard_map/rows/ppermute | solution.py:255
  55.6 30.1 %collective-permute-start.10 = (bf16[4,16,64,128]{3,2,1,0:T(8,128)(2,1)}, bf16[4,16,64,128]{3,2,1,0:T(8,128)(2,1)}, u32[]{:S(2)}, u32[]{:S(2)}) collective-permute-start(bf16[4,16,64,128]{3,2,1,0:T(8,128)(2,1)} %pad_maximum_fusion.x0), channel_id=1, source_target_pairs={{0,12},{1,13},{2,14},{3,15},{4,0},{5,1},{6,2},{7,3},{8,4},{9,5},{1... | collective-permute-start | bytes 3145736 | tf_op jit(solution)/shard_map/rows/ppermute | solution.py:255
  71.3 31.2 %copy-start.21 = (bf16[128,128]{1,0:T(8,128)(2,1)S(1)}, bf16[128,128]{1,0:T(8,128)(2,1)}, u32[]{:S(2)}) copy-start(bf16[128,128]{1,0:T(8,128)(2,1)} %param.14) | copy-start | bytes 98308
  71.3 31.3 %copy-start.22 = (bf16[128,128]{1,0:T(8,128)(2,1)S(1)}, bf16[128,128]{1,0:T(8,128)(2,1)}, u32[]{:S(2)}) copy-start(bf16[128,128]{1,0:T(8,128)(2,1)} %param.16) | copy-start | bytes 98308
  71.3 31.5 %copy-start.23 = (bf16[128,128]{1,0:T(8,128)(2,1)S(1)}, bf16[128,128]{1,0:T(8,128)(2,1)}, u32[]{:S(2)}) copy-start(bf16[128,128]{1,0:T(8,128)(2,1)} %param.17) | copy-start | bytes 98308
  71.3 31.6 %copy-start.24 = (f32[128]{0:T(128)S(1)}, f32[128]{0:T(128)}, u32[]{:S(2)}) copy-start(f32[128]{0:T(128)} %param.18) | copy-start | bytes 1540
  71.3 31.8 %copy-start.2 = (f32[8,128,128]{2,1,0:T(8,128)S(1)}, f32[8,128,128]{2,1,0:T(8,128)}, u32[]{:S(2)}) copy-start(f32[8,128,128]{2,1,0:T(8,128)} %tie.5.b00) | copy-start | bytes 1572868
  71.3 31.8 %copy-start.9 = (bf16[128,128]{1,0:T(8,128)(2,1)S(1)}, bf16[128,128]{1,0:T(8,128)(2,1)}, u32[]{:S(2)}) copy-start(bf16[128,128]{1,0:T(8,128)(2,1)} %w_key.3) | copy-start | bytes 98308
  71.4 31.8 %copy-start.10 = (bf16[128,128]{1,0:T(8,128)(2,1)S(1)}, bf16[128,128]{1,0:T(8,128)(2,1)}, u32[]{:S(2)}) copy-start(bf16[128,128]{1,0:T(8,128)(2,1)} %w_out.3) | copy-start | bytes 98308
  71.4 31.8 %copy-start.11 = (f32[128]{0:T(128)S(1)}, f32[128]{0:T(128)}, u32[]{:S(2)}) copy-start(f32[128]{0:T(128)} %param.21) | copy-start | bytes 1540
  71.4 14.3 %collective-permute-start.16 = (f32[8,128,128]{2,1,0:T(8,128)}, f32[8,128,128]{2,1,0:T(8,128)S(1)}, u32[]{:S(2)}, u32[]{:S(2)}) collective-permute-start(f32[8,128,128]{2,1,0:T(8,128)} %tie.5.b00), channel_id=1, source_target_pairs={{0,192},{1,193},{2,194},{3,195},{4,196},{5,197},{6,198},{7,199},{8... | collective-permute-start | bytes 1572872 | tf_op jit(solution)/shard_map/bias/ppermute | solution.py:255
  73.2 23.7 %collective-permute-start.14 = (f32[8,128,128]{2,1,0:T(8,128)}, f32[8,128,128]{2,1,0:T(8,128)S(1)}, u32[]{:S(2)}, u32[]{:S(2)}) collective-permute-start(f32[8,128,128]{2,1,0:T(8,128)} %tie.5.b00), channel_id=1, source_target_pairs={{0,128},{1,129},{2,130},{3,131},{4,132},{5,133},{6,134},{7,135},{8... | collective-permute-start | bytes 1572872 | tf_op jit(solution)/shard_map/bias/ppermute | solution.py:255
  73.5 26.6 %collective-permute-start.12 = (f32[8,128,128]{2,1,0:T(8,128)}, f32[8,128,128]{2,1,0:T(8,128)S(1)}, u32[]{:S(2)}, u32[]{:S(2)}) collective-permute-start(f32[8,128,128]{2,1,0:T(8,128)} %tie.5.b00), channel_id=1, source_target_pairs={{0,64},{1,65},{2,66},{3,67},{4,68},{5,69},{6,70},{7,71},{8,72},{9,... | collective-permute-start | bytes 1572872 | tf_op jit(solution)/shard_map/bias/ppermute | solution.py:255
  73.9 28.5 %collective-permute-start.11 = (f32[8,128,128]{2,1,0:T(8,128)}, f32[8,128,128]{2,1,0:T(8,128)S(1)}, u32[]{:S(2)}, u32[]{:S(2)}) collective-permute-start(f32[8,128,128]{2,1,0:T(8,128)} %tie.5.b00), channel_id=1, source_target_pairs={{0,16},{1,17},{2,18},{3,19},{4,20},{5,21},{6,22},{7,23},{8,24},{9,... | collective-permute-start | bytes 1572872 | tf_op jit(solution)/shard_map/bias/ppermute | solution.py:255
  85.6 17.4 %collective-permute-start.9 = (bf16[4,8,64,128]{3,2,1,0:T(8,128)(2,1)}, bf16[4,8,64,128]{3,2,1,0:T(8,128)(2,1)}, u32[]{:S(2)}, u32[]{:S(2)}) collective-permute-start(bf16[4,8,64,128]{3,2,1,0:T(8,128)(2,1)} %slice.44), channel_id=1, source_target_pairs={{0,4},{1,5},{2,6},{3,7},{4,8},{5,9},{6,10},{7,11},{8,12},{9,13},{1... | collective-permute-start | bytes 1572872 | tf_op jit(solution)/shard_map/rows/ppermute | solution.py:255
  85.7 17.4 %collective-permute-start.17 = (f32[8,128,128]{2,1,0:T(8,128)S(1)}, f32[8,128,128]{2,1,0:T(8,128)S(1)}, u32[]{:S(2)}, u32[]{:S(2)}) collective-permute-start(f32[8,128,128]{2,1,0:T(8,128)S(1)} %collective-permute-done.16.b30), channel_id=1, source_target_pairs={{0,16},{1,17},{2,18},{3,19},{4,20},{5,21},{6,22},{7,23},{8,24},{9,... | collective-permute-start | bytes 1572872 | tf_op jit(solution)/shard_map/bias/ppermute | solution.py:255
  96.9 6.1 %collective-permute-start.15 = (f32[8,128,128]{2,1,0:T(8,128)S(1)}, f32[8,128,128]{2,1,0:T(8,128)}, u32[]{:S(2)}, u32[]{:S(2)}) collective-permute-start(f32[8,128,128]{2,1,0:T(8,128)S(1)} %collective-permute-done.14.b20), channel_id=1, source_target_pairs={{0,16},{1,17},{2,18},{3,19},{4,20},{5,21},{6,22},{7,23},{8,24},{9,... | collective-permute-start | bytes 1572872 | tf_op jit(solution)/shard_map/bias/ppermute | solution.py:255
  100.1 3.0 %collective-permute-start.13 = (f32[8,128,128]{2,1,0:T(8,128)S(1)}, f32[8,128,128]{2,1,0:T(8,128)}, u32[]{:S(2)}, u32[]{:S(2)}) collective-permute-start(f32[8,128,128]{2,1,0:T(8,128)S(1)} %collective-permute-done.12.b10), channel_id=1, source_target_pairs={{0,16},{1,17},{2,18},{3,19},{4,20},{5,21},{6,22},{7,23},{8,24},{9,... | collective-permute-start | bytes 1572872 | tf_op jit(solution)/shard_map/bias/ppermute | solution.py:255
  102.4 47.6 %collective-permute-start.18 = (bf16[4,8,64,128]{3,2,1,0:T(8,128)(2,1)}, bf16[4,8,64,128]{3,2,1,0:T(8,128)(2,1)}, u32[]{:S(2)}, u32[]{:S(2)}) collective-permute-start(bf16[4,8,64,128]{3,2,1,0:T(8,128)(2,1)} %slice.45), channel_id=1, source_target_pairs={{0,12},{1,13},{2,14},{3,15},{4,0},{5,1},{6,2},{7,3},{8,4},{9,5},{1... | collective-permute-start | bytes 1572872 | tf_op jit(solution)/shard_map/rows/ppermute | solution.py:255
  103.1 35.2 %copy-start.7 = (f32[8,128,128]{2,1,0:T(8,128)}, f32[8,128,128]{2,1,0:T(8,128)S(1)}, u32[]{:S(2)}) copy-start(f32[8,128,128]{2,1,0:T(8,128)S(1)} %collective-permute-done.17.b31) | copy-start | bytes 1572868
  139.1 10.9 %copy-start.6 = (s32[4]{0:T(128)S(1)}, s32[4]{0:T(128)}, u32[]{:S(2)}) copy-start(s32[4]{0:T(128)} %tie.6.at.array) | copy-start | bytes 52
  139.1 10.9 %copy-start.8 = (f32[8,128,128]{2,1,0:T(8,128)S(1)}, f32[8,128,128]{2,1,0:T(8,128)}, u32[]{:S(2)}) copy-start(f32[8,128,128]{2,1,0:T(8,128)} %copy-done.7) | copy-start | bytes 1572868
  141.0 45.3 %collective-permute-start.21 = (bf16[8,64,128]{2,1,0:T(8,128)(2,1)S(1)}, bf16[8,64,128]{2,1,0:T(8,128)(2,1)S(1)}, u32[]{:S(2)}, u32[]{:S(2)}) collective-permute-start(bf16[8,64,128]{2,1,0:T(8,128)(2,1)S(1)} %get-tuple-element.13), channel_id=1, source_target_pairs={{0,1},{1,2},{2,3},{3,0},{4,5},{5,6},{6,7},{7,4},{8,9},{9,10},{10,1... | collective-permute-start | bytes 393224 | tf_op jit(solution)/shard_map/update/ppermute | solution.py:255
  143.5 45.8 %collective-permute-start.20 = (bf16[8,64,128]{2,1,0:T(8,128)(2,1)}, bf16[8,64,128]{2,1,0:T(8,128)(2,1)}, u32[]{:S(2)}, u32[]{:S(2)}) collective-permute-start(bf16[8,64,128]{2,1,0:T(8,128)(2,1)} %get-tuple-element.14), channel_id=1, source_target_pairs={{0,2},{1,3},{2,0},{3,1},{4,6},{5,7},{6,4},{7,5},{8,10},{9,11},{10,... | collective-permute-start | bytes 393224 | tf_op jit(solution)/shard_map/update/ppermute | solution.py:255
  147.7 41.7 %collective-permute-start.19 = (bf16[8,64,128]{2,1,0:T(8,128)(2,1)}, bf16[8,64,128]{2,1,0:T(8,128)(2,1)}, u32[]{:S(2)}, u32[]{:S(2)}) collective-permute-start(bf16[8,64,128]{2,1,0:T(8,128)(2,1)} %get-tuple-element.15), channel_id=1, source_target_pairs={{0,3},{1,0},{2,1},{3,2},{4,7},{5,4},{6,5},{7,6},{8,11},{9,8},{10,9... | collective-permute-start | bytes 393224 | tf_op jit(solution)/shard_map/update/ppermute | solution.py:255
  185.2 4.1 %copy-start.3 = (bf16[4,8,64,128]{3,2,1,0:T(8,128)(2,1)}, bf16[4,8,64,128]{3,2,1,0:T(8,128)(2,1)S(1)}, u32[]{:S(2)}) copy-start(bf16[4,8,64,128]{3,2,1,0:T(8,128)(2,1)S(1)} %attention.3.rest_0_) | copy-start | bytes 1572868
  186.0 5.8 %collective-permute-start.24 = (bf16[8,64,128]{2,1,0:T(8,128)(2,1)S(1)}, bf16[8,64,128]{2,1,0:T(8,128)(2,1)S(1)}, u32[]{:S(2)}, u32[]{:S(2)}) collective-permute-start(bf16[8,64,128]{2,1,0:T(8,128)(2,1)S(1)} %get-tuple-element.9), channel_id=1, source_target_pairs={{0,1},{1,2},{2,3},{3,0},{4,5},{5,6},{6,7},{7,4},{8,9},{9,10},{10,1... | collective-permute-start | bytes 393224 | tf_op jit(solution)/shard_map/update/ppermute | solution.py:255
  186.0 9.7 %collective-permute-start.23 = (bf16[8,64,128]{2,1,0:T(8,128)(2,1)S(1)}, bf16[8,64,128]{2,1,0:T(8,128)(2,1)S(1)}, u32[]{:S(2)}, u32[]{:S(2)}) collective-permute-start(bf16[8,64,128]{2,1,0:T(8,128)(2,1)S(1)} %get-tuple-element.10), channel_id=1, source_target_pairs={{0,2},{1,3},{2,0},{3,1},{4,6},{5,7},{6,4},{7,5},{8,10},{9,11},{10,... | collective-permute-start | bytes 393224 | tf_op jit(solution)/shard_map/update/ppermute | solution.py:255
  186.3 9.7 %copy-start.17 = (bf16[8,64,128]{2,1,0:T(8,128)(2,1)}, bf16[8,64,128]{2,1,0:T(8,128)(2,1)S(1)}, u32[]{:S(2)}) copy-start(bf16[8,64,128]{2,1,0:T(8,128)(2,1)S(1)} %collective-permute-done.21.refs_3_) | copy-start | bytes 393220
  186.3 9.7 %collective-permute-start.22 = (bf16[8,64,128]{2,1,0:T(8,128)(2,1)S(1)}, bf16[8,64,128]{2,1,0:T(8,128)(2,1)S(1)}, u32[]{:S(2)}, u32[]{:S(2)}) collective-permute-start(bf16[8,64,128]{2,1,0:T(8,128)(2,1)S(1)} %get-tuple-element.11), channel_id=1, source_target_pairs={{0,3},{1,0},{2,1},{3,2},{4,7},{5,4},{6,5},{7,6},{8,11},{9,8},{10,9... | collective-permute-start | bytes 393224 | tf_op jit(solution)/shard_map/update/ppermute | solution.py:255
  191.8 4.2 %copy-start.18 = (bf16[8,64,128]{2,1,0:T(8,128)(2,1)}, bf16[8,64,128]{2,1,0:T(8,128)(2,1)S(1)}, u32[]{:S(2)}) copy-start(bf16[8,64,128]{2,1,0:T(8,128)(2,1)S(1)} %collective-permute-done.24.refs_7_) | copy-start | bytes 393220
  (5 other events, 4.1 us)

commit v4 on v2

--- a/solution.py
+++ b/solution.py
@@ -226,11 +226,12 @@
     pass
 
 
-def after(array, *earlier):
+def after(array, *earlier, where=pltpu.VMEM):
     return pl.pallas_call(
         tie_kernel,
         out_shape=jax.ShapeDtypeStruct(array.shape, array.dtype),
-        in_specs=[pl.BlockSpec(memory_space=pl.ANY)] * (1 + len(earlier)),
+        in_specs=[pl.BlockSpec(memory_space=pl.ANY)]
+        + [pl.BlockSpec(memory_space=where)] * len(earlier),
         out_specs=pl.BlockSpec(memory_space=pl.ANY),
         input_output_aliases={0: 0},
         name="tie",
@@ -338,7 +339,7 @@
                 w_out,
                 out_shift[None],
             )
-            place = after(place, part)
+            place = after(place, part, where=pl.ANY)
         with jax.named_scope("update"):
             for step in range(4):
                 back = part[step]

time: 198 us -> 201 us (1.015)
  Pallas kernels: 72.4 us -> 75.2 us
    pallas_call x4, Pallas kernels: 0.01 us -> 2.77 us  [after(): pl.pallas_call(tie_kernel, out_shape=jax.ShapeDtypeStruct(array.shape, ar...]
where the time goes in v4:
time: 201 us; the launch traced here: 199 us
  Pallas kernels  75.2 us (37%)
  starting transfers between devices  52.5 us (26%)
  waiting for transfers between devices  29 us (14%)
  blocking collectives  23 us (11%)
  local copies, waits for them, and re-layouts  10.6 us (5%)
  other arithmetic  5.82 us (3%)
  matrix products  2.53 us (1%)
    pallas_call x2, Pallas kernels, attend(): pl.pallas_call(attend_kernel, out_shape=jax.ShapeDtypeStruct((4, count, 6...  70.1 us
    ppermute x24, starting transfers between devices, move(): return lax.ppermute(array, AXES, pairs)  52.5 us
    ppermute x24, waiting for transfers between devices, move(): return lax.ppermute(array, AXES, pairs)  29 us
    all_to_all x1, blocking collectives, on_device(): lax.all_to_all(jnp.broadcast_to(block[None], (8, 128, 128)), ('zh', 'zl')...  23 us
    unnamed x63, local copies, waits for them, and re-layouts  5.77 us
  transfers between devices with their start and end apart: 24, of which 9 were waited for; matrix products, arithmetic and copies ran while one was open for 2% of the time, Pallas kernels for 18%

profile of v4, /device:TPU:1, one launch (start us, length us, event | category | flops | bytes accessed | tf_op | source)
XLA Modules:
  0.0 199.1 jit_solution(17049095673879430605)
XLA Ops:
  0.0 1.9 convert_reduce_fusion
  2.0 1.3 fusion.2
  3.3 1.3 fusion.5
  4.6 2.5 %fusion.6 = f32[64,64,4]{1,2,0:T(4,128)S(1)} fusion(bf16[64,64,128]{2,1,0:T(8,128)(2,1)S(1)} %fusion.5, f32[128,4]{0,1:T(4,128)S(1)} %copy-done), kind=kOutput, calls=%fused_computation.38 | convolution fusion | flops 25165824 | bytes 1116160 | tf_op jit(solution)/shard_map/bias/jkc,ch->hkj/dot_general | solution.py:295
  7.4 3.3 %collective-permute-start.6 = (f32[4,32,64]{1,0,2:T(4,128)S(1)}, f32[4,32,64]{1,0,2:T(4,128)S(1)}, u32[]{:S(2)}, u32[]{:S(2)}) collective-permute-start(f32[4,32,64]{1,0,2:T(4,128)S(1)} %get-tuple-element.18), channel_id=1, source_target_pairs={{0,16},{1,17},{2,18},{3,19},{4,20},{5,21},{6,22},{7,23},{8,24},{9,... | collective-permute-start | bytes 98312 | tf_op jit(solution)/shard_map/bias/ppermute | solution.py:254
  10.8 0.9 collective-permute-done.6
  11.9 0.7 collective-permute-start.7
  12.7 2.7 %collective-permute-start.2 = (bf16[16,64,128]{2,1,0:T(8,128)(2,1)S(1)}, bf16[16,64,128]{2,1,0:T(8,128)(2,1)S(1)}, u32[]{:S(2)}, u32[]{:S(2)}) collective-permute-start(bf16[16,64,128]{2,1,0:T(8,128)(2,1)S(1)} %get-tuple-element.6), channel_id=1, source_target_pairs={{0,3},{1,0},{2,1},{3,2},{4,7},{5,4},{6,5},{7,6},{8,11},{9,8},{10,9... | collective-permute-start | bytes 786440 | tf_op jit(solution)/shard_map/rows/ppermute | solution.py:254
  15.7 6.1 %collective-permute-start.10 = (f32[32,128]{1,0:T(8,128)S(1)}, f32[32,128]{1,0:T(8,128)S(1)}, u32[]{:S(2)}, u32[]{:S(2)}) collective-permute-start(f32[32,128]{1,0:T(8,128)S(1)} %get-tuple-element.19), channel_id=1, source_target_pairs={{0,192},{1,193},{2,194},{3,195},{4,0},{5,1},{6,2},{7,3},{8,64},{9,... | collective-permute-start | bytes 49160 | tf_op jit(solution)/shard_map/bias/ppermute | solution.py:254
  21.9 1.9 collective-permute-start.8
  23.8 2.5 %collective-permute-done.8 = f32[32,128]{1,0:T(8,128)S(1)} collective-permute-done((f32[32,128]{1,0:T(8,128)S(1)}, f32[32,128]{1,0:T(8,128)S(1)}, u32[]{:S(2)}, u32[]{:S(2)}) %collective-permute-start.8) | collective-permute-done | bytes 16416 | tf_op jit(solution)/shard_map/bias/ppermute | solution.py:254
  26.2 3.2 %collective-permute-start.9 = (f32[32,128]{1,0:T(8,128)S(1)}, f32[32,128]{1,0:T(8,128)S(1)}, u32[]{:S(2)}, u32[]{:S(2)}) collective-permute-start(f32[32,128]{1,0:T(8,128)S(1)} %get-tuple-element.20), channel_id=1, source_target_pairs={{0,128},{1,129},{2,130},{3,131},{4,192},{5,193},{6,194},{7,195},{8... | collective-permute-start | bytes 49160 | tf_op jit(solution)/shard_map/bias/ppermute | solution.py:254
  29.5 1.0 collective-permute-done.9
  30.5 6.6 %collective-permute-done.1 = bf16[16,64,128]{2,1,0:T(8,128)(2,1)S(1)} collective-permute-done((bf16[16,64,128]{2,1,0:T(8,128)(2,1)S(1)}, bf16[16,64,128]{2,1,0:T(8,128)(2,1)S(1)}, u32[]{:S(2)}, u32[]{:S(2)}) %collective-permute-start.1) | collective-permute-done | bytes 262176 | tf_op jit(solution)/shard_map/rows/ppermute | solution.py:254
  37.1 1.1 pad_maximum_fusion.rest_0_.x0
  38.2 6.1 %collective-permute-start.5 = (bf16[4,16,64,128]{3,2,1,0:T(8,128)(2,1)}, bf16[4,16,64,128]{3,2,1,0:T(8,128)(2,1)S(1)}, u32[]{:S(2)}, u32[]{:S(2)}) collective-permute-start(bf16[4,16,64,128]{3,2,1,0:T(8,128)(2,1)} %pad_maximum_fusion.rest_0_.x0), channel_id=1, source_target_pairs={{0,12},{1,13},{2,14},{3,15},{4,0},{5,1},{6,2},{7,3},{8,4},{9,5},{1... | collective-permute-start | bytes 3145736 | tf_op jit(solution)/shard_map/rows/ppermute | solution.py:254
  44.3 0.6 constant_dynamic-slice_fusion
  44.9 1.2 tie.4
  46.2 0.9 broadcast_in_dim.6
  47.0 23.0 %all_to_all.5.array = f32[8,128,128]{2,1,0:T(8,128)} all-to-all(f32[8,128,128]{2,1,0:T(8,128)S(1)} %broadcast_in_dim.6), channel_id=1, replica_groups=mesh['y'=4,'zh'=2,'core'=2,'x'=4,'zl'=4] {'zh','zl'}, dimensions={0} | all-to-all | bytes 1048576 | tf_op jit(solution)/shard_map/bias/all_to_all | solution.py:311
  70.1 1.0 copy-done.15
  71.1 1.0 copy-done.16
  72.1 1.5 tie.5.b00
  73.7 1.1 collective-permute-start.16
  74.8 1.9 collective-permute-start.4
  76.7 1.5 collective-permute-start.14
  78.1 3.8 %collective-permute-start.11 = (f32[8,128,128]{2,1,0:T(8,128)}, f32[8,128,128]{2,1,0:T(8,128)S(1)}, u32[]{:S(2)}, u32[]{:S(2)}) collective-permute-start(f32[8,128,128]{2,1,0:T(8,128)} %tie.5.b00), channel_id=1, source_target_pairs={{0,16},{1,17},{2,18},{3,19},{4,20},{5,21},{6,22},{7,23},{8,24},{9,... | collective-permute-start | bytes 1572872 | tf_op jit(solution)/shard_map/bias/ppermute | solution.py:254
  81.9 2.6 %collective-permute-done.16.b30 = f32[8,128,128]{2,1,0:T(8,128)S(1)} collective-permute-done((f32[8,128,128]{2,1,0:T(8,128)}, f32[8,128,128]{2,1,0:T(8,128)S(1)}, u32[]{:S(2)}, u32[]{:S(2)}) %collective-permute-start.16) | collective-permute-done | bytes 524320 | tf_op jit(solution)/shard_map/bias/ppermute | solution.py:254
  84.5 7.2 %collective-permute-start.17 = (f32[8,128,128]{2,1,0:T(8,128)S(1)}, f32[8,128,128]{2,1,0:T(8,128)S(1)}, u32[]{:S(2)}, u32[]{:S(2)}) collective-permute-start(f32[8,128,128]{2,1,0:T(8,128)S(1)} %collective-permute-done.16.b30), channel_id=1, source_target_pairs={{0,16},{1,17},{2,18},{3,19},{4,20},{5,21},{6,22},{7,23},{8,24},{9,... | collective-permute-start | bytes 1572872 | tf_op jit(solution)/shard_map/bias/ppermute | solution.py:254
  91.7 5.2 %collective-permute-start.15 = (f32[8,128,128]{2,1,0:T(8,128)S(1)}, f32[8,128,128]{2,1,0:T(8,128)S(1)}, u32[]{:S(2)}, u32[]{:S(2)}) collective-permute-start(f32[8,128,128]{2,1,0:T(8,128)S(1)} %collective-permute-done.14.b20), channel_id=1, source_target_pairs={{0,16},{1,17},{2,18},{3,19},{4,20},{5,21},{6,22},{7,23},{8,24},{9,... | collective-permute-start | bytes 1572872 | tf_op jit(solution)/shard_map/bias/ppermute | solution.py:254
  96.9 6.6 %collective-permute-done.12.b10 = f32[8,128,128]{2,1,0:T(8,128)S(1)} collective-permute-done((f32[8,128,128]{2,1,0:T(8,128)}, f32[8,128,128]{2,1,0:T(8,128)S(1)}, u32[]{:S(2)}, u32[]{:S(2)}) %collective-permute-start.12) | collective-permute-done | bytes 524320 | tf_op jit(solution)/shard_map/bias/ppermute | solution.py:254
  103.5 0.5 collective-permute-start.13
  104.6 1.0 collective-permute-done.13.b11
  105.6 1.0 copy-done.3
  106.7 35.0 %attention.2.rest_0_ = bf16[4,8,64,128]{3,2,1,0:T(8,128)(2,1)S(1)} custom-call(s32[4]{0:T(128)S(1)} %pad_add_fusion.at.array, bf16[4,16,64,128]{3,2,1,0:T(8,128)(2,1)} %pad_maximum_fusion.rest_0_.x0, bf16[4,16,64,128]{3,2,1,0:T(8,128)(2,1)} %copy-done.16, bf16[4,16,64,128]{3,2,1,0:T(8,128)(2,1)} %collective-permute-done.4.x2, ...), custom_call_target="tpu_custom_call" | custom-call | flops 2400000000 | bytes 8388608 | tf_op jit(solution)/shard_map/attention/attention/pallas_call | solution.py:168
  141.8 0.8 copy-done.2
  142.6 0.8 copy-done.9
  143.4 2.0 slice_bitcast_fusion.4
  145.6 1.2 collective-permute-start.19
  146.8 1.8 collective-permute-start.18
  148.7 35.0 %attention.3.rest_0_ = bf16[4,8,64,128]{3,2,1,0:T(8,128)(2,1)S(1)} custom-call(s32[4]{0:T(128)S(1)} %copy-done.6, bf16[4,16,64,128]{3,2,1,0:T(8,128)(2,1)} %pad_maximum_fusion.rest_0_.x0, bf16[4,16,64,128]{3,2,1,0:T(8,128)(2,1)} %copy-done.16, bf16[4,16,64,128]{3,2,1,0:T(8,128)(2,1)} %collective-permute-done.4.x2, bf16[4,16,64,128]{3,2,1,0:T(8,128)(2,1)} %copy-done.15, ...), custom_call_target="tpu_custom_call" | custom-call | flops 2400000000 | bytes 8388608 | tf_op jit(solution)/shard_map/attention/attention/pallas_call | solution.py:168
  183.7 0.8 slice_bitcast_fusion
  184.8 1.2 collective-permute-start.22
  186.0 2.4 %collective-permute-start.21 = (bf16[8,64,128]{2,1,0:T(8,128)(2,1)S(1)}, bf16[8,64,128]{2,1,0:T(8,128)(2,1)S(1)}, u32[]{:S(2)}, u32[]{:S(2)}) collective-permute-start(bf16[8,64,128]{2,1,0:T(8,128)(2,1)S(1)} %get-tuple-element.11), channel_id=1, source_target_pairs={{0,3},{1,0},{2,1},{3,2},{4,7},{5,4},{6,5},{7,6},{8,11},{9,8},{10,9... | collective-permute-start | bytes 393224 | tf_op jit(solution)/shard_map/update/ppermute | solution.py:254
  188.3 2.2 %collective-permute-done.23.refs_7_ = bf16[8,64,128]{2,1,0:T(8,128)(2,1)S(1)} collective-permute-done((bf16[8,64,128]{2,1,0:T(8,128)(2,1)S(1)}, bf16[8,64,128]{2,1,0:T(8,128)(2,1)S(1)}, u32[]{:S(2)}, u32[]{:S(2)}) %collective-permute-start.23) | collective-permute-done | bytes 131104 | tf_op jit(solution)/shard_map/update/ppermute | solution.py:254
  190.5 5.5 %collective-permute-done.22.refs_6_ = bf16[8,64,128]{2,1,0:T(8,128)(2,1)S(1)} collective-permute-done((bf16[8,64,128]{2,1,0:T(8,128)(2,1)S(1)}, bf16[8,64,128]{2,1,0:T(8,128)(2,1)S(1)}, u32[]{:S(2)}, u32[]{:S(2)}) %collective-permute-start.22) | collective-permute-done | bytes 131104 | tf_op jit(solution)/shard_map/update/ppermute | solution.py:254
  196.1 0.6 copy-done.19
  196.8 2.3 %assemble_update.1 = bf16[64,64,128]{2,1,0:T(8,128)(2,1)} custom-call(s32[4]{0:T(128)} %tie.7.at, bf16[8,64,128]{2,1,0:T(8,128)(2,1)} %get-tuple-element.16.refs_0_, bf16[8,64,128]{2,1,0:T(8,128)(2,1)} %collective-permute-done.18.refs_1_, bf16[8,64,128]{2,1,0:T(8,128)(2,1)} %collective-permute-done.19.refs_2_, bf16[8,64,128]{2,1,0:T(8,128)(2,1)} %copy-done.17, ...), custom_call_target="tpu_custom_call" | custom-call | tf_op jit(solution)/shard_map/assemble_update/pallas_call | solution.py:215
  (91 shorter events, 2.3 us)
Async XLA Ops:
  0.0 4.6 %copy-start = (f32[128,4]{0,1:T(4,128)S(1)}, f32[128,4]{0,1:T(4,128)}, u32[]{:S(2)}) copy-start(f32[128,4]{0,1:T(4,128)} %param.19) | copy-start | bytes 6148
  0.0 2.0 copy-start.14
  0.0 3.3 %copy-start.25 = (f32[128]{0:T(128)S(1)}, f32[128]{0:T(128)}, u32[]{:S(2)}) copy-start(f32[128]{0:T(128)} %param.13) | copy-start | bytes 1540
  0.0 3.3 %copy-start.26 = (f32[128]{0:T(128)S(1)}, f32[128]{0:T(128)}, u32[]{:S(2)}) copy-start(f32[128]{0:T(128)} %param.12) | copy-start | bytes 1540
  7.4 4.3 %collective-permute-start.6 = (f32[4,32,64]{1,0,2:T(4,128)S(1)}, f32[4,32,64]{1,0,2:T(4,128)S(1)}, u32[]{:S(2)}, u32[]{:S(2)}) collective-permute-start(f32[4,32,64]{1,0,2:T(4,128)S(1)} %get-tuple-element.18), channel_id=1, source_target_pairs={{0,16},{1,17},{2,18},{3,19},{4,20},{5,21},{6,22},{7,23},{8,24},{9,... | collective-permute-start | bytes 98312 | tf_op jit(solution)/shard_map/bias/ppermute | solution.py:254
  11.9 10.0 %collective-permute-start.7 = (f32[32,128]{1,0:T(8,128)S(1)}, f32[32,128]{1,0:T(8,128)S(1)}, u32[]{:S(2)}, u32[]{:S(2)}) collective-permute-start(f32[32,128]{1,0:T(8,128)S(1)} %get-tuple-element.22), channel_id=1, source_target_pairs={{0,0},{1,1},{2,2},{3,3},{4,64},{5,65},{6,66},{7,67},{8,128},{9,129... | collective-permute-start | bytes 49160 | tf_op jit(solution)/shard_map/bias/ppermute | solution.py:254
  12.7 17.9 %collective-permute-start.2 = (bf16[16,64,128]{2,1,0:T(8,128)(2,1)S(1)}, bf16[16,64,128]{2,1,0:T(8,128)(2,1)S(1)}, u32[]{:S(2)}, u32[]{:S(2)}) collective-permute-start(bf16[16,64,128]{2,1,0:T(8,128)(2,1)S(1)} %get-tuple-element.6), channel_id=1, source_target_pairs={{0,3},{1,0},{2,1},{3,2},{4,7},{5,4},{6,5},{7,6},{8,11},{9,8},{10,9... | collective-permute-start | bytes 786440 | tf_op jit(solution)/shard_map/rows/ppermute | solution.py:254
  15.4 21.8 %collective-permute-start.1 = (bf16[16,64,128]{2,1,0:T(8,128)(2,1)S(1)}, bf16[16,64,128]{2,1,0:T(8,128)(2,1)S(1)}, u32[]{:S(2)}, u32[]{:S(2)}) collective-permute-start(bf16[16,64,128]{2,1,0:T(8,128)(2,1)S(1)} %get-tuple-element.7), channel_id=1, source_target_pairs={{0,2},{1,3},{2,0},{3,1},{4,6},{5,7},{6,4},{7,5},{8,10},{9,11},{10,... | collective-permute-start | bytes 786440 | tf_op jit(solution)/shard_map/rows/ppermute | solution.py:254
  15.4 21.8 %collective-permute-start = (bf16[16,64,128]{2,1,0:T(8,128)(2,1)S(1)}, bf16[16,64,128]{2,1,0:T(8,128)(2,1)S(1)}, u32[]{:S(2)}, u32[]{:S(2)}) collective-permute-start(bf16[16,64,128]{2,1,0:T(8,128)(2,1)S(1)} %get-tuple-element.8), channel_id=1, source_target_pairs={{0,1},{1,2},{2,3},{3,0},{4,5},{5,6},{6,7},{7,4},{8,9},{9,10},{10,1... | collective-permute-start | bytes 786440 | tf_op jit(solution)/shard_map/rows/ppermute | solution.py:254
  15.7 14.7 %collective-permute-start.10 = (f32[32,128]{1,0:T(8,128)S(1)}, f32[32,128]{1,0:T(8,128)S(1)}, u32[]{:S(2)}, u32[]{:S(2)}) collective-permute-start(f32[32,128]{1,0:T(8,128)S(1)} %get-tuple-element.19), channel_id=1, source_target_pairs={{0,192},{1,193},{2,194},{3,195},{4,0},{5,1},{6,2},{7,3},{8,64},{9,... | collective-permute-start | bytes 49160 | tf_op jit(solution)/shard_map/bias/ppermute | solution.py:254
  21.9 4.4 %collective-permute-start.8 = (f32[32,128]{1,0:T(8,128)S(1)}, f32[32,128]{1,0:T(8,128)S(1)}, u32[]{:S(2)}, u32[]{:S(2)}) collective-permute-start(f32[32,128]{1,0:T(8,128)S(1)} %get-tuple-element.21), channel_id=1, source_target_pairs={{0,64},{1,65},{2,66},{3,67},{4,128},{5,129},{6,130},{7,131},{8,192... | collective-permute-start | bytes 49160 | tf_op jit(solution)/shard_map/bias/ppermute | solution.py:254
  26.2 4.2 %collective-permute-start.9 = (f32[32,128]{1,0:T(8,128)S(1)}, f32[32,128]{1,0:T(8,128)S(1)}, u32[]{:S(2)}, u32[]{:S(2)}) collective-permute-start(f32[32,128]{1,0:T(8,128)S(1)} %get-tuple-element.20), channel_id=1, source_target_pairs={{0,128},{1,129},{2,130},{3,131},{4,192},{5,193},{6,194},{7,195},{8... | collective-permute-start | bytes 49160 | tf_op jit(solution)/shard_map/bias/ppermute | solution.py:254
  38.2 31.9 %collective-permute-start.5 = (bf16[4,16,64,128]{3,2,1,0:T(8,128)(2,1)}, bf16[4,16,64,128]{3,2,1,0:T(8,128)(2,1)S(1)}, u32[]{:S(2)}, u32[]{:S(2)}) collective-permute-start(bf16[4,16,64,128]{3,2,1,0:T(8,128)(2,1)} %pad_maximum_fusion.rest_0_.x0), channel_id=1, source_target_pairs={{0,12},{1,13},{2,14},{3,15},{4,0},{5,1},{6,2},{7,3},{8,4},{9,5},{1... | collective-permute-start | bytes 3145736 | tf_op jit(solution)/shard_map/rows/ppermute | solution.py:254
  44.3 25.9 %collective-permute-start.3 = (bf16[4,16,64,128]{3,2,1,0:T(8,128)(2,1)}, bf16[4,16,64,128]{3,2,1,0:T(8,128)(2,1)S(1)}, u32[]{:S(2)}, u32[]{:S(2)}) collective-permute-start(bf16[4,16,64,128]{3,2,1,0:T(8,128)(2,1)} %pad_maximum_fusion.rest_0_.x0), channel_id=1, source_target_pairs={{0,4},{1,5},{2,6},{3,7},{4,8},{5,9},{6,10},{7,11},{8,12},{9,13},{1... | collective-permute-start | bytes 3145736 | tf_op jit(solution)/shard_map/rows/ppermute | solution.py:254
  70.1 33.9 %copy-start.21 = (bf16[128,128]{1,0:T(8,128)(2,1)S(1)}, bf16[128,128]{1,0:T(8,128)(2,1)}, u32[]{:S(2)}) copy-start(bf16[128,128]{1,0:T(8,128)(2,1)} %param.14) | copy-start | bytes 98308
  70.1 34.0 %copy-start.22 = (bf16[128,128]{1,0:T(8,128)(2,1)S(1)}, bf16[128,128]{1,0:T(8,128)(2,1)}, u32[]{:S(2)}) copy-start(bf16[128,128]{1,0:T(8,128)(2,1)} %param.16) | copy-start | bytes 98308
  70.1 34.1 %copy-start.23 = (bf16[128,128]{1,0:T(8,128)(2,1)S(1)}, bf16[128,128]{1,0:T(8,128)(2,1)}, u32[]{:S(2)}) copy-start(bf16[128,128]{1,0:T(8,128)(2,1)} %param.17) | copy-start | bytes 98308
  70.1 34.3 %copy-start.24 = (f32[128]{0:T(128)S(1)}, f32[128]{0:T(128)}, u32[]{:S(2)}) copy-start(f32[128]{0:T(128)} %param.18) | copy-start | bytes 1540
  70.1 35.6 %copy-start.11 = (bf16[128,128]{1,0:T(8,128)(2,1)S(1)}, bf16[128,128]{1,0:T(8,128)(2,1)}, u32[]{:S(2)}) copy-start(bf16[128,128]{1,0:T(8,128)(2,1)} %w_key.3) | copy-start | bytes 98308
  70.1 35.5 %copy-start.12 = (bf16[128,128]{1,0:T(8,128)(2,1)S(1)}, bf16[128,128]{1,0:T(8,128)(2,1)}, u32[]{:S(2)}) copy-start(bf16[128,128]{1,0:T(8,128)(2,1)} %w_out.3) | copy-start | bytes 98308
  70.1 35.5 %copy-start.13 = (f32[128]{0:T(128)S(1)}, f32[128]{0:T(128)}, u32[]{:S(2)}) copy-start(f32[128]{0:T(128)} %param.21) | copy-start | bytes 1540
  70.1 1.0 copy-start.15
  71.1 1.0 copy-start.16
  73.7 10.9 %collective-permute-start.16 = (f32[8,128,128]{2,1,0:T(8,128)}, f32[8,128,128]{2,1,0:T(8,128)S(1)}, u32[]{:S(2)}, u32[]{:S(2)}) collective-permute-start(f32[8,128,128]{2,1,0:T(8,128)} %tie.5.b00), channel_id=1, source_target_pairs={{0,192},{1,193},{2,194},{3,195},{4,196},{5,197},{6,198},{7,199},{8... | collective-permute-start | bytes 1572872 | tf_op jit(solution)/shard_map/bias/ppermute | solution.py:254
  74.8 29.8 %collective-permute-start.4 = (bf16[4,16,64,128]{3,2,1,0:T(8,128)(2,1)}, bf16[4,16,64,128]{3,2,1,0:T(8,128)(2,1)}, u32[]{:S(2)}, u32[]{:S(2)}) collective-permute-start(bf16[4,16,64,128]{3,2,1,0:T(8,128)(2,1)} %pad_maximum_fusion.rest_0_.x0), channel_id=1, source_target_pairs={{0,8},{1,9},{2,10},{3,11},{4,12},{5,13},{6,14},{7,15},{8,0},{9,1},... | collective-permute-start | bytes 3145736 | tf_op jit(solution)/shard_map/rows/ppermute | solution.py:254
  76.7 15.0 %collective-permute-start.14 = (f32[8,128,128]{2,1,0:T(8,128)}, f32[8,128,128]{2,1,0:T(8,128)S(1)}, u32[]{:S(2)}, u32[]{:S(2)}) collective-permute-start(f32[8,128,128]{2,1,0:T(8,128)} %tie.5.b00), channel_id=1, source_target_pairs={{0,128},{1,129},{2,130},{3,131},{4,132},{5,133},{6,134},{7,135},{8... | collective-permute-start | bytes 1572872 | tf_op jit(solution)/shard_map/bias/ppermute | solution.py:254
  78.1 25.3 %collective-permute-start.12 = (f32[8,128,128]{2,1,0:T(8,128)}, f32[8,128,128]{2,1,0:T(8,128)S(1)}, u32[]{:S(2)}, u32[]{:S(2)}) collective-permute-start(f32[8,128,128]{2,1,0:T(8,128)} %tie.5.b00), channel_id=1, source_target_pairs={{0,64},{1,65},{2,66},{3,67},{4,68},{5,69},{6,70},{7,71},{8,72},{9,... | collective-permute-start | bytes 1572872 | tf_op jit(solution)/shard_map/bias/ppermute | solution.py:254
  78.1 26.4 %collective-permute-start.11 = (f32[8,128,128]{2,1,0:T(8,128)}, f32[8,128,128]{2,1,0:T(8,128)S(1)}, u32[]{:S(2)}, u32[]{:S(2)}) collective-permute-start(f32[8,128,128]{2,1,0:T(8,128)} %tie.5.b00), channel_id=1, source_target_pairs={{0,16},{1,17},{2,18},{3,19},{4,20},{5,21},{6,22},{7,23},{8,24},{9,... | collective-permute-start | bytes 1572872 | tf_op jit(solution)/shard_map/bias/ppermute | solution.py:254
  84.5 20.0 %collective-permute-start.17 = (f32[8,128,128]{2,1,0:T(8,128)S(1)}, f32[8,128,128]{2,1,0:T(8,128)S(1)}, u32[]{:S(2)}, u32[]{:S(2)}) collective-permute-start(f32[8,128,128]{2,1,0:T(8,128)S(1)} %collective-permute-done.16.b30), channel_id=1, source_target_pairs={{0,16},{1,17},{2,18},{3,19},{4,20},{5,21},{6,22},{7,23},{8,24},{9,... | collective-permute-start | bytes 1572872 | tf_op jit(solution)/shard_map/bias/ppermute | solution.py:254
  91.7 12.9 %collective-permute-start.15 = (f32[8,128,128]{2,1,0:T(8,128)S(1)}, f32[8,128,128]{2,1,0:T(8,128)S(1)}, u32[]{:S(2)}, u32[]{:S(2)}) collective-permute-start(f32[8,128,128]{2,1,0:T(8,128)S(1)} %collective-permute-done.14.b20), channel_id=1, source_target_pairs={{0,16},{1,17},{2,18},{3,19},{4,20},{5,21},{6,22},{7,23},{8,24},{9,... | collective-permute-start | bytes 1572872 | tf_op jit(solution)/shard_map/bias/ppermute | solution.py:254
  103.5 2.2 %collective-permute-start.13 = (f32[8,128,128]{2,1,0:T(8,128)S(1)}, f32[8,128,128]{2,1,0:T(8,128)}, u32[]{:S(2)}, u32[]{:S(2)}) collective-permute-start(f32[8,128,128]{2,1,0:T(8,128)S(1)} %collective-permute-done.12.b10), channel_id=1, source_target_pairs={{0,16},{1,17},{2,18},{3,19},{4,20},{5,21},{6,22},{7,23},{8,24},{9,... | collective-permute-start | bytes 1572872 | tf_op jit(solution)/shard_map/bias/ppermute | solution.py:254
  104.5 37.2 %copy-start.5 = (s32[4]{0:T(128)}, s32[4]{0:T(128)S(1)}, u32[]{:S(2)}) copy-start(s32[4]{0:T(128)S(1)} %pad_add_fusion.at.array) | copy-start | bytes 52
  104.6 37.2 %copy-start.7 = (f32[8,128,128]{2,1,0:T(8,128)}, f32[8,128,128]{2,1,0:T(8,128)S(1)}, u32[]{:S(2)}) copy-start(f32[8,128,128]{2,1,0:T(8,128)S(1)} %collective-permute-done.17.b31) | copy-start | bytes 1572868
  105.6 1.0 copy-start.3
  141.7 0.8 copy-start.2
  143.4 5.3 %copy-start.4 = (f32[8,128,128]{2,1,0:T(8,128)S(1)}, f32[8,128,128]{2,1,0:T(8,128)}, u32[]{:S(2)}) copy-start(f32[8,128,128]{2,1,0:T(8,128)} %tie.5.b00) | copy-start | bytes 1572868
  143.4 5.3 %copy-start.6 = (s32[4]{0:T(128)S(1)}, s32[4]{0:T(128)}, u32[]{:S(2)}) copy-start(s32[4]{0:T(128)} %tie.6.at.array) | copy-start | bytes 52
  143.4 5.3 %copy-start.8 = (f32[8,128,128]{2,1,0:T(8,128)S(1)}, f32[8,128,128]{2,1,0:T(8,128)}, u32[]{:S(2)}) copy-start(f32[8,128,128]{2,1,0:T(8,128)} %copy-done.7) | copy-start | bytes 1572868
  143.4 5.3 %copy-start.10 = (f32[8,128,128]{2,1,0:T(8,128)S(1)}, f32[8,128,128]{2,1,0:T(8,128)}, u32[]{:S(2)}) copy-start(f32[8,128,128]{2,1,0:T(8,128)} %copy-done.9) | copy-start | bytes 1572868
  145.4 40.6 %collective-permute-start.20 = (bf16[8,64,128]{2,1,0:T(8,128)(2,1)S(1)}, bf16[8,64,128]{2,1,0:T(8,128)(2,1)S(1)}, u32[]{:S(2)}, u32[]{:S(2)}) collective-permute-start(bf16[8,64,128]{2,1,0:T(8,128)(2,1)S(1)} %get-tuple-element.13), channel_id=1, source_target_pairs={{0,1},{1,2},{2,3},{3,0},{4,5},{5,6},{6,7},{7,4},{8,9},{9,10},{10,1... | collective-permute-start | bytes 393224 | tf_op jit(solution)/shard_map/update/ppermute | solution.py:254
  145.6 42.7 %collective-permute-start.19 = (bf16[8,64,128]{2,1,0:T(8,128)(2,1)}, bf16[8,64,128]{2,1,0:T(8,128)(2,1)}, u32[]{:S(2)}, u32[]{:S(2)}) collective-permute-start(bf16[8,64,128]{2,1,0:T(8,128)(2,1)} %get-tuple-element.14), channel_id=1, source_target_pairs={{0,2},{1,3},{2,0},{3,1},{4,6},{5,7},{6,4},{7,5},{8,10},{9,11},{10,... | collective-permute-start | bytes 393224 | tf_op jit(solution)/shard_map/update/ppermute | solution.py:254
  146.8 41.5 %collective-permute-start.18 = (bf16[8,64,128]{2,1,0:T(8,128)(2,1)}, bf16[8,64,128]{2,1,0:T(8,128)(2,1)}, u32[]{:S(2)}, u32[]{:S(2)}) collective-permute-start(bf16[8,64,128]{2,1,0:T(8,128)(2,1)} %get-tuple-element.15), channel_id=1, source_target_pairs={{0,3},{1,0},{2,1},{3,2},{4,7},{5,4},{6,5},{7,6},{8,11},{9,8},{10,9... | collective-permute-start | bytes 393224 | tf_op jit(solution)/shard_map/update/ppermute | solution.py:254
  183.7 4.6 %copy-start.1 = (bf16[4,8,64,128]{3,2,1,0:T(8,128)(2,1)}, bf16[4,8,64,128]{3,2,1,0:T(8,128)(2,1)S(1)}, u32[]{:S(2)}) copy-start(bf16[4,8,64,128]{3,2,1,0:T(8,128)(2,1)S(1)} %attention.3.rest_0_) | copy-start | bytes 1572868
  184.5 6.0 %collective-permute-start.23 = (bf16[8,64,128]{2,1,0:T(8,128)(2,1)S(1)}, bf16[8,64,128]{2,1,0:T(8,128)(2,1)S(1)}, u32[]{:S(2)}, u32[]{:S(2)}) collective-permute-start(bf16[8,64,128]{2,1,0:T(8,128)(2,1)S(1)} %get-tuple-element.9), channel_id=1, source_target_pairs={{0,1},{1,2},{2,3},{3,0},{4,5},{5,6},{6,7},{7,4},{8,9},{9,10},{10,1... | collective-permute-start | bytes 393224 | tf_op jit(solution)/shard_map/update/ppermute | solution.py:254
  184.8 11.3 %collective-permute-start.22 = (bf16[8,64,128]{2,1,0:T(8,128)(2,1)S(1)}, bf16[8,64,128]{2,1,0:T(8,128)(2,1)S(1)}, u32[]{:S(2)}, u32[]{:S(2)}) collective-permute-start(bf16[8,64,128]{2,1,0:T(8,128)(2,1)S(1)} %get-tuple-element.10), channel_id=1, source_target_pairs={{0,2},{1,3},{2,0},{3,1},{4,6},{5,7},{6,4},{7,5},{8,10},{9,11},{10,... | collective-permute-start | bytes 393224 | tf_op jit(solution)/shard_map/update/ppermute | solution.py:254
  186.0 10.1 %copy-start.17 = (bf16[8,64,128]{2,1,0:T(8,128)(2,1)}, bf16[8,64,128]{2,1,0:T(8,128)(2,1)S(1)}, u32[]{:S(2)}) copy-start(bf16[8,64,128]{2,1,0:T(8,128)(2,1)S(1)} %collective-permute-done.20.refs_3_) | copy-start | bytes 393220
  186.0 10.1 %collective-permute-start.21 = (bf16[8,64,128]{2,1,0:T(8,128)(2,1)S(1)}, bf16[8,64,128]{2,1,0:T(8,128)(2,1)S(1)}, u32[]{:S(2)}, u32[]{:S(2)}) collective-permute-start(bf16[8,64,128]{2,1,0:T(8,128)(2,1)S(1)} %get-tuple-element.11), channel_id=1, source_target_pairs={{0,3},{1,0},{2,1},{3,2},{4,7},{5,4},{6,5},{7,6},{8,11},{9,8},{10,9... | collective-permute-start | bytes 393224 | tf_op jit(solution)/shard_map/update/ppermute | solution.py:254
  190.5 5.5 %copy-start.18 = (bf16[8,64,128]{2,1,0:T(8,128)(2,1)}, bf16[8,64,128]{2,1,0:T(8,128)(2,1)S(1)}, u32[]{:S(2)}) copy-start(bf16[8,64,128]{2,1,0:T(8,128)(2,1)S(1)} %collective-permute-done.23.refs_7_) | copy-start | bytes 393220
  (3 other events, 2.2 us)
